TPU v7x, 32 devices: a whole 2x2x4 slice. The times are simulated.
32 devices in a mesh: dp: 2 (over x), seq: 16 (over z, y, core).
Axes of the slice: x: 2, y: 2, z: 4, core: 2. Of those that a mesh axis runs over, the one named last changes fastest.
Arguments:
- tokens: bfloat16 [2, 2048, 1024], P('dp', 'seq'), may hold values from -6 to 6
- cotangent: bfloat16 [2, 2048, 1024], P('dp', 'seq'), may hold values from -6 to 6
- first_gain: float32 [1024], replicated, may hold values from 0.5 to 1.5
- first_shift: float32 [1024], replicated, may hold values from -1 to 1
- input_weight: bfloat16 [1024, 3072], P(('dp', 'seq')), may hold values from -0.1875 to 0.1875
- input_bias: float32 [3072], replicated, may hold values from -1 to 1
- short_weight: float32 [3, 3072], replicated, may hold values from -3 to 3
- short_bias: float32 [3072], replicated, may hold values from -1 to 1
- feat_weight: float32 [33, 64], replicated, may hold values from -1 to 1
- feat_bias: float32 [64], replicated, may hold values from -3 to 3
- feat_freq: float32 [64], replicated, may hold values from 1 to 8
- inner_weight: float32 [64, 64], replicated, may hold values from -0.75 to 0.75
- inner_bias: float32 [64], replicated, may hold values from -3 to 3
- inner_freq: float32 [64], replicated, may hold values from 1 to 8
- filter_weight: float32 [64, 1024], replicated, may hold values from -0.0625 to 0.0625
- skip_gain: float32 [1024], replicated, may hold values from -4 to 4
- decay_rates: float32 [1024], replicated, may hold values from 1 to 32
- output_weight: bfloat16 [1024, 1024], P(('dp', 'seq')), may hold values from -0.1875 to 0.1875
- output_bias: float32 [1024], replicated, may hold values from -1 to 1
- second_gain: float32 [1024], replicated, may hold values from 0.5 to 1.5
- second_shift: float32 [1024], replicated, may hold values from -1 to 1
- up_weight: bfloat16 [1024, 4096], P(('dp', 'seq')), may hold values from -0.1875 to 0.1875
- up_bias: float32 [4096], replicated, may hold values from -1 to 1
- down_weight: bfloat16 [4096, 1024], P(('dp', 'seq')), may hold values from -0.09375 to 0.09375
- down_bias: float32 [1024], replicated, may hold values from -1 to 1
Outputs:
- block_out: bfloat16 [2, 2048, 1024], P('dp', 'seq')
- tokens_grad: bfloat16 [2, 2048, 1024], P('dp', 'seq')
- first_gain_grad: float32 [1024], replicated
- first_shift_grad: float32 [1024], replicated
- input_weight_grad: float32 [1024, 3072], P(('dp', 'seq'))
- input_bias_grad: float32 [3072], replicated
- short_weight_grad: float32 [3, 3072], replicated
- short_bias_grad: float32 [3072], replicated
- feat_weight_grad: float32 [33, 64], replicated
- feat_bias_grad: float32 [64], replicated
- feat_freq_grad: float32 [64], replicated
- inner_weight_grad: float32 [64, 64], replicated
- inner_bias_grad: float32 [64], replicated
- inner_freq_grad: float32 [64], replicated
- filter_weight_grad: float32 [64, 1024], replicated
- skip_gain_grad: float32 [1024], replicated
- output_weight_grad: float32 [1024, 1024], P(('dp', 'seq'))
- output_bias_grad: float32 [1024], replicated
- second_gain_grad: float32 [1024], replicated
- second_shift_grad: float32 [1024], replicated
- up_weight_grad: float32 [1024, 4096], P(('dp', 'seq'))
- up_bias_grad: float32 [4096], replicated
- down_weight_grad: float32 [4096, 1024], P(('dp', 'seq'))
- down_bias_grad: float32 [1024], replicated
All inputs are finite; a program needn't handle non-finite values.
Results may differ from a plain program's by a relative error of at most 0.014.
Values may be sent and summed in bfloat16 or wider, within the bound.
A program may use at most 192 MiB of HBM per device.

v0:
```python
import functools
import math

import jax
import jax.numpy as jnp
from jax import lax
from jax.sharding import PartitionSpec as P

FEAT = 33


exact_precision = lax.Precision.HIGHEST


def from_behind(x, axis, by):
    size = lax.axis_size(axis)
    pairs = [(i, i + by) for i in range(size) if 0 <= i + by < size]
    return lax.ppermute(x, axis, pairs)


def layer_norm(values, gain_vec, offset):
    center = values - jnp.mean(values, -1, keepdims=True)
    spread = jnp.mean(center * center, -1, keepdims=True)
    return center * lax.rsqrt(spread + 1e-05) * gain_vec + offset


def position_features(stamps, length):
    stamp_float = stamps.astype(jnp.float32)
    linear_ramp = stamp_float / (length - 1)
    band_rates = 0.0001 + jnp.arange((FEAT - 1) // 2).astype(jnp.float32) * ((15.0 - 0.0001) / 15.0)
    phase_angle = (stamp_float * (2.0 * math.pi / length))[:, None] * band_rates[None, :]
    return jnp.concatenate([linear_ramp[:, None], jnp.cos(phase_angle), -jnp.sin(phase_angle)], 1)


def filter_net(
    feat_weight,
    feat_bias,
    feat_freq,
    inner_weight,
    inner_bias,
    inner_freq,
    filter_weight,
    feature_rows,
    modulate,
):
    hidden = jnp.sin(
        feat_freq * (jnp.dot(feature_rows, feat_weight, precision=exact_precision) + feat_bias)
    )
    hidden = jnp.sin(
        inner_freq * (jnp.dot(hidden, inner_weight, precision=exact_precision) + inner_bias)
    )
    raw_filter = lax.dot_general(
        filter_weight, hidden, (((0,), (1,)), ((), ())), precision=exact_precision
    )
    return raw_filter * modulate


def short_conv(padded, kernel, offset):
    col_count = padded.shape[1] - 2
    return (
        offset[:, None]
        + kernel[0][:, None] * padded[:, :col_count]
        + kernel[1][:, None] * padded[:, 1 : col_count + 1]
        + kernel[2][:, None] * padded[:, 2:]
    )


def unit_angles(rows, cols, period):
    row_index = lax.broadcasted_iota(jnp.int32, (rows, cols), 0)
    col_index = lax.broadcasted_iota(jnp.int32, (rows, cols), 1)
    phase_angle = (row_index * col_index % period).astype(jnp.float32) * (2.0 * math.pi / period)
    return (jnp.cos(phase_angle), jnp.sin(phase_angle))


def forward_frequency_domain(signal, outer_size, period):
    block_count = signal.shape[1]
    row_count = signal.shape[2]
    cos_first, sin_first = unit_angles(outer_size, block_count, outer_size)
    real_first = jnp.einsum("dn,cnt->cdt", cos_first, signal, precision=exact_precision)
    imag_first = -jnp.einsum("dn,cnt->cdt", sin_first, signal, precision=exact_precision)
    cos_turn, sin_turn = unit_angles(outer_size, row_count, period)
    real_turned = real_first * cos_turn + imag_first * sin_turn
    imag_turned = imag_first * cos_turn - real_first * sin_turn
    cos_last, sin_last = unit_angles(row_count, row_count, row_count)
    real_out = jnp.einsum(
        "cdb,bk->cdk", real_turned, cos_last, precision=exact_precision
    ) + jnp.einsum("cdb,bk->cdk", imag_turned, sin_last, precision=exact_precision)
    imag_out = jnp.einsum(
        "cdb,bk->cdk", imag_turned, cos_last, precision=exact_precision
    ) - jnp.einsum("cdb,bk->cdk", real_turned, sin_last, precision=exact_precision)
    return (real_out, imag_out)


def inverse_spectrum(real_part, imag_part, block_count, period):
    outer_size = real_part.shape[1]
    row_count = real_part.shape[2]
    cos_last, sin_last = unit_angles(row_count, row_count, row_count)
    real_back = jnp.einsum(
        "cdk,kb->cdb", real_part, cos_last, precision=exact_precision
    ) - jnp.einsum("cdk,kb->cdb", imag_part, sin_last, precision=exact_precision)
    imag_back = jnp.einsum(
        "cdk,kb->cdb", real_part, sin_last, precision=exact_precision
    ) + jnp.einsum("cdk,kb->cdb", imag_part, cos_last, precision=exact_precision)
    cos_turn, sin_turn = unit_angles(outer_size, row_count, period)
    real_turned = real_back * cos_turn - imag_back * sin_turn
    imag_turned = real_back * sin_turn + imag_back * cos_turn
    cos_first, sin_first = unit_angles(block_count, outer_size, outer_size)
    summed = jnp.einsum(
        "nd,cdt->cnt", cos_first, real_turned, precision=exact_precision
    ) - jnp.einsum("nd,cdt->cnt", sin_first, imag_turned, precision=exact_precision)
    return summed / period


def on_device(
    tokens,
    cotangent,
    first_gain,
    first_shift,
    input_weight,
    input_bias,
    short_weight,
    short_bias,
    feat_weight,
    feat_bias,
    feat_freq,
    inner_weight,
    inner_bias,
    inner_freq,
    filter_weight,
    skip_gain,
    decay_rates,
    output_weight,
    output_bias,
    second_gain,
    second_shift,
    up_weight,
    up_bias,
    down_weight,
    down_bias,
):
    sequence_count = lax.axis_size("seq")
    seq_index = lax.axis_index("seq")
    row_count = tokens.shape[1]
    model_width = tokens.shape[2]
    length = row_count * sequence_count
    period = 2 * length
    outer_size = 2 * sequence_count
    narrow = model_width // sequence_count
    inputs = tokens[0].astype(jnp.float32)
    cotan_rows = cotangent[0].astype(jnp.float32)
    w_in, w_out, w_up, w_down = (
        lax.all_gather(input_weight, ("dp", "seq"), axis=0, tiled=True),
        lax.all_gather(output_weight, ("dp", "seq"), axis=0, tiled=True),
        lax.all_gather(up_weight, ("dp", "seq"), axis=0, tiled=True),
        lax.all_gather(down_weight, ("dp", "seq"), axis=0, tiled=True),
    )
    normed_one, norm_one_back = jax.vjp(layer_norm, inputs, first_gain, first_shift)
    act_one = normed_one.astype(jnp.bfloat16)
    projected = lax.dot_general(
        w_in, act_one, (((0,), (1,)), ((), ())), preferred_element_type=jnp.float32
    )
    projected = projected + input_bias[:, None]
    rim_rows = from_behind(projected[:, row_count - 2 :], "seq", 1)
    padded = jnp.concatenate([rim_rows, projected], 1)
    conv_out, short_back = jax.vjp(short_conv, padded, short_weight, short_bias)
    leading_gate = conv_out[:model_width]
    second_gate = conv_out[model_width : 2 * model_width]
    value_part = conv_out[2 * model_width :]
    carried = leading_gate * value_part
    stamps = seq_index * row_count + lax.iota(jnp.int32, row_count)
    modulate = jnp.exp(-decay_rates[:, None] * (stamps.astype(jnp.float32) / (length - 1))[None, :])
    filter_fixed = functools.partial(
        filter_net, feature_rows=position_features(stamps, length), modulate=modulate
    )
    filters, filter_back = jax.vjp(
        filter_fixed,
        feat_weight,
        feat_bias,
        feat_freq,
        inner_weight,
        inner_bias,
        inner_freq,
        filter_weight,
    )
    carried_blocks = carried.reshape(sequence_count, narrow, row_count)
    filter_blocks = filters.reshape(sequence_count, narrow, row_count)
    carried_chan, filter_chan = (
        lax.all_to_all(
            carried_blocks.astype(jnp.bfloat16), "seq", split_axis=0, concat_axis=2, tiled=True
        ).astype(carried_blocks.dtype),
        lax.all_to_all(
            filter_blocks.astype(jnp.bfloat16), "seq", split_axis=0, concat_axis=2, tiled=True
        ).astype(filter_blocks.dtype),
    )
    carried_chan = carried_chan.reshape(narrow, sequence_count, row_count)
    filter_chan = filter_chan.reshape(narrow, sequence_count, row_count)
    carried_real, carried_imag = forward_frequency_domain(carried_chan, outer_size, period)
    filter_real, filter_imag = forward_frequency_domain(filter_chan, outer_size, period)
    conv_chan = inverse_spectrum(
        carried_real * filter_real - carried_imag * filter_imag,
        carried_real * filter_imag + carried_imag * filter_real,
        sequence_count,
        period,
    )
    conv_rows = lax.all_to_all(
        conv_chan.reshape(1, narrow, length).astype(jnp.bfloat16),
        "seq",
        split_axis=2,
        concat_axis=0,
        tiled=True,
    ).astype(jnp.float32)
    long_out = conv_rows.reshape(model_width, row_count) + skip_gain[:, None] * carried
    act_pre = (second_gate * long_out).astype(jnp.bfloat16)
    branch_out = lax.dot_general(
        act_pre, w_out, (((0,), (0,)), ((), ())), preferred_element_type=jnp.float32
    )
    residual = inputs + branch_out + output_bias
    normed_two, norm_two_back = jax.vjp(layer_norm, residual, second_gain, second_shift)
    act_two = normed_two.astype(jnp.bfloat16)
    upper = jnp.dot(act_two, w_up, preferred_element_type=jnp.float32) + up_bias
    gelu_out, gelu_back = jax.vjp(jax.nn.gelu, upper)
    act_three = gelu_out.astype(jnp.bfloat16)
    result = residual + jnp.dot(act_three, w_down, preferred_element_type=jnp.float32) + down_bias
    block_out = result.astype(jnp.bfloat16)[None]
    grad_final = cotan_rows.astype(jnp.bfloat16)
    down_grad = lax.dot_general(
        act_three, grad_final, (((0,), (0,)), ((), ())), preferred_element_type=jnp.float32
    )
    down_bias_grad = jnp.sum(grad_final, 0, dtype=jnp.float32)
    grad_act_three = lax.dot_general(
        grad_final, w_down, (((1,), (1,)), ((), ())), preferred_element_type=jnp.float32
    )
    (grad_upper,) = gelu_back(grad_act_three)
    grad_upper = grad_upper.astype(jnp.bfloat16)
    up_grad = lax.dot_general(
        act_two, grad_upper, (((0,), (0,)), ((), ())), preferred_element_type=jnp.float32
    )
    up_bias_grad = jnp.sum(grad_upper, 0, dtype=jnp.float32)
    grad_norm_two = lax.dot_general(
        grad_upper, w_up, (((1,), (1,)), ((), ())), preferred_element_type=jnp.float32
    )
    grad_resid_norm, second_gain_grad, second_shift_grad = norm_two_back(grad_norm_two)
    grad_residual = cotan_rows + grad_resid_norm
    grad_branch = grad_residual.astype(jnp.bfloat16)
    output_grad = jnp.dot(act_pre, grad_branch, preferred_element_type=jnp.float32)
    output_bias_grad = jnp.sum(grad_branch, 0, dtype=jnp.float32)
    grad_pre = lax.dot_general(
        w_out, grad_branch, (((1,), (1,)), ((), ())), preferred_element_type=jnp.float32
    )
    grad_second = grad_pre * long_out
    grad_long = grad_pre * second_gate
    skip_gain_grad = jnp.sum(grad_long * carried, 1)
    grad_long_blocks = grad_long.reshape(sequence_count, narrow, row_count)
    grad_chan, carried_again, filter_again = (
        lax.all_to_all(
            grad_long_blocks.astype(jnp.bfloat16), "seq", split_axis=0, concat_axis=2, tiled=True
        ).astype(grad_long_blocks.dtype),
        lax.all_to_all(
            carried_blocks.astype(jnp.bfloat16), "seq", split_axis=0, concat_axis=2, tiled=True
        ).astype(carried_blocks.dtype),
        lax.all_to_all(
            filter_blocks.astype(jnp.bfloat16), "seq", split_axis=0, concat_axis=2, tiled=True
        ).astype(filter_blocks.dtype),
    )
    carried_real, carried_imag = forward_frequency_domain(
        carried_again.reshape(narrow, sequence_count, row_count), outer_size, period
    )
    filter_real, filter_imag = forward_frequency_domain(
        filter_again.reshape(narrow, sequence_count, row_count), outer_size, period
    )
    grad_real, grad_imag = forward_frequency_domain(
        grad_chan.reshape(narrow, sequence_count, row_count), outer_size, period
    )
    carried_back = inverse_spectrum(
        filter_real * grad_real + filter_imag * grad_imag,
        filter_real * grad_imag - filter_imag * grad_real,
        sequence_count,
        period,
    )
    filter_grad_chan = inverse_spectrum(
        carried_real * grad_real + carried_imag * grad_imag,
        carried_real * grad_imag - carried_imag * grad_real,
        sequence_count,
        period,
    )
    carried_got, filters_got = (
        lax.all_to_all(
            carried_back.reshape(1, narrow, length).astype(jnp.bfloat16),
            "seq",
            split_axis=2,
            concat_axis=0,
            tiled=True,
        ).astype(jnp.float32),
        lax.all_to_all(
            filter_grad_chan.reshape(1, narrow, length).astype(jnp.bfloat16),
            "seq",
            split_axis=2,
            concat_axis=0,
            tiled=True,
        ).astype(jnp.float32),
    )
    grad_carried = carried_got.reshape(model_width, row_count) + skip_gain[:, None] * grad_long
    grad_filters = filters_got.reshape(model_width, row_count)
    (
        feat_weight_grad,
        feat_bias_grad,
        feat_freq_grad,
        inner_weight_grad,
        inner_bias_grad,
        inner_freq_grad,
        filter_weight_grad,
    ) = filter_back(grad_filters)
    grad_conv = jnp.concatenate(
        [grad_carried * value_part, grad_second, grad_carried * leading_gate], 0
    )
    grad_padded, short_weight_grad, short_bias_grad = short_back(grad_conv)
    rim_grad = from_behind(grad_padded[:, :2], "seq", -1)
    grad_projected = jnp.concatenate(
        [grad_padded[:, 2:row_count], grad_padded[:, row_count:] + rim_grad], 1
    )
    grad_projected = grad_projected.astype(jnp.bfloat16)
    input_grad = lax.dot_general(
        act_one, grad_projected, (((0,), (1,)), ((), ())), preferred_element_type=jnp.float32
    )
    input_bias_grad = jnp.sum(grad_projected, 1, dtype=jnp.float32)
    first_norm_gradient = lax.dot_general(
        grad_projected, w_in, (((0,), (1,)), ((), ())), preferred_element_type=jnp.float32
    )
    grad_inputs, first_gain_grad, first_shift_grad = norm_one_back(first_norm_gradient)
    tokens_grad = (grad_inputs + grad_residual).astype(jnp.bfloat16)[None]
    input_weight_grad, output_weight_grad, up_weight_grad, down_weight_grad = (
        lax.psum_scatter(input_grad, ("dp", "seq"), scatter_dimension=0, tiled=True),
        lax.psum_scatter(output_grad, ("dp", "seq"), scatter_dimension=0, tiled=True),
        lax.psum_scatter(up_grad, ("dp", "seq"), scatter_dimension=0, tiled=True),
        lax.psum_scatter(down_grad, ("dp", "seq"), scatter_dimension=0, tiled=True),
    )
    (
        first_gain_grad,
        first_shift_grad,
        input_bias_grad,
        short_weight_grad,
        short_bias_grad,
        feat_weight_grad,
        feat_bias_grad,
        feat_freq_grad,
        inner_weight_grad,
        inner_bias_grad,
        inner_freq_grad,
        filter_weight_grad,
        skip_gain_grad,
        output_bias_grad,
        second_gain_grad,
        second_shift_grad,
        up_bias_grad,
        down_bias_grad,
    ) = lax.psum(
        (
            first_gain_grad,
            first_shift_grad,
            input_bias_grad,
            short_weight_grad,
            short_bias_grad,
            feat_weight_grad,
            feat_bias_grad,
            feat_freq_grad,
            inner_weight_grad,
            inner_bias_grad,
            inner_freq_grad,
            filter_weight_grad,
            skip_gain_grad,
            output_bias_grad,
            second_gain_grad,
            second_shift_grad,
            up_bias_grad,
            down_bias_grad,
        ),
        ("dp", "seq"),
    )
    return (
        block_out,
        tokens_grad,
        first_gain_grad,
        first_shift_grad,
        input_weight_grad,
        input_bias_grad,
        short_weight_grad,
        short_bias_grad,
        feat_weight_grad,
        feat_bias_grad,
        feat_freq_grad,
        inner_weight_grad,
        inner_bias_grad,
        inner_freq_grad,
        filter_weight_grad,
        skip_gain_grad,
        output_weight_grad,
        output_bias_grad,
        second_gain_grad,
        second_shift_grad,
        up_weight_grad,
        up_bias_grad,
        down_weight_grad,
        down_bias_grad,
    )


def solution(mesh):
    placed = (
        P("dp", "seq", None),
        P("dp", "seq", None),
        P(),
        P(),
        P(("dp", "seq"), None),
        P(),
        P(),
        P(),
        P(),
        P(),
        P(),
        P(),
        P(),
        P(),
        P(),
        P(),
        P(),
        P(("dp", "seq"), None),
        P(),
        P(),
        P(),
        P(("dp", "seq"), None),
        P(),
        P(("dp", "seq"), None),
        P(),
    )
    return jax.shard_map(
        on_device,
        mesh=mesh,
        in_specs=placed,
        out_specs=(
            P("dp", "seq", None),
            P("dp", "seq", None),
            P(),
            P(),
            P(("dp", "seq"), None),
            P(),
            P(),
            P(),
            P(),
            P(),
            P(),
            P(),
            P(),
            P(),
            P(),
            P(),
            P(("dp", "seq"), None),
            P(),
            P(),
            P(),
            P(("dp", "seq"), None),
            P(),
            P(("dp", "seq"), None),
            P(),
        ),
        check_vma=False,
    )
```

profile of v0, /device:TPU:0, one launch (start us, length us, event | category | flops | bytes accessed | tf_op | source)
XLA Modules:
  0.0 1481.1 jit_solution(3484503642572581542)
XLA Ops:
  15.4 7.4 all-to-all-start.1
  23.8 11.7 all-to-all-done.1
  36.9 2.2 fusion.80
  39.1 46.4 %all-gather.5.cloned.1.call-done = bf16[1024,3072]{1,0:T(8,128)(2,1)} async-done(((bf16[32,3072]{1,0:T(8,128)(2,1)}), bf16[1024,3072]{1,0:T(8,128)(2,1)}) %all-gather.5.cloned.1.call-update) | async-done | bytes 6291472 | tf_op jit(solution)/shard_map/all_gather | solution.py:152
  85.6 4.0 fusion
  89.6 2.3 collective-permute-start
  91.9 2.2 convolution_subtract_fusion.4
  96.8 5.0 all-to-all-start
  103.0 2.2 convolution_add_fusion.6
  105.2 6.6 all-to-all-done
  117.2 2.4 multiply_add_fusion.4
  127.9 11.5 reduce.1
  139.9 13.4 all_to_all.82
  157.7 2.2 fusion.393
  161.5 61.6 %all-gather.9.cloned.1.call-done = bf16[1024,4096]{1,0:T(8,128)(2,1)} async-done(((bf16[32,4096]{1,0:T(8,128)(2,1)}), bf16[1024,4096]{1,0:T(8,128)(2,1)}) %all-gather.9.cloned.1.call-update) | async-done | bytes 8388624 | tf_op jit(solution)/shard_map/all_gather | solution.py:154
  223.1 6.1 convolution_add_fusion
  229.2 72.9 %all-gather.11.cloned.1.call-done = bf16[4096,1024]{1,0:T(8,128)(2,1)} async-done(((bf16[128,1024]{1,0:T(8,128)(2,1)}), bf16[4096,1024]{1,0:T(8,128)(2,1)}) %all-gather.11.cloned.1.call-update) | async-done | bytes 8388624 | tf_op jit(solution)/shard_map/all_gather | solution.py:155
  302.0 8.4 convert_reduce_fusion
  310.4 3.6 multiply_reduce_fusion.3
  315.9 2.3 multiply_reduce_fusion.4
  319.2 14.1 all_to_all.83
  339.3 2.7 multiply_subtract_fusion
  344.4 2.2 fusion.115
  346.6 2.2 fusion.131
  355.0 2.0 copy.117
  356.9 12.6 reduce.3
  370.6 4.6 all-to-all-start.5
  375.2 2.9 convolution_add_fusion.3
  384.8 12.6 reduce.2
  398.5 6.1 all-to-all-start.4
  404.7 3.6 reshape.309
  408.2 3.4 copy.118
  415.0 2.2 multiply_reduce_fusion.7
  420.4 3.4 reshape.307
  423.8 2.3 copy.114
  427.2 2.1 copy.116
  438.2 2.8 fusion.388
  445.2 2.7 fusion.394
  448.0 6.4 fusion.106
  456.0 8.1 fusion.86
  464.8 9.5 fusion.386
  474.9 5.7 fusion.26
  480.6 159.9 %all-reduce.12.cloned.1.call-done = (f32[1024]{0:T(1024)}, f32[1024]{0:T(1024)}, f32[3072]{0:T(1024)}, f32[3,3072]{1,0:T(4,128)}, f32[3072]{0:T(1024)}, /*index=...) async-done(((f32[1024]{0:T(1024)}, f32[1024]{0:T(1024)}, ...) | async-done | bytes 132368 | tf_op jit(solution)/shard_map/psum | solution.py:356
  640.5 135.1 %all-reduce.10.cloned.1.call-done = f32[64,1024]{1,0:T(8,128)} async-done(((f32[64,1024]{1,0:T(8,128)}), f32[64,1024]{1,0:T(8,128)}) %all-reduce.10.cloned.1.call-update) | async-done | bytes 262160 | tf_op jit(solution)/shard_map/psum | solution.py:356
  775.6 143.5 %reduce-scatter.7.cloned.1.call-done = f32[32,1024]{1,0:T(8,128)} async-done(((f32[1024,1024]{1,0:T(8,128)}), f32[32,1024]{1,0:T(8,128)}) %reduce-scatter.7.cloned.1.call-update) | async-done | bytes 131088 | tf_op jit(solution)/shard_map/reduce_scatter | solution.py:333
  919.1 158.2 %reduce-scatter.5.cloned.1.call-done = f32[32,3072]{1,0:T(8,128)} async-done(((f32[1024,3072]{1,0:T(8,128)}), f32[32,3072]{1,0:T(8,128)}) %reduce-scatter.5.cloned.1.call-update) | async-done | bytes 393232 | tf_op jit(solution)/shard_map/reduce_scatter | solution.py:332
  1077.4 185.8 %reduce-scatter.11.cloned.1.call-done = f32[128,1024]{1,0:T(8,128)} async-done(((f32[4096,1024]{1,0:T(8,128)}), f32[128,1024]{1,0:T(8,128)}) %reduce-scatter.11.cloned.1.call-update) | async-done | bytes 524304 | tf_op jit(solution)/shard_map/reduce_scatter | solution.py:335
  1263.2 187.6 %reduce-scatter.9.cloned.1.call-done = f32[32,4096]{1,0:T(8,128)} async-done(((f32[1024,4096]{1,0:T(8,128)}), f32[32,4096]{1,0:T(8,128)}) %reduce-scatter.9.cloned.1.call-update) | async-done | bytes 524304 | tf_op jit(solution)/shard_map/reduce_scatter | solution.py:334
  (289 shorter events, 106.9 us)
Async XLA Ops:
  7.2 5.9 copy-start
  7.2 15.6 %copy-start.3 = (bf16[1,128,1024]{2,1,0:T(8,128)(2,1)S(1)}, bf16[1,128,1024]{2,1,0:T(8,128)(2,1)}, u32[]{:S(2)}) copy-start(bf16[1,128,1024]{2,1,0:T(8,128)(2,1)} %param.25) | copy-start | bytes 786436
  7.2 16.5 %copy-start.47 = (f32[3,3072]{1,0:T(4,128)S(1)}, f32[3,3072]{1,0:T(4,128)}, u32[]{:S(2)}) copy-start(f32[3,3072]{1,0:T(4,128)} %param.31) | copy-start | bytes 110596
  7.2 78.3 %all-gather.5.cloned.1.call-start = ((), (), s32[]{:S(2)}) async-start(), calls=%async_computation.10 | async-start | bytes 6488064 | tf_op jit(solution)/shard_map/all_gather | solution.py:152
  8.0 149.8 %all-gather.7.cloned.1.call-start = ((), (), s32[]{:S(2)}) async-start(), calls=%async_computation.11 | async-start | bytes 2162688 | tf_op jit(solution)/shard_map/all_gather | solution.py:153
  8.7 214.4 %all-gather.9.cloned.1.call-start = ((), (), s32[]{:S(2)}) async-start(), calls=%async_computation.12 | async-start | bytes 8650752 | tf_op jit(solution)/shard_map/all_gather | solution.py:154
  9.4 292.6 %all-gather.11.cloned.1.call-start = ((), (), s32[]{:S(2)}) async-start(), calls=%async_computation.13 | async-start | bytes 8650752 | tf_op jit(solution)/shard_map/all_gather | solution.py:155
  10.7 12.5 copy-start.65
  10.8 12.5 copy-start.60
  11.9 11.3 copy-start.45
  15.4 20.1 %all-to-all-start.1 = ((bf16[16,64,128]{2,1,0:T(8,128)(2,1)}), bf16[16,64,128]{2,1,0:T(8,128)(2,1)S(1)}, u32[]{:S(2)}, u32[]{:S(2)}) async-start(bf16[16,64,128]{2,1,0:T(8,128)(2,1)} %bitcast.18), calls=%async_computation.1 | async-start | bytes 524288 | tf_op jit(solution)/shard_map/all_to_all | solution.py:191
  23.0 62.6 %copy-start.48 = (f32[128]{0:T(128)}, f32[128]{0:T(128)S(1)}, u32[]{:S(2)}) copy-start(f32[128]{0:T(128)S(1)} %broadcast_multiply_fusion.4) | copy-start | bytes 1540
  23.8 61.8 %copy-start.53 = (f32[128]{0:T(128)}, f32[128]{0:T(128)S(1)}, u32[]{:S(2)}) copy-start(f32[128]{0:T(128)S(1)} %fusion.233) | copy-start | bytes 1540
  36.2 49.4 %copy-start.34 = (f32[1024]{0:T(1024)S(1)}, f32[1024]{0:T(1024)}, u32[]{:S(2)}) copy-start(f32[1024]{0:T(1024)} %param.27) | copy-start | bytes 12292
  36.2 49.4 %copy-start.36 = (f32[1024]{0:T(1024)S(1)}, f32[1024]{0:T(1024)}, u32[]{:S(2)}) copy-start(f32[1024]{0:T(1024)} %param.28) | copy-start | bytes 12292
  36.2 49.4 %copy-start.57 = (f32[3072]{0:T(1024)S(1)}, f32[3072]{0:T(1024)}, u32[]{:S(2)}) copy-start(f32[3072]{0:T(1024)} %param.30) | copy-start | bytes 36868
  85.6 6.3 copy-start.28
  89.5 4.6 copy-start.4
  89.6 4.6 copy-start.58
  89.6 4.5 collective-permute-start
  96.8 15.1 %all-to-all-start = ((bf16[16,64,128]{2,1,0:T(8,128)(2,1)}), bf16[16,64,128]{2,1,0:T(8,128)(2,1)S(1)}, u32[]{:S(2)}, u32[]{:S(2)}) async-start(bf16[16,64,128]{2,1,0:T(8,128)(2,1)} %bitcast.277), calls=%async_computation | async-start | bytes 524288 | tf_op jit(solution)/shard_map/all_to_all | solution.py:188
  157.7 65.4 %copy-start.35 = (f32[1024]{0:T(1024)S(1)}, f32[1024]{0:T(1024)}, u32[]{:S(2)}) copy-start(f32[1024]{0:T(1024)} %param.44) | copy-start | bytes 12292
  157.7 65.4 %copy-start.37 = (f32[1024]{0:T(1024)S(1)}, f32[1024]{0:T(1024)}, u32[]{:S(2)}) copy-start(f32[1024]{0:T(1024)} %param.45) | copy-start | bytes 12292
  161.5 140.5 %copy-start.29 = (bf16[1,128,1024]{2,1,0:T(8,128)(2,1)S(1)}, bf16[1,128,1024]{2,1,0:T(8,128)(2,1)}, u32[]{:S(2)}) copy-start(bf16[1,128,1024]{2,1,0:T(8,128)(2,1)} %param.26) | copy-start | bytes 786436
  302.0 8.4 copy-start.2
  302.0 8.4 copy-start.51
  302.0 8.4 copy-start.55
  310.4 3.6 copy-start.25
  310.4 3.6 copy-start.70
  370.6 27.9 %all-to-all-start.5 = ((bf16[16,2,4096]{2,1,0:T(2,128)(2,1)}), bf16[16,2,4096]{2,1,0:T(2,128)(2,1)}, u32[]{:S(2)}, u32[]{:S(2)}) async-start(bf16[16,2,4096]{2,1,0:T(2,128)(2,1)} %reshape.308), calls=%async_computation.6 | async-start | bytes 524288 | tf_op jit(solution)/shard_map/all_to_all | solution.py:294
  398.5 21.9 %all-to-all-start.4 = ((bf16[16,2,4096]{2,1,0:T(2,128)(2,1)}), bf16[16,2,4096]{2,1,0:T(2,128)(2,1)}, u32[]{:S(2)}, u32[]{:S(2)}) async-start(bf16[16,2,4096]{2,1,0:T(2,128)(2,1)} %reshape.306), calls=%async_computation.4 | async-start | bytes 524288 | tf_op jit(solution)/shard_map/all_to_all | solution.py:287
  404.6 235.8 %all-reduce.12.cloned.1.call-start = ((), (), s32[]{:S(2)}) async-start(), calls=%async_computation.19 | async-start | bytes 348160 | tf_op jit(solution)/shard_map/psum | solution.py:356
  412.6 4.5 copy-start.46
  415.0 11.2 copy-start.22
  427.2 3.5 copy-start.21
  433.5 4.6 slice-start
  433.6 4.6 slice-start.1
  434.0 3.4 collective-permute-start.1
  438.2 3.8 copy-start.20
  438.2 3.8 copy-start.64
  441.0 4.1 copy-start.31
  441.0 4.1 copy-start.33
  443.6 332.0 %all-reduce.10.cloned.1.call-start = ((), (), s32[]{:S(2)}) async-start(), calls=%async_computation.15 | async-start | bytes 524288 | tf_op jit(solution)/shard_map/psum | solution.py:356
  445.1 474.0 %reduce-scatter.7.cloned.1.call-start = ((), (), s32[]{:S(2)}) async-start(), calls=%async_computation.16 | async-start | bytes 4325376 | tf_op jit(solution)/shard_map/reduce_scatter | solution.py:333
  447.9 629.4 %reduce-scatter.5.cloned.1.call-start = ((), (), s32[]{:S(2)}) async-start(), calls=%async_computation.14 | async-start | bytes 12976128 | tf_op jit(solution)/shard_map/reduce_scatter | solution.py:332
  454.4 808.8 %reduce-scatter.11.cloned.1.call-start = ((), (), s32[]{:S(2)}) async-start(), calls=%async_computation.18 | async-start | bytes 17301504 | tf_op jit(solution)/shard_map/reduce_scatter | solution.py:335
  464.1 986.7 %reduce-scatter.9.cloned.1.call-start = ((), (), s32[]{:S(2)}) async-start(), calls=%async_computation.17 | async-start | bytes 17301504 | tf_op jit(solution)/shard_map/reduce_scatter | solution.py:334
  474.9 999.1 %copy-start.1 = (f32[64,1024]{1,0:T(8,128)S(1)}, f32[64,1024]{1,0:T(8,128)}, u32[]{:S(2)}) copy-start(f32[64,1024]{1,0:T(8,128)} %param.39) | copy-start | bytes 786436
  (42 other events, 77.3 us)
Sparse Core Ops, SparseCore 0:
  11.0 74.5 all-gather.4
  88.4 55.5 all-gather.6
  146.9 76.1 all-gather.8
  225.8 76.1 all-gather.10
  443.7 196.7 all-reduce.11
  648.6 126.8 all-reduce.9
  778.4 140.6 reduce-scatter.6
  925.7 151.5 reduce-scatter.4
  1080.3 182.8 reduce-scatter.10
  1266.0 184.7 reduce-scatter.8
where the time goes:
time: 1490 us; the launch traced here: 1480 us
  waiting for transfers between devices  1170 us (79%)
  matrix products  123 us (8%)
  local copies, waits for them, and re-layouts  66.8 us (4%)
  other arithmetic  48.8 us (3%)
  starting transfers between devices  27.6 us (2%)
  blocking collectives  27.5 us (2%)
  between operations  15.6 us (1%)
    psum x2, waiting for transfers between devices, on_device(): lax.psum((first_gain_grad, first_shift_grad, input_bias_grad, short_weigh...  295 us
    reduce_scatter x1, waiting for transfers between devices, on_device(): lax.psum_scatter(up_grad, ('dp', 'seq'), scatter_dimension=0, tiled=True)  188 us
    reduce_scatter x1, waiting for transfers between devices, on_device(): lax.psum_scatter(down_grad, ('dp', 'seq'), scatter_dimension=0, tiled=True)  186 us
    reduce_scatter x1, waiting for transfers between devices, on_device(): lax.psum_scatter(input_grad, ('dp', 'seq'), scatter_dimension=0, tiled=True)  158 us
    reduce_scatter x1, waiting for transfers between devices, on_device(): lax.psum_scatter(output_grad, ('dp', 'seq'), scatter_dimension=0, tiled=T...  144 us
    all_gather x1, waiting for transfers between devices, on_device(): lax.all_gather(down_weight, ('dp', 'seq'), axis=0, tiled=True)  72.9 us
    all_gather x1, waiting for transfers between devices, on_device(): lax.all_gather(up_weight, ('dp', 'seq'), axis=0, tiled=True)  61.6 us
    all_gather x1, waiting for transfers between devices, on_device(): lax.all_gather(input_weight, ('dp', 'seq'), axis=0, tiled=True)  46.4 us
  transfers between devices with their start and end apart: 16, of which 11 were waited for; matrix products, arithmetic and copies ran while one was open for 9% of the time, Pallas kernels for 0%

commit v1 on v0

--- a/solution.py
+++ b/solution.py
@@ -1,12 +1,19 @@
 import functools
 import math
+import types
+from typing import NamedTuple
 
 import jax
 import jax.numpy as jnp
+import ml_dtypes
+import numpy as np
 from jax import lax
+from jax.experimental import pallas as pl
+from jax.experimental.pallas import tpu as pltpu
 from jax.sharding import PartitionSpec as P
 
 FEAT = 33
+FILT = 64
 
 
 exact_precision = lax.Precision.HIGHEST
@@ -404,6 +411,1197 @@
     )
 
 
+f32 = jnp.float32
+bf16 = jnp.bfloat16
+ON_MESH = pl.DeviceIdType.MESH
+INNER = 4
+LANES = 128
+CT_FILTER = 64
+PS_ROWS = 256
+AT_VECTOR = 64
+AT_SECOND_GAIN = 96
+AT_SECOND_SHIFT = 104
+AT_OUTPUT_BIAS = 112
+AT_DOWN_BIAS = 120
+AT_FIRST_GAIN = 128
+AT_FIRST_SHIFT = 136
+AT_UP_BIAS = 144
+AT_FEAT = 176
+
+
+def dot_nn(a, b, precision=None):
+    return lax.dot_general(
+        a, b, (((1,), (0,)), ((), ())), precision=precision, preferred_element_type=f32
+    )
+
+
+def dot_nt(a, b, precision=None):
+    return lax.dot_general(
+        a, b, (((1,), (1,)), ((), ())), precision=precision, preferred_element_type=f32
+    )
+
+
+def step_at(index, size):
+    return pl.ds(pl.multiple_of(index * size, size), size)
+
+
+def times_unit(value, turns):
+    re, im = value
+    c, s = math.cos(2 * math.pi * turns), math.sin(2 * math.pi * turns)
+    if abs(s) < 1e-12:
+        return (re, im) if c > 0 else (-re, -im)
+    if abs(c) < 1e-12:
+        return (-im, re) if s > 0 else (im, -re)
+    return re * c - im * s, re * s + im * c
+
+
+def small_transform(values, sign):
+    size = len(values)
+    if size == 1:
+        return values
+    even = small_transform(values[0::2], sign)
+    odd = small_transform(values[1::2], sign)
+    turned = [times_unit(odd[k], sign * k / size) for k in range(size // 2)]
+    return [(e[0] + t[0], e[1] + t[1]) for e, t in zip(even, turned)] + [
+        (e[0] - t[0], e[1] - t[1]) for e, t in zip(even, turned)
+    ]
+
+
+@functools.lru_cache(None)
+def constant_tables(blocks, lanes):
+    length = blocks * lanes
+    n2 = np.arange(lanes)
+    angle = 2 * np.pi * np.outer(n2, n2) / lanes
+    c, s = np.cos(angle), np.sin(angle)
+    forth = np.block([[c, -s], [s, c]])
+    back = np.block([[c, s], [-s, c]])
+
+    def split(x):
+        high = x.astype(ml_dtypes.bfloat16)
+        return high, (x - high.astype(np.float64)).astype(ml_dtypes.bfloat16)
+
+    turn = 2 * np.pi * np.outer(np.arange(blocks) + 0.25, n2) / length
+    turns = np.concatenate([np.cos(turn), np.sin(turn)], 1).astype(np.float32)
+    rates = 1e-4 + np.arange((FEAT - 1) // 2) * ((15.0 - 1e-4) / 15.0)
+    phase = (2 * np.pi * np.arange(length) / length)[None, :] * rates[:, None]
+    ramp = (np.arange(length) / (length - 1))[None, :]
+    features = np.concatenate([ramp, np.cos(phase), -np.sin(phase)], 0)
+    features = np.pad(features, ((0, -FEAT % 8), (0, 0))).astype(np.float32)
+    return split(forth) + split(back) + (turns, features)
+
+
+def split_dot(x, high, low):
+    head = x.astype(bf16)
+    tail = (x - head.astype(f32)).astype(bf16)
+    return dot_nn(head, high) + dot_nn(tail, high) + dot_nn(head, low)
+
+
+def sin_cos(x):
+    count = jnp.floor(x * (2 / math.pi) + 0.5)
+    r = x - count * 1.5703125
+    r = r - count * 4.837512969970703e-4
+    r = r - count * 7.549789948768648e-8
+    r2 = r * r
+    s = r + r * r2 * (-1.6666654611e-1 + r2 * (8.3321608736e-3 + r2 * -1.9515295891e-4))
+    c = 1.0 - 0.5 * r2 + r2 * r2 * (
+        4.166664568298827e-2 + r2 * (-1.388731625493765e-3 + r2 * 2.443315711809948e-5)
+    )
+    quarter = count - 4.0 * jnp.floor(count * 0.25)
+    odd = (quarter == 1.0) | (quarter == 3.0)
+    sine = jnp.where(odd, c, s)
+    cosine = jnp.where(odd, s, c)
+    sine = jnp.where(quarter >= 2.0, -sine, sine)
+    cosine = jnp.where((quarter == 1.0) | (quarter == 2.0), -cosine, cosine)
+    return sine, cosine
+
+
+class Inputs(NamedTuple):
+    tokens: jax.Array
+    cotangent: jax.Array
+    first_gain: jax.Array
+    first_shift: jax.Array
+    input_weight: jax.Array
+    input_bias: jax.Array
+    short_weight: jax.Array
+    short_bias: jax.Array
+    feat_weight: jax.Array
+    feat_bias: jax.Array
+    feat_freq: jax.Array
+    inner_weight: jax.Array
+    inner_bias: jax.Array
+    inner_freq: jax.Array
+    filter_weight: jax.Array
+    skip_gain: jax.Array
+    decay_rates: jax.Array
+    output_weight: jax.Array
+    output_bias: jax.Array
+    second_gain: jax.Array
+    second_shift: jax.Array
+    up_weight: jax.Array
+    up_bias: jax.Array
+    down_weight: jax.Array
+    down_bias: jax.Array
+    forth_high: jax.Array
+    forth_low: jax.Array
+    back_high: jax.Array
+    back_low: jax.Array
+    turns: jax.Array
+    features: jax.Array
+
+
+def scratch_buffers(g):
+    tok, width, pt, ch = g.tok, g.width, g.plane_tokens, g.chan
+    ff, blocks = g.ff_part, g.blocks
+    return dict(
+        w_in=((width, 3 * LANES), bf16),
+        w_in_send=((g.members * g.rows, 3 * LANES), bf16),
+        w_up_send=((g.members * g.rows, ff), bf16),
+        w_in_t=((3 * LANES, width), bf16),
+        w_out=((width, width), bf16),
+        w_up=((width, ff), bf16),
+        w_down=((ff, width), bf16),
+        act_one=((pt, width), bf16),
+        act_two=((pt, width), bf16),
+        cotan=((pt, width), bf16),
+        proj_send=((3 * LANES, pt), bf16),
+        proj_recv=((3 * LANES, pt), bf16),
+        square=((LANES, LANES), f32),
+        param_cols=((LANES, LANES), f32),
+        taps=((4, 3 * ch, LANES), f32),
+        skip=((ch, LANES), f32),
+        decay=((ch, LANES), f32),
+        net_weights=((4, LANES, LANES), f32),
+        net_cols=((LANES, LANES), f32),
+        p_one=((FILT, g.length), f32),
+        hid_one=((FILT, g.length), f32),
+        cos_one=((FILT, g.length), f32),
+        p_two=((FILT, g.length), f32),
+        hid_two=((LANES, g.length), f32),
+        cos_two=((FILT, g.length), f32),
+        filt=((blocks, ch, LANES), f32),
+        padded=((2, blocks + 1, 3 * ch, LANES), f32),
+        conv=((2 * blocks, 3 * ch, LANES), f32),
+        carried=((blocks, 2 * ch, LANES), f32),
+        long=((blocks, 2 * ch, LANES), f32),
+        grad_long=((blocks, 2 * ch, LANES), f32),
+        grad_conv=((2, blocks + 1, 3 * ch, LANES), f32),
+        stage=((blocks, 2 * ch, 2 * LANES), f32),
+        stage_filt=((blocks, ch, 2 * LANES), f32),
+        spec_filt=((blocks, ch, 2 * LANES), f32),
+        spec_car=((blocks, 2 * ch, 2 * LANES), f32),
+        spec_grad=((blocks, 2 * ch, 2 * LANES), f32),
+        back_sig=((blocks, 2 * ch, LANES), f32),
+        back_filt=((blocks, ch, LANES), f32),
+        sums=((6, 3 * ch, LANES), f32),
+        pre_send=((width, tok), bf16),
+        pre_recv=((width, tok), bf16),
+        gpre_send=((width, tok), bf16),
+        gpre_recv=((width, tok), bf16),
+        residual=((tok, width), f32),
+        xhat_two=((tok, width), f32),
+        xhat_one=((tok, width), f32),
+        grad_res=((tok, width), f32),
+        grad_branch=((tok, width), bf16),
+        act_three=((pt, ff), bf16),
+        grad_up=((pt, ff), bf16),
+        up_send=((width, ff), bf16),
+        down_send=((ff, width), bf16),
+        in_send=((width, 3 * LANES), bf16),
+        out_sum=((LANES, width), bf16),
+        gproj_send=((3 * LANES, pt), bf16),
+        gproj_recv=((3 * LANES, pt), bf16),
+        ct=((width, LANES), f32),
+        ps=((PS_ROWS, LANES), f32),
+        ps_recv=((PS_ROWS, LANES), f32),
+        ps_all=((PS_ROWS, LANES), f32),
+        gn_two_own=((pt, width), bf16),
+        gn_two_send=((pt // 2, width), bf16),
+        gn_two_sib=((pt // 2, width), bf16),
+        gn_two_recv=((3 * tok, width), bf16),
+        result_own=((pt, width), bf16),
+        result_send=((pt // 2, width), bf16),
+        result_sib=((pt // 2, width), bf16),
+        result_recv=((3 * tok, width), bf16),
+        w_out_grad_sib=((pt // 2, width), bf16),
+        w_out_grad_recv=((3 * tok, width), bf16),
+        gn_one_sib=((pt // 2, width), bf16),
+        gn_one_recv=((3 * tok, width), bf16),
+    )
+
+
+SEMAPHORES = dict(
+    w_in=32,
+    w_up=32,
+    up_grad=32,
+    in_grad=32,
+    pre=32,
+    gpre=32,
+    ps=32,
+    ps_back=32,
+    w_down=8,
+    w_out_z=8,
+    proj=8,
+    gproj=8,
+    down_grad=8,
+    out_grad=8,
+    ct_z=8,
+    act_one=8,
+    act_two=8,
+    cotan=8,
+    w_out=32,
+    ct=8,
+    gn_two=8,
+    result=8,
+    w_out_grad=8,
+    gn_one=8,
+)
+
+
+class Geometry:
+    def __init__(self, n_dp, n_seq, tok, width, hidden, rows, down_rows):
+        self.n_dp, self.n_seq = n_dp, n_seq
+        self.devices = n_dp * n_seq
+        self.planes = n_seq // INNER
+        self.members = n_dp * INNER
+        self.chips = self.members // 2
+        self.tok, self.width, self.hidden = tok, width, hidden
+        self.rows, self.down_rows = rows, down_rows
+        self.plane_tokens = self.members * tok
+        self.length = n_seq * tok
+        self.blocks = n_seq
+        self.ff_part = hidden // self.members
+        self.chan = LANES // max(self.planes, 1)
+
+    def fits(self):
+        return (
+            self.n_dp == 2
+            and self.n_seq % INNER == 0
+            and self.tok == LANES
+            and self.width == self.members * LANES
+            and self.down_rows % LANES == 0
+            and self.rows % 16 == 0
+            and self.chan % 16 == 0
+            and self.down_rows * self.planes == self.ff_part
+        )
+
+
+class Net:
+    def __init__(self, g):
+        self.g = g
+        self.x, self.s = lax.axis_index("dp"), lax.axis_index("seq")
+        self.z, self.q = self.s // INNER, self.s % INNER
+        self.m = self.x * INNER + self.q
+        self.p, self.c = self.m // 2, self.m % 2
+        self.flat = self.x * g.n_seq + self.s
+        self.sib = 2 * self.p + 1 - self.c
+        self.chan_block = self.m * g.planes + self.z
+        self.ends = []
+
+    def device(self, flat):
+        return (flat // self.g.n_seq, flat % self.g.n_seq)
+
+    def member(self, m):
+        return (m // INNER, self.z * INNER + m % INNER)
+
+    def in_plane(self, z):
+        return (self.x, z * INNER + self.q)
+
+    def copy(self, src, dst, sems, k, device, sent=None):
+        send, recv = sems
+        return pltpu.make_async_remote_copy(
+            src_ref=src,
+            dst_ref=dst,
+            send_sem=send.at[k if sent is None else sent],
+            recv_sem=recv.at[k],
+            device_id=device,
+            device_id_type=ON_MESH,
+        )
+
+    def finish(self):
+        for end in self.ends:
+            end()
+
+
+class ToAll:
+    def __init__(self, net, sems, src, dst):
+        self.net, self.sems, self.src, self.dst = net, sems, src, dst
+        net.ends.append(self.wait_send)
+
+    def one(self, j):
+        net = self.net
+        target = lax.rem(net.flat + j, net.g.devices)
+        return net.copy(self.src(target), self.dst, self.sems, j, net.device(target))
+
+    def each(self, act):
+        @pl.loop(1, self.net.g.devices)
+        def _(j):
+            act(self.one(j))
+
+    def start(self):
+        self.each(lambda copy: copy.start())
+
+    def wait(self):
+        self.each(lambda copy: copy.wait_recv())
+
+    def wait_send(self):
+        self.each(lambda copy: copy.wait_send())
+
+
+class AlongPlanes:
+    def __init__(self, net, sems, src, dst):
+        self.net, self.sems, self.src, self.dst = net, sems, src, dst
+        net.ends.append(self.wait_send)
+
+    def each(self, act):
+        net = self.net
+        for j in range(1, net.g.planes):
+            z = lax.rem(net.z + j, net.g.planes)
+            act(net.copy(self.src(z), self.dst, self.sems, j, net.in_plane(z)))
+
+    def start(self):
+        self.each(lambda copy: copy.start())
+
+    def wait(self):
+        self.each(lambda copy: copy.wait_recv())
+
+    def wait_send(self):
+        self.each(lambda copy: copy.wait_send())
+
+
+class PlaneGather:
+    def __init__(self, net, sems, piece, base=0):
+        self.net, self.sems, self.piece, self.base = net, sems, piece, base
+        net.ends.append(self.wait_send)
+
+    def peer(self, j):
+        return 2 * lax.rem(self.net.p + j, self.net.g.chips) + self.net.c
+
+    def source(self, j):
+        return 2 * lax.rem(self.net.p + self.net.g.chips - j, self.net.g.chips) + self.net.c
+
+    def across(self, j):
+        net = self.net
+        mine = self.piece(net.m)
+        return net.copy(mine, mine, self.sems, self.base + j, net.member(self.peer(j)))
+
+    def beside(self, j):
+        net = self.net
+        held = self.piece(self.source(j) if j else net.m)
+        return net.copy(held, held, self.sems, self.base + net.g.chips + j, net.member(net.sib))
+
+    def start(self):
+        for j in range(1, self.net.g.chips):
+            self.across(j).start()
+        self.beside(0).start()
+
+    def forward(self, j):
+        self.across(j).wait_recv()
+        self.beside(j).start()
+
+    def wait(self, j):
+        self.beside(j).wait_recv()
+
+    def forward_all(self):
+        for j in range(1, self.net.g.chips):
+            self.forward(j)
+
+    def wait_all(self):
+        for j in range(self.net.g.chips):
+            self.wait(j)
+
+    def wait_send(self):
+        for j in range(1, self.net.g.chips):
+            self.across(j).wait_send()
+        for j in range(self.net.g.chips):
+            self.beside(j).wait_send()
+
+
+class PlaneSum:
+    def __init__(self, net, sems, sib, recv, own=None, send=None, after=None):
+        self.net, self.sems, self.sib, self.recv = net, sems, sib, recv
+        if after is None:
+            self.own, self.send = own, send
+        else:
+            self.own, self.send = after.own, after.send
+            after.wait_send()
+            net.ends.remove(after.wait_send)
+        net.ends.append(self.wait_send)
+
+    def block(self, ref, k):
+        return ref.at[step_at(k, self.net.g.tok)]
+
+    def beside(self, chip):
+        net = self.net
+        return net.copy(
+            self.block(self.own, 2 * chip + 1 - net.c), self.block(self.sib, chip), self.sems, chip, net.member(net.sib)
+        )
+
+    def across(self, j):
+        net = self.net
+        chip = lax.rem(net.p + j, net.g.chips)
+        return net.copy(
+            self.block(self.send, chip),
+            self.block(self.recv, j - 1),
+            self.sems,
+            net.g.chips + j,
+            net.member(2 * chip + net.c),
+        )
+
+    def start(self, chip):
+        self.beside(chip).start()
+
+    def pair(self, chip):
+        self.beside(chip).wait_recv()
+        mine = self.own[step_at(2 * chip + self.net.c, self.net.g.tok), :].astype(f32)
+        return mine + self.sib[step_at(chip, self.net.g.tok), :].astype(f32)
+
+    def relay(self, j):
+        chip = lax.rem(self.net.p + j, self.net.g.chips)
+        self.send[step_at(chip, self.net.g.tok), :] = self.pair(chip).astype(bf16)
+        self.across(j).start()
+
+    def result(self):
+        total = self.pair(self.net.p)
+        tok = self.net.g.tok
+        for j in range(1, self.net.g.chips):
+            self.across(j).wait_recv()
+            total = total + self.recv[(j - 1) * tok : j * tok, :].astype(f32)
+        return total
+
+    def wait_send(self):
+        for chip in range(self.net.g.chips):
+            self.beside(chip).wait_send()
+        for j in range(1, self.net.g.chips):
+            self.across(j).wait_send()
+
+
+def to_rows(ref, at, row):
+    for k in range(row.shape[1] // LANES):
+        ref[at + k : at + k + 1, :] = row[:, k * LANES : (k + 1) * LANES]
+
+
+def column_sum(x):
+    return jnp.sum(x, 0, keepdims=True)
+
+
+def normalized(x):
+    center = x - jnp.mean(x, -1, keepdims=True)
+    inverse = lax.rsqrt(jnp.mean(center * center, -1, keepdims=True) + 1e-5)
+    return center * inverse, inverse
+
+
+def norm_back(grad, xhat, inverse, gain):
+    e = grad * gain
+    return (e - jnp.mean(e, -1, keepdims=True) - xhat * jnp.mean(e * xhat, -1, keepdims=True)) * inverse
+
+
+def gelu_pair(v):
+    scale = math.sqrt(2 / math.pi)
+    v2 = v * v
+    t = jnp.tanh(scale * v * (1.0 + 0.044715 * v2))
+    half = 0.5 * (1.0 + t)
+    return v * half, half + 0.5 * v * (1.0 - t * t) * (scale * (1.0 + 3 * 0.044715 * v2))
+
+
+def to_spectrum(g, signal, rows, stage, turns, high, low, out):
+    @pl.loop(0, rows // 8)
+    def _(step):
+        at = step_at(step, 8)
+        first = []
+        for n in range(g.blocks):
+            block = signal[n, at, :]
+            angle = -2 * math.pi * n / (4 * g.blocks)
+            first.append((block * math.cos(angle), block * math.sin(angle)))
+        for k, (re, im) in enumerate(small_transform(first, -1)):
+            c, s = turns[k : k + 1, :LANES], turns[k : k + 1, LANES:]
+            stage[k, at, :LANES] = re * c + im * s
+            stage[k, at, LANES:] = im * c - re * s
+
+    group = 256 // rows
+
+    @pl.loop(0, g.blocks // group)
+    def _(step):
+        at = step_at(step, group)
+        x = stage[at].reshape(group * rows, 2 * LANES)
+        out[at] = split_dot(x, high[...], low[...]).reshape(group, rows, 2 * LANES)
+
+
+def from_spectrum(g, product, rows, stage, turns, high, low, signal):
+    group = 256 // rows
+
+    @pl.loop(0, g.blocks // group)
+    def _(step):
+        at = step_at(step, group)
+        re, im = product(at)
+        x = jnp.concatenate([re, im], -1).reshape(group * rows, 2 * LANES)
+        stage[at] = split_dot(x, high[...], low[...]).reshape(group, rows, 2 * LANES)
+
+    @pl.loop(0, rows // 8)
+    def _(step):
+        at = step_at(step, 8)
+        values = []
+        for k in range(g.blocks):
+            re, im = stage[k, at, :LANES], stage[k, at, LANES:]
+            c, s = turns[k : k + 1, :LANES], turns[k : k + 1, LANES:]
+            values.append((re * c - im * s, re * s + im * c))
+        for n, (re, im) in enumerate(small_transform(values, 1)):
+            angle = 2 * math.pi * n / (4 * g.blocks)
+            signal[n, at, :] = (re * math.cos(angle) - im * math.sin(angle)) * (1.0 / g.length)
+
+
+def halves(x):
+    return x[..., :LANES], x[..., LANES:]
+
+
+def later(here, before, by):
+    lane = lax.broadcasted_iota(jnp.int32, here.shape, 1)
+    return jnp.where(lane < by, pltpu.roll(before, by, 1), pltpu.roll(here, by, 1))
+
+
+def sooner(here, after, by):
+    lane = lax.broadcasted_iota(jnp.int32, here.shape, 1)
+    back = LANES - by
+    return jnp.where(lane >= back, pltpu.roll(after, back, 1), pltpu.roll(here, back, 1))
+
+
+def block_kernel(g, *refs):
+    refs = list(refs)
+    r = Inputs(*(refs.pop(0) for _ in Inputs._fields))
+    block_out, tokens_grad, ct_out, ps_out, in_recv, up_recv, down_recv, out_recv = (refs.pop(0) for _ in range(8))
+    w = types.SimpleNamespace(**{name: refs.pop(0) for name in scratch_buffers(g)})
+    sems = types.SimpleNamespace(**{name: (refs.pop(0), refs.pop(0)) for name in SEMAPHORES})
+    local_sem = refs.pop(0)
+    net = Net(g)
+    tok, width, pt, ch, ff = g.tok, g.width, g.plane_tokens, g.chan, g.ff_part
+    rows, planes, members, chips, blocks = g.rows, g.planes, g.members, g.chips, g.blocks
+    part = g.down_rows
+    exact = lax.Precision.HIGHEST
+
+    barrier = pltpu.get_barrier_semaphore()
+
+    @pl.loop(1, g.devices)
+    def _(j):
+        there = net.device(lax.rem(net.flat + j, g.devices))
+        pl.semaphore_signal(barrier, inc=1, device_id=there, device_id_type=ON_MESH)
+
+    xhat_one, inverse_one = normalized(r.tokens[...].astype(f32))
+    w.xhat_one[...] = xhat_one
+    mine = step_at(net.m, tok)
+    w.act_one[mine, :] = (xhat_one * r.first_gain[...] + r.first_shift[...]).astype(bf16)
+    w.cotan[mine, :] = r.cotangent[...]
+    for m in range(members):
+        for b in range(3):
+            at = b * width + m * LANES
+            w.w_in_send[m * rows : (m + 1) * rows, b * LANES : (b + 1) * LANES] = r.input_weight[:, at : at + LANES]
+        for z in range(planes):
+            at = ((m // INNER) * g.n_seq + z * INNER + m % INNER) * part
+            w.w_up_send[m * rows : (m + 1) * rows, z * part : (z + 1) * part] = r.up_weight[:, at : at + part]
+    w.w_in[step_at(net.flat, rows), :] = w.w_in_send[step_at(net.m, rows), :]
+    w.w_up[step_at(net.flat, rows), :] = w.w_up_send[step_at(net.m, rows), :]
+    w.w_down[step_at(net.z, part), :] = r.down_weight[...]
+    w.w_out[step_at(net.flat, rows), :] = r.output_weight[...]
+
+    pl.semaphore_wait(barrier, g.devices - 1)
+
+    def member_of(target):
+        x, s = net.device(target)
+        return x * INNER + s % INNER
+
+    move_in = ToAll(
+        net, sems.w_in, lambda t: w.w_in_send.at[step_at(member_of(t), rows)], w.w_in.at[step_at(net.flat, rows)]
+    )
+    move_up = ToAll(
+        net, sems.w_up, lambda t: w.w_up_send.at[step_at(member_of(t), rows)], w.w_up.at[step_at(net.flat, rows)]
+    )
+    move_down = AlongPlanes(net, sems.w_down, lambda z: r.down_weight, w.w_down.at[step_at(net.z, part)])
+    gather_one = PlaneGather(net, sems.act_one, lambda m: w.act_one.at[step_at(m, tok)])
+    gather_cotan = PlaneGather(net, sems.cotan, lambda m: w.cotan.at[step_at(m, tok)])
+    out_z = AlongPlanes(
+        net, sems.w_out_z, lambda z: w.w_out.at[step_at(net.flat, rows)], w.w_out.at[step_at(net.flat, rows)]
+    )
+
+    def out_rows(z):
+        return lambda m: w.w_out.at[step_at((m // INNER) * g.n_seq + z * INNER + m % INNER, rows)]
+
+    gather_out = [PlaneGather(net, sems.w_out, out_rows(z), 8 * z) for z in range(planes)]
+
+    gather_one.start()
+    move_in.start()
+
+    w.square[...] = jnp.zeros_like(w.square)
+    lane_of = step_at(net.m, LANES)
+
+    def param(row, ref, k, at):
+        w.square[row : row + 1, :] = ref[k : k + 1, pl.ds(pl.multiple_of(at + net.m * LANES, LANES), LANES)]
+
+    for b in range(3):
+        param(b, r.input_bias, 0, b * width)
+        for i in range(3):
+            param(3 + 3 * i + b, r.short_weight, i, b * width)
+        param(12 + b, r.short_bias, 0, b * width)
+    param(15, r.skip_gain, 0, 0)
+    param(16, r.decay_rates, 0, 0)
+    w.param_cols[...] = w.square[...].T
+    here = step_at(net.z, ch)
+
+    def spread(col):
+        return jnp.broadcast_to(w.param_cols[here, col : col + 1], (ch, LANES))
+
+    for b in range(3):
+        for i in range(3):
+            w.taps[i, b * ch : (b + 1) * ch, :] = spread(3 + 3 * i + b)
+        w.taps[3, b * ch : (b + 1) * ch, :] = spread(12 + b)
+    w.skip[...] = spread(15)
+    w.decay[...] = spread(16)
+
+    w.square[...] = jnp.zeros_like(w.square)
+    for k, ref in enumerate((r.feat_bias, r.feat_freq, r.inner_bias, r.inner_freq)):
+        w.square[k : k + 1, :FILT] = ref[...]
+    w.net_cols[...] = w.square[...].T
+    w.square[...] = jnp.zeros_like(w.square)
+    w.square[:FEAT, :FILT] = r.feat_weight[...]
+    w.net_weights[0] = w.square[...].T
+    w.square[...] = jnp.zeros_like(w.square)
+    w.square[:FILT, :FILT] = r.inner_weight[...]
+    w.net_weights[1] = w.square[...].T
+    w.square[...] = jnp.zeros_like(w.square)
+    w.square[:FILT, :] = r.filter_weight[:, lane_of]
+    w.net_weights[3] = w.square[...].T
+    w.square[...] = jnp.zeros_like(w.square)
+    w.square[:ch, :] = w.net_weights[3, here, :]
+    w.net_weights[2] = w.square[...]
+    w.net_weights[3] = w.square[...].T
+    w.hid_two[...] = jnp.zeros_like(w.hid_two)
+
+    span = 4 * LANES
+    col = lambda k: w.net_cols[:FILT, k : k + 1]
+    features_rows = r.features.shape[0]
+
+    @pl.loop(0, g.length // span)
+    def _(step):
+        at = step_at(step, span)
+        feats = r.features[:, at]
+        p_one = dot_nn(w.net_weights[0, :FILT, :features_rows], feats, exact) + col(0)
+        hid_one, cos_one = sin_cos(col(1) * p_one)
+        p_two = dot_nn(w.net_weights[1, :FILT, :FILT], hid_one, exact) + col(2)
+        hid_two, cos_two = sin_cos(col(3) * p_two)
+        w.p_one[:, at], w.hid_one[:, at], w.cos_one[:, at] = p_one, hid_one, cos_one
+        w.p_two[:, at], w.hid_two[:FILT, at], w.cos_two[:, at] = p_two, hid_two, cos_two
+        filters = dot_nn(w.net_weights[2, :ch, :FILT], hid_two, exact)
+        for k in range(span // LANES):
+            cut = slice(k * LANES, (k + 1) * LANES)
+            w.filt[step * (span // LANES) + k] = filters[:, cut] * jnp.exp(-w.decay[...] * feats[:1, cut])
+
+    to_spectrum(g, w.filt, ch, w.stage_filt, r.turns, r.forth_high, r.forth_low, w.spec_filt)
+
+    gather_one.forward_all()
+    move_in.wait()
+    for b in range(3):
+        turned = w.w_in[:, b * LANES : (b + 1) * LANES].astype(f32).T.astype(bf16)
+        for z in range(planes):
+            at = z * 3 * ch + b * ch
+            w.w_in_t[at : at + ch, :] = turned[z * ch : (z + 1) * ch, :]
+    gather_one.wait_all()
+    biases = jnp.concatenate(
+        [w.param_cols[z * ch : (z + 1) * ch, b : b + 1] for z in range(planes) for b in range(3)], 0
+    )
+
+    @pl.loop(0, members // 2)
+    def _(step):
+        at = step_at(step, 2 * tok)
+        w.proj_send[:, at] = (dot_nt(w.w_in_t[...], w.act_one[at, :]) + biases).astype(bf16)
+
+    move_proj = AlongPlanes(
+        net, sems.proj, lambda z: w.proj_send.at[step_at(z, 3 * ch)], w.proj_recv.at[step_at(net.z, 3 * ch)]
+    )
+    move_proj.start()
+    w.proj_recv[step_at(net.z, 3 * ch), :] = w.proj_send[step_at(net.z, 3 * ch), :]
+    gather_cotan.start()
+    out_z.start()
+    gather_cotan.forward_all()
+    out_z.wait()
+    for k in gather_out:
+        k.start()
+    move_proj.wait()
+    move_up.start()
+
+    def place(d):
+        a, n = d // blocks, d % blocks
+        return a, n, step_at(n // INNER, 3 * ch), step_at(a * INNER + n % INNER, LANES)
+
+    for a in range(2):
+        w.padded[a, 0] = jnp.zeros((3 * ch, LANES), f32)
+        w.grad_conv[a, blocks] = jnp.zeros((3 * ch, LANES), f32)
+
+    @pl.loop(0, 2 * blocks)
+    def _(d):
+        a, n, from_rows, from_lanes = place(d)
+        w.padded[a, n + 1] = w.proj_recv[from_rows, from_lanes].astype(f32)
+
+    @pl.loop(0, 2 * blocks)
+    def _(d):
+        a, n, _, _ = place(d)
+        now, before = w.padded[a, n + 1], w.padded[a, n]
+        conv = w.taps[3] + w.taps[2] * now + w.taps[1] * later(now, before, 1) + w.taps[0] * later(now, before, 2)
+        w.conv[d] = conv
+        w.carried[n, step_at(a, ch), :] = conv[:ch] * conv[2 * ch :]
+
+    def both(filt):
+        return jnp.concatenate([filt, filt], 1)
+
+    to_spectrum(g, w.carried, 2 * ch, w.stage, r.turns, r.forth_high, r.forth_low, w.spec_car)
+
+    def forth_product(at):
+        (hr, hi), (xr, xi) = halves(both(w.spec_filt[at])), halves(w.spec_car[at])
+        return xr * hr - xi * hi, xr * hi + xi * hr
+
+    from_spectrum(g, forth_product, 2 * ch, w.stage, r.turns, r.back_high, r.back_low, w.back_sig)
+
+    @pl.loop(0, 2 * blocks)
+    def _(d):
+        a, n, _, _ = place(d)
+        at = step_at(a, ch)
+        long_out = w.back_sig[n, at, :] + w.skip[...] * w.carried[n, at, :]
+        w.long[n, at, :] = long_out
+        w.pre_send[step_at(d, ch), :] = (w.conv[d, ch : 2 * ch, :] * long_out).astype(bf16)
+
+    own_block, own_slot = step_at(net.chan_block, ch), step_at(net.flat, ch)
+
+    def chan_block_of(target):
+        x, s = net.device(target)
+        return (x * INNER + s % INNER) * planes + s // INNER
+
+    move_pre = ToAll(net, sems.pre, lambda t: w.pre_send.at[step_at(t, ch)], w.pre_recv.at[own_block])
+    move_pre.start()
+    w.pre_recv[own_block, :] = w.pre_send[own_slot, :]
+    for k in gather_out:
+        k.forward_all()
+    for k in gather_out:
+        k.wait_all()
+    move_pre.wait()
+    move_down.start()
+
+    pre_rows = w.pre_recv[...].astype(f32).T.astype(bf16)
+    branch = dot_nn(pre_rows, w.w_out[...])
+    residual = r.tokens[...].astype(f32) + branch + r.output_bias[...]
+    w.residual[...] = residual
+    xhat_two, inverse_two = normalized(residual)
+    w.xhat_two[...] = xhat_two
+    w.act_two[mine, :] = (xhat_two * r.second_gain[...] + r.second_shift[...]).astype(bf16)
+    gather_two = PlaneGather(net, sems.act_two, lambda m: w.act_two.at[step_at(m, tok)])
+    gather_two.start()
+
+    gather_cotan.wait_all()
+    move_up.wait()
+    sum_two = PlaneSum(net, sems.gn_two, w.gn_two_sib, w.gn_two_recv, w.gn_two_own, w.gn_two_send)
+    w.ps[...] = jnp.zeros_like(w.ps)
+    hidden_block = [net.x * g.n_seq + z * INNER + net.q for z in range(planes)]
+    up_bias = jnp.concatenate([r.up_bias[:, step_at(k, part)] for k in hidden_block], 1)
+    bias_sum = jnp.zeros((1, ff), f32)
+    for j in range(chips):
+        if j == 1:
+            gather_two.forward_all()
+        gather_two.wait(j)
+        chip = lax.rem(net.p + chips - j, chips)
+        at = step_at(chip, 2 * tok)
+        upper = dot_nn(w.act_two[at, :], w.w_up[...]) + up_bias
+        gelu, slope = gelu_pair(upper)
+        w.act_three[at, :] = gelu.astype(bf16)
+        if j == 0:
+            move_down.wait()
+        grad_upper = (dot_nt(w.cotan[at, :], w.w_down[...]) * slope).astype(bf16)
+        w.grad_up[at, :] = grad_upper
+        bias_sum = bias_sum + column_sum(grad_upper.astype(f32))
+        sum_two.own[at, :] = dot_nt(grad_upper, w.w_up[...]).astype(bf16)
+        sum_two.start(chip)
+    for z, k in enumerate(hidden_block):
+        w.ps[pl.ds(AT_UP_BIAS + k, 1), :] = bias_sum[:, z * part : (z + 1) * part]
+    for j in range(1, chips):
+        sum_two.relay(j)
+
+    def to_local(src, dst):
+        copy = pltpu.make_async_copy(src, dst, local_sem)
+        copy.start()
+        copy.wait()
+
+    own_rows = step_at(net.flat, rows)
+    move_up_grad = ToAll(net, sems.up_grad, lambda t: w.up_send.at[step_at(t, rows)], up_recv.at[own_rows])
+    @pl.loop(0, width // LANES)
+    def _(step):
+        at = step_at(step, LANES)
+        turned = w.act_two[:, at].astype(f32).T.astype(bf16)
+        w.up_send[at, :] = dot_nn(turned, w.grad_up[...]).astype(bf16)
+
+    move_up_grad.start()
+    to_local(w.up_send.at[own_rows], up_recv.at[own_rows])
+    sum_result = PlaneSum(net, sems.result, w.result_sib, w.result_recv, w.result_own, w.result_send)
+    for j in range(1, chips + 1):
+        chip = lax.rem(net.p + j, chips)
+        at = step_at(chip, 2 * tok)
+        sum_result.own[at, :] = dot_nn(w.act_three[at, :], w.w_down[...]).astype(bf16)
+    grad_two = sum_two.result()
+
+    xhat_two = w.xhat_two[...]
+    to_rows(w.ps, AT_SECOND_GAIN, column_sum(grad_two * xhat_two))
+    to_rows(w.ps, AT_SECOND_SHIFT, column_sum(grad_two))
+    cotan = r.cotangent[...].astype(f32)
+    to_rows(w.ps, AT_DOWN_BIAS, column_sum(cotan))
+    grad_res = cotan + norm_back(grad_two, xhat_two, inverse_two, r.second_gain[...])
+    w.grad_res[...] = grad_res
+    grad_branch = grad_res.astype(bf16)
+    w.grad_branch[...] = grad_branch
+    to_rows(w.ps, AT_OUTPUT_BIAS, column_sum(grad_branch.astype(f32)))
+
+    @pl.loop(0, width // 256)
+    def _(step):
+        at = step_at(step, 256)
+        w.gpre_send[at, :] = dot_nt(w.w_out[at, :], w.grad_branch[...]).astype(bf16)
+
+    move_gpre = ToAll(net, sems.gpre, lambda t: w.gpre_send.at[step_at(chan_block_of(t), ch)], w.gpre_recv.at[own_slot])
+    move_gpre.start()
+    w.gpre_recv[own_slot, :] = w.gpre_send[own_block, :]
+
+    for j in range(1, chips + 1):
+        sum_result.start(lax.rem(net.p + j, chips))
+
+    @pl.loop(0, ff // LANES)
+    def _(step):
+        at = step_at(step, LANES)
+        turned = w.act_three[:, at].astype(f32).T.astype(bf16)
+        w.down_send[at, :] = dot_nn(turned, w.cotan[...]).astype(bf16)
+
+    move_gpre.wait()
+    move_down_grad = AlongPlanes(
+        net, sems.down_grad, lambda z: w.down_send.at[step_at(z, part)], down_recv.at[step_at(net.z, part)]
+    )
+    move_down_grad.start()
+    to_local(w.down_send.at[step_at(net.z, part)], down_recv.at[step_at(net.z, part)])
+
+    w.sums[...] = jnp.zeros_like(w.sums)
+
+    @pl.loop(0, 2 * blocks)
+    def _(d):
+        a, n, _, _ = place(d)
+        at = step_at(a, ch)
+        grad_pre = w.gpre_recv[step_at(d, ch), :].astype(f32)
+        grad_long = grad_pre * w.conv[d, ch : 2 * ch, :]
+        w.grad_long[n, at, :] = grad_long
+        w.grad_conv[a, n, ch : 2 * ch, :] = grad_pre * w.long[n, at, :]
+        w.sums[5, :ch, :] += grad_long * w.carried[n, at, :]
+
+    to_spectrum(g, w.grad_long, 2 * ch, w.stage, r.turns, r.forth_high, r.forth_low, w.spec_grad)
+
+    def back_product(at):
+        (hr, hi), (gr, gi) = halves(both(w.spec_filt[at])), halves(w.spec_grad[at])
+        return hr * gr + hi * gi, hr * gi - hi * gr
+
+    from_spectrum(g, back_product, 2 * ch, w.stage, r.turns, r.back_high, r.back_low, w.back_sig)
+
+    @pl.loop(0, 2 * blocks)
+    def _(d):
+        a, n, _, _ = place(d)
+        at = step_at(a, ch)
+        grad_car = w.back_sig[n, at, :] + w.skip[...] * w.grad_long[n, at, :]
+        w.grad_conv[a, n, :ch, :] = grad_car * w.conv[d, 2 * ch :, :]
+        w.grad_conv[a, n, 2 * ch :, :] = grad_car * w.conv[d, :ch, :]
+
+    @pl.loop(0, 2 * blocks)
+    def _(d):
+        a, n, to_row, to_lane = place(d)
+        now, after = w.grad_conv[a, n], w.grad_conv[a, n + 1]
+        grad = w.taps[2] * now + w.taps[1] * sooner(now, after, 1) + w.taps[0] * sooner(now, after, 2)
+        grad = grad.astype(bf16)
+        w.gproj_send[to_row, to_lane] = grad
+        w.sums[4] += grad.astype(f32)
+
+    move_gproj = AlongPlanes(
+        net, sems.gproj, lambda z: w.gproj_send.at[step_at(z, 3 * ch)], w.gproj_recv.at[step_at(net.z, 3 * ch)]
+    )
+    move_gproj.start()
+    w.gproj_recv[step_at(net.z, 3 * ch), :] = w.gproj_send[step_at(net.z, 3 * ch), :]
+
+    for j in range(1, chips):
+        sum_result.relay(j)
+
+    sum_out = PlaneSum(net, sems.w_out_grad, w.w_out_grad_sib, w.w_out_grad_recv, after=sum_two)
+    for j in range(1, chips + 1):
+        chip = lax.rem(net.p + j, chips)
+        at = step_at(chip, 2 * tok)
+        sum_out.own[at, :] = dot_nn(w.pre_recv[at, :], w.grad_branch[...]).astype(bf16)
+        sum_out.start(chip)
+
+    @pl.loop(0, 2 * blocks)
+    def _(d):
+        a, n, _, _ = place(d)
+        grad, now, before = w.grad_conv[a, n], w.padded[a, n + 1], w.padded[a, n]
+        w.sums[3] += grad
+        w.sums[2] += grad * now
+        w.sums[1] += grad * later(now, before, 1)
+        w.sums[0] += grad * later(now, before, 2)
+
+    for j in range(1, chips):
+        sum_out.relay(j)
+
+    def filt_product(at):
+        out = []
+        for a in range(2):
+            cut = slice(a * ch, (a + 1) * ch)
+            (xr, xi), (gr, gi) = halves(w.spec_car[at, cut, :]), halves(w.spec_grad[at, cut, :])
+            out.append((xr * gr + xi * gi, xr * gi - xi * gr))
+        return out[0][0] + out[1][0], out[0][1] + out[1][1]
+
+    from_spectrum(g, filt_product, ch, w.stage_filt, r.turns, r.back_high, r.back_low, w.back_filt)
+
+    ones = jnp.ones((8, span), f32)
+    chan_rows = step_at(net.chan_block, ch)
+    w.ct[chan_rows, :] = jnp.zeros((ch, LANES), f32)
+
+    @pl.loop(0, g.length // span)
+    def _(step):
+        at = step_at(step, span)
+        feats = r.features[:, at]
+        gate = []
+        for k in range(span // LANES):
+            fade = jnp.exp(-w.decay[...] * feats[:1, k * LANES : (k + 1) * LANES])
+            gate.append(w.back_filt[step * (span // LANES) + k] * fade)
+        gate = jnp.concatenate(gate, 1)
+        w.ct[chan_rows, :] += dot_nt(gate, w.hid_two[:, at], exact)
+        q_two = dot_nn(w.net_weights[3, :FILT, :ch], gate, exact)
+        slope_two = q_two * w.cos_two[:, at]
+        r_two = slope_two * col(3)
+        w.ps[:FILT, :FILT] += dot_nt(w.hid_one[:, at], r_two, exact)
+        q_one = dot_nn(r.inner_weight[...], r_two, exact)
+        slope_one = q_one * w.cos_one[:, at]
+        r_one = slope_one * col(1)
+        w.ps[AT_FEAT : AT_FEAT + features_rows, :FILT] += dot_nt(feats, r_one, exact)
+        for k, x in enumerate((r_one, slope_one * w.p_one[:, at], r_two, slope_two * w.p_two[:, at])):
+            w.ps[AT_VECTOR + 8 * k : AT_VECTOR + 8 * k + 8, :FILT] += dot_nt(ones, x, exact)
+
+    lane = lax.broadcasted_iota(jnp.int32, (ch, LANES), 1)
+    tile = w.ct[chan_rows, :]
+
+    def put(tile, k, x):
+        return jnp.where(lane == CT_FILTER + k, jnp.sum(x, 1, keepdims=True), tile)
+
+    for b in range(3):
+        cut = slice(b * ch, (b + 1) * ch)
+        tile = put(tile, b, w.sums[4, cut, :])
+        for i in range(3):
+            tile = put(tile, 3 + 3 * i + b, w.sums[i, cut, :])
+        tile = put(tile, 12 + b, w.sums[3, cut, :])
+    tile = put(tile, 15, w.sums[5, :ch, :])
+    w.ct[chan_rows, :] = tile
+    ct_z = AlongPlanes(net, sems.ct_z, lambda z: w.ct.at[chan_rows], w.ct.at[chan_rows])
+    ct_z.start()
+
+    w.out_sum[...] = sum_out.result().astype(bf16)
+    own_part = LANES // rows
+
+    def out_grad_copy(k):
+        return net.copy(
+            w.out_sum.at[k * rows : (k + 1) * rows],
+            out_recv.at[step_at(net.z, rows)],
+            sems.out_grad,
+            net.z,
+            net.device(net.m * own_part + k),
+            k,
+        )
+
+    def out_grad_send(k, act):
+        @pl.when(net.m * own_part + k != net.flat)
+        def _():
+            act(out_grad_copy(k))
+
+    for k in range(own_part):
+        out_grad_send(k, lambda copy: copy.start())
+
+        @pl.when(net.m * own_part + k == net.flat)
+        def _():
+            to_local(w.out_sum.at[k * rows : (k + 1) * rows], out_recv.at[step_at(net.z, rows)])
+
+    def out_grad_end():
+        for k in range(own_part):
+            out_grad_send(k, lambda copy: copy.wait_send())
+        for z in range(planes):
+
+            @pl.when((net.flat // own_part != net.m) | (net.z != z))
+            def _():
+                here = out_recv.at[z * rows : (z + 1) * rows]
+                net.copy(here, here, sems.out_grad, z, net.member(net.sib)).wait_recv()
+
+    block_out[...] = (w.residual[...] + sum_result.result() + r.down_bias[...]).astype(bf16)
+    move_gproj.wait()
+    sum_one = PlaneSum(net, sems.gn_one, w.gn_one_sib, w.gn_one_recv, after=sum_result)
+    shift_sum = gain_sum = jnp.zeros((1, width), f32)
+    for j in range(1, chips + 1):
+        chip = lax.rem(net.p + j, chips)
+        at = step_at(chip, 2 * tok)
+        turned = w.gproj_recv[:, at].astype(f32).T.astype(bf16)
+        partial = dot_nn(turned, w.w_in_t[...])
+        sum_one.own[at, :] = partial.astype(bf16)
+        sum_one.start(chip)
+        shift_sum = shift_sum + column_sum(partial)
+        gain_sum = gain_sum + column_sum(partial * w.act_one[at, :].astype(f32))
+    to_rows(w.ps, AT_FIRST_GAIN, (gain_sum - r.first_shift[...] * shift_sum) / r.first_gain[...])
+    to_rows(w.ps, AT_FIRST_SHIFT, shift_sum)
+    share = PS_ROWS // g.devices
+    own_share = step_at(net.flat, share)
+    move_ps = ToAll(net, sems.ps, lambda t: w.ps.at[step_at(t, share)], w.ps_recv.at[own_share])
+    move_ps.start()
+    w.ps_recv[own_share, :] = w.ps[own_share, :]
+
+    @pl.loop(0, width // LANES)
+    def _(step):
+        at = step_at(step, LANES)
+        grad = dot_nn(w.gproj_recv[...], w.act_one[:, at])
+        for b in range(3):
+            piece = [grad[z * 3 * ch + b * ch : z * 3 * ch + (b + 1) * ch] for z in range(planes)]
+            w.in_send[at, b * LANES : (b + 1) * LANES] = jnp.concatenate(piece, 0).T.astype(bf16)
+
+    move_in_grad = ToAll(net, sems.in_grad, lambda t: w.in_send.at[step_at(t, rows)], in_recv.at[own_rows])
+    move_in_grad.start()
+    to_local(w.in_send.at[own_rows], in_recv.at[own_rows])
+    for j in range(1, chips):
+        sum_one.relay(j)
+    ct_z.wait()
+    gather_ct = PlaneGather(net, sems.ct, lambda m: w.ct.at[step_at(m, LANES)])
+    gather_ct.start()
+    move_ps.wait()
+    total = w.ps_recv[:share, :]
+    for k in range(1, g.devices):
+        total = total + w.ps_recv[k * share : (k + 1) * share, :]
+    w.ps_all[own_share, :] = total
+    move_back = ToAll(net, sems.ps_back, lambda t: w.ps_all.at[own_share], w.ps_all.at[own_share])
+    move_back.start()
+    gather_ct.forward_all()
+    grad_one = sum_one.result()
+
+    grad_tokens = norm_back(grad_one, w.xhat_one[...], inverse_one, r.first_gain[...])
+    tokens_grad[...] = (w.grad_res[...] + grad_tokens).astype(bf16)
+    gather_ct.wait_all()
+    ct_out[...] = w.ct[...]
+    move_back.wait()
+    ps_out[...] = w.ps_all[...]
+    move_in_grad.wait()
+    move_up_grad.wait()
+    move_down_grad.wait()
+    out_grad_end()
+    net.finish()
+
+
+def finish_kernel(g, *refs):
+    ins, outs = refs[:8], refs[8:]
+    block_in, tokens_in, ct, ps, in_recv, up_recv, down_recv, out_recv = ins
+    (
+        block_out, tokens_grad, first_gain, first_shift, input_weight, input_bias, short_weight, short_bias, feat_weight,
+        feat_bias, feat_freq, inner_weight, inner_bias, inner_freq, filter_weight, skip_gain, output_weight, output_bias,
+        second_gain, second_shift, up_weight, up_bias, down_weight, down_bias,
+    ) = outs
+    rows, planes, width, ff = g.rows, g.planes, g.width, g.ff_part
+    block_out[...] = block_in[...]
+    tokens_grad[...] = tokens_in[...]
+    for m in range(g.members):
+        x, q = m // INNER, m % INNER
+        parts = [x * g.n_seq + z * INNER + q for z in range(planes)]
+        total = sum(in_recv[k * rows : (k + 1) * rows, :].astype(f32) for k in parts)
+        for b in range(3):
+            input_weight[:, b * width + m * LANES : b * width + (m + 1) * LANES] = total[:, b * LANES : (b + 1) * LANES]
+        total = sum(up_recv[k * rows : (k + 1) * rows, :].astype(f32) for k in parts)
+        for z, k in enumerate(parts):
+            cut = slice(z * g.down_rows, (z + 1) * g.down_rows)
+            up_weight[:, k * g.down_rows : (k + 1) * g.down_rows] = total[:, cut]
+    down_weight[...] = sum(down_recv[z * g.down_rows : (z + 1) * g.down_rows, :].astype(f32) for z in range(planes))
+    output_weight[...] = sum(out_recv[z * rows : (z + 1) * rows, :].astype(f32) for z in range(planes))
+    for m in range(g.members):
+        cut = slice(m * LANES, (m + 1) * LANES)
+        turned = ct[cut, :].T
+        filter_weight[:, cut] = turned[:FILT, :]
+        line = lambda k: turned[CT_FILTER + k : CT_FILTER + k + 1, :]
+        for b in range(3):
+            at = b * g.members + m
+            input_bias[at : at + 1, :] = line(b)
+            for i in range(3):
+                short_weight[i : i + 1, b * width + m * LANES : b * width + (m + 1) * LANES] = line(3 + 3 * i + b)
+            short_bias[at : at + 1, :] = line(12 + b)
+        skip_gain[m : m + 1, :] = line(15)
+    for out, at in (
+        (first_gain, AT_FIRST_GAIN), (first_shift, AT_FIRST_SHIFT), (second_gain, AT_SECOND_GAIN), (up_bias, AT_UP_BIAS),
+        (second_shift, AT_SECOND_SHIFT), (output_bias, AT_OUTPUT_BIAS), (down_bias, AT_DOWN_BIAS),
+    ):
+        out[...] = ps[at : at + out.shape[0], :]
+    feat_weight[...] = ps[AT_FEAT : AT_FEAT + FEAT, :FILT]
+    inner_weight[...] = ps[:FILT, :FILT]
+    for k, out in enumerate((feat_bias, feat_freq, inner_bias, inner_freq)):
+        out[...] = ps[AT_VECTOR + 8 * k : AT_VECTOR + 8 * k + 1, :FILT]
+
+
+def on_device_in_kernels(g, *args):
+    operands = [a[0] if a.ndim == 3 else a[None] if a.ndim == 1 else a for a in args]
+    operands += [jnp.asarray(table) for table in constant_tables(g.blocks, LANES)]
+    tok, width = g.tok, g.width
+    in_vmem = pl.BlockSpec(memory_space=pltpu.VMEM)
+    anywhere = pl.BlockSpec(memory_space=pl.ANY)
+    S = jax.ShapeDtypeStruct
+    parts = pl.pallas_call(
+        functools.partial(block_kernel, g),
+        out_shape=[
+            S((tok, width), bf16),
+            S((tok, width), bf16),
+            S((width, LANES), f32),
+            S((PS_ROWS, LANES), f32),
+            S((g.devices * g.rows, 3 * LANES), bf16),
+            S((g.devices * g.rows, g.ff_part), bf16),
+            S((g.planes * g.down_rows, width), bf16),
+            S((g.planes * g.rows, width), bf16),
+        ],
+        in_specs=[in_vmem] * len(operands),
+        out_specs=[in_vmem] * 4 + [anywhere] * 4,
+        scratch_shapes=[pltpu.VMEM(shape, dtype) for shape, dtype in scratch_buffers(g).values()]
+        + [pltpu.SemaphoreType.DMA((count,)) for count in SEMAPHORES.values() for _ in range(2)]
+        + [pltpu.SemaphoreType.DMA],
+        compiler_params=pltpu.CompilerParams(
+            collective_id=0, has_side_effects=True, vmem_limit_bytes=63 * 1024 * 1024
+        ),
+        name="block",
+    )(*operands)
+
+    def out_shape(a):
+        if a.ndim == 3:
+            return S(a.shape[1:], bf16)
+        if a.ndim == 1:
+            return S((a.shape[0] // LANES, LANES) if a.shape[0] % LANES == 0 else (1, a.shape[0]), f32)
+        return S(a.shape, f32)
+
+    named = Inputs(*args, *operands[len(args) :])
+    wanted = [a for a in args if a is not named.cotangent and a is not named.decay_rates]
+    wanted = [named.tokens] + wanted
+    outs = pl.pallas_call(
+        functools.partial(finish_kernel, g),
+        out_shape=[out_shape(a) for a in wanted],
+        in_specs=[in_vmem] * 8,
+        out_specs=[in_vmem] * len(wanted),
+        compiler_params=pltpu.CompilerParams(vmem_limit_bytes=63 * 1024 * 1024),
+        name="finish",
+    )(*parts)
+    return tuple(o.reshape(a.shape) for o, a in zip(outs, wanted))
+
+
+def on_device_by_size(tokens, cotangent, *args):
+    named = Inputs(tokens, cotangent, *args, *[None] * 6)
+    g = Geometry(
+        lax.axis_size("dp"),
+        lax.axis_size("seq"),
+        tokens.shape[1],
+        tokens.shape[2],
+        named.up_weight.shape[1],
+        named.input_weight.shape[0],
+        named.down_weight.shape[0],
+    )
+    if g.fits():
+        return on_device_in_kernels(g, tokens, cotangent, *args)
+    return on_device(tokens, cotangent, *args)
+
+
 def solution(mesh):
     placed = (
         P("dp", "seq", None),
@@ -433,7 +1631,7 @@
         P(),
     )
     return jax.shard_map(
-        on_device,
+        on_device_by_size,
         mesh=mesh,
         in_specs=placed,
         out_specs=(

time: 1490 us -> 247 us (0.17)
  waiting for transfers between devices: 1170 us -> 0 us
  Pallas kernels: 0 us -> 242 us
  matrix products: 123 us -> 0 us
  local copies, waits for them, and re-layouts: 66.8 us -> 0 us
  other arithmetic: 48.8 us -> 0 us
  starting transfers between devices: 27.6 us -> 0 us
  blocking collectives: 27.5 us -> 0 us
    reduce_scatter x4 -> x0, waiting for transfers between devices: 675 us -> none  [the longest x1 188 us: on_device(): lax.psum_scatter(up_grad, ('dp', 'seq'), scatter_dimension=0, tiled=True)]
    psum x2 -> x0, waiting for transfers between devices: 295 us -> none  [on_device(): lax.psum((first_gain_grad, first_shift_grad, input_bias_grad, short_weigh...]
    pallas_call x0 -> x2, Pallas kernels: none -> 242 us  [the longest x1 238 us: on_device_in_kernels(): pl.pallas_call(functools.partial(block_kernel, g), out_shape=[S((tok, wid...]
    all_gather x4 -> x0, waiting for transfers between devices: 181 us -> none  [the longest x1 72.9 us: on_device(): lax.all_gather(down_weight, ('dp', 'seq'), axis=0, tiled=True)]
    dot_general x56 -> x0, matrix products: 123 us -> none  [the longest x1 9.46 us: on_device(): lax.dot_general(act_two, grad_upper, (((0,), (0,)), ((), ())), preferred_...]
    unnamed x176 -> x0, local copies, waits for them, and re-layouts: 44.1 us -> none
    unnamed x7 -> x0, other arithmetic: 37.7 us -> none
    all_to_all x2 -> x0, blocking collectives: 27.5 us -> none  [the longest x1 14.1 us: on_device(): lax.all_to_all(grad_long_blocks.astype(jnp.bfloat16), 'seq', split_axis=0...]
  transfers between devices with their start and end apart: 16 -> 0, of which waited for: 11 -> 0; matrix products, arithmetic and copies ran while one was open for 9% -> 0% of each run, Pallas kernels for 0% -> 0%
where the time goes in v1:
time: 247 us; the launch traced here: 243 us
  Pallas kernels  242 us (98%)
    pallas_call x1, Pallas kernels, on_device_in_kernels(): pl.pallas_call(functools.partial(block_kernel, g), out_shape=[S((tok, wid...  238 us

profile of v1, /device:TPU:0, one launch (start us, length us, event | category | flops | bytes accessed | tf_op | source)
XLA Modules:
  0.0 242.7 jit_solution(18092030132664585952)
XLA Ops:
  0.7 238.0 %block.1 = (bf16[128,1024]{1,0:T(8,128)(2,1)}, bf16[128,1024]{1,0:T(8,128)(2,1)}, f32[1024,128]{1,0:T(8,128)}, f32[256,128]{1,0:T(8,128)}, bf16[1024,384]{1,0:T(...) custom-call(bf16[128,1024]{1,0:T(8,128)(2,1)} %bitcast.33, ...), custom_call_target="tpu_custom_call" | custom-call | tf_op jit(solution)/shard_map/block/pallas_call | solution.py:1545
  238.7 3.9 %finish.1 = (bf16[128,1024]{1,0:T(8,128)(2,1)}, bf16[128,1024]{1,0:T(8,128)(2,1)}, f32[8,128]{1,0:T(8,128)}, f32[8,128]{1,0:T(8,128)}, f32[32,3072]{1,0:T(8,128)...) custom-call(bf16[128,1024]{1,0:T(8,128)(2,1)} %get-tuple-element.56., ...), custom_call_target="tpu_custom_call" | custom-call | tf_op jit(solution)/shard_map/finish/pallas_call | solution.py:1578

commit v2 on v1

--- a/solution.py
+++ b/solution.py
@@ -416,17 +416,17 @@
 ON_MESH = pl.DeviceIdType.MESH
 INNER = 4
 LANES = 128
-CT_FILTER = 64
-PS_ROWS = 256
+PS_ROWS = 320
 AT_VECTOR = 64
-AT_SECOND_GAIN = 96
-AT_SECOND_SHIFT = 104
-AT_OUTPUT_BIAS = 112
-AT_DOWN_BIAS = 120
-AT_FIRST_GAIN = 128
-AT_FIRST_SHIFT = 136
-AT_UP_BIAS = 144
-AT_FEAT = 176
+AT_SECOND_GAIN = 72
+AT_SECOND_SHIFT = 80
+AT_OUTPUT_BIAS = 88
+AT_DOWN_BIAS = 96
+AT_FIRST_GAIN = 104
+AT_FIRST_SHIFT = 112
+AT_UP_BIAS = 120
+AT_FEAT = 152
+AT_CHANNEL = 192
 
 
 def dot_nn(a, b, precision=None):
@@ -563,12 +563,36 @@
         act_one=((pt, width), bf16),
         act_two=((pt, width), bf16),
         cotan=((pt, width), bf16),
-        proj_send=((3 * LANES, pt), bf16),
-        proj_recv=((3 * LANES, pt), bf16),
+        proj=((3 * LANES, pt), bf16),
+        conv=((3 * LANES, pt), f32),
+        grad_conv=((3 * LANES, pt), f32),
+        carried=((LANES, pt), f32),
+        long=((LANES, pt), f32),
+        grad_long=((LANES, pt), f32),
+        car_send=((LANES, pt), bf16),
+        car_recv=((LANES, pt), bf16),
+        y_send=((LANES, pt), bf16),
+        y_recv=((LANES, pt), bf16),
+        gl_send=((LANES, pt), bf16),
+        gl_recv=((LANES, pt), bf16),
+        gc_send=((LANES, pt), bf16),
+        gc_recv=((LANES, pt), bf16),
+        act_pre=((LANES, pt), bf16),
+        gpre=((LANES, pt), bf16),
+        gproj=((3 * LANES, pt), bf16),
+        signal=((blocks, 2 * ch, LANES), f32),
+        taps=((4, 3 * LANES, LANES), f32),
+        skip=((LANES, LANES), f32),
+        edge_send=((16, 3 * LANES), f32),
+        edge_recv=((16, 3 * LANES), f32),
+        back_edge_send=((16, 3 * LANES), f32),
+        back_edge_recv=((16, 3 * LANES), f32),
+        edge=((2, 3 * LANES, LANES), f32),
+        back_edge=((2, 3 * LANES, LANES), f32),
+        ps_recv=((PS_ROWS, LANES), f32),
+        ps_line=((PS_ROWS // g.members * g.planes, LANES), f32),
         square=((LANES, LANES), f32),
         param_cols=((LANES, LANES), f32),
-        taps=((4, 3 * ch, LANES), f32),
-        skip=((ch, LANES), f32),
         decay=((ch, LANES), f32),
         net_weights=((4, LANES, LANES), f32),
         net_cols=((LANES, LANES), f32),
@@ -579,12 +603,6 @@
         hid_two=((LANES, g.length), f32),
         cos_two=((FILT, g.length), f32),
         filt=((blocks, ch, LANES), f32),
-        padded=((2, blocks + 1, 3 * ch, LANES), f32),
-        conv=((2 * blocks, 3 * ch, LANES), f32),
-        carried=((blocks, 2 * ch, LANES), f32),
-        long=((blocks, 2 * ch, LANES), f32),
-        grad_long=((blocks, 2 * ch, LANES), f32),
-        grad_conv=((2, blocks + 1, 3 * ch, LANES), f32),
         stage=((blocks, 2 * ch, 2 * LANES), f32),
         stage_filt=((blocks, ch, 2 * LANES), f32),
         spec_filt=((blocks, ch, 2 * LANES), f32),
@@ -592,11 +610,9 @@
         spec_grad=((blocks, 2 * ch, 2 * LANES), f32),
         back_sig=((blocks, 2 * ch, LANES), f32),
         back_filt=((blocks, ch, LANES), f32),
-        sums=((6, 3 * ch, LANES), f32),
-        pre_send=((width, tok), bf16),
         pre_recv=((width, tok), bf16),
+        pre_line=((width, tok), bf16),
         gpre_send=((width, tok), bf16),
-        gpre_recv=((width, tok), bf16),
         residual=((tok, width), f32),
         xhat_two=((tok, width), f32),
         xhat_one=((tok, width), f32),
@@ -605,20 +621,26 @@
         act_three=((pt, ff), bf16),
         grad_up=((pt, ff), bf16),
         up_send=((width, ff), bf16),
+        up_parts=((width, ff), bf16),
+        up_pre=((width // g.planes, ff), bf16),
+        up_mid=((width // g.planes, ff), bf16),
+        down_parts=((ff, width), bf16),
+        down_pre=((g.down_rows, width), bf16),
+        down_total=((g.down_rows, width), f32),
         down_send=((ff, width), bf16),
+        in_mid=((width // g.planes, 3 * LANES), bf16),
         in_send=((width, 3 * LANES), bf16),
         out_sum=((LANES, width), bf16),
-        gproj_send=((3 * LANES, pt), bf16),
-        gproj_recv=((3 * LANES, pt), bf16),
+        out_parts=((LANES, width), bf16),
+        out_pre=((g.rows, width), bf16),
+        out_total=((g.rows, width), f32),
         ct=((width, LANES), f32),
         ps=((PS_ROWS, LANES), f32),
-        ps_recv=((PS_ROWS, LANES), f32),
         ps_all=((PS_ROWS, LANES), f32),
         gn_two_own=((pt, width), bf16),
         gn_two_send=((pt // 2, width), bf16),
         gn_two_sib=((pt // 2, width), bf16),
         gn_two_recv=((3 * tok, width), bf16),
-        result_own=((pt, width), bf16),
         result_send=((pt // 2, width), bf16),
         result_sib=((pt // 2, width), bf16),
         result_recv=((3 * tok, width), bf16),
@@ -629,32 +651,39 @@
     )
 
 
-SEMAPHORES = dict(
-    w_in=32,
-    w_up=32,
-    up_grad=32,
-    in_grad=32,
-    pre=32,
-    gpre=32,
-    ps=32,
-    ps_back=32,
-    w_down=8,
-    w_out_z=8,
-    proj=8,
-    gproj=8,
-    down_grad=8,
-    out_grad=8,
-    ct_z=8,
-    act_one=8,
-    act_two=8,
-    cotan=8,
-    w_out=32,
-    ct=8,
-    gn_two=8,
-    result=8,
-    w_out_grad=8,
-    gn_one=8,
-)
+def semaphore_counts(g):
+    plane, line, n, far = g.members - 1, g.planes - 1, g.planes, g.n_dp
+    gather, add = (n + 1, n), (n, n + 1)
+    both = lambda counts: (counts[0] * far, counts[1] * far)
+    chips = (2 * g.chips - 1,) * 2
+    return dict(
+        w_in=(plane,) * 2,
+        w_up=(plane,) * 2,
+        pre=(plane,) * 2,
+        ps=(plane,) * 2,
+        ps_back=(plane,) * 2,
+        car=(line,) * 2,
+        y=(line,) * 2,
+        ps_line=(line,) * 2,
+        ct_z=(line,) * 2,
+        edge=(1, 1),
+        back_edge=(1, 1),
+        act_one=chips,
+        act_two=chips,
+        cotan=chips,
+        w_out=chips,
+        gn_two=chips,
+        result=chips,
+        w_out_grad=chips,
+        w_in_line=both(gather),
+        w_up_line=both(gather),
+        w_down=gather,
+        w_out_line=gather,
+        up_grad=both(add),
+        in_grad=both(add),
+        down_grad=add,
+        out_grad=add,
+    )
 
 
 class Geometry:
@@ -717,34 +746,14 @@
             device_id_type=ON_MESH,
         )
 
+    def sent(self, *moves):
+        for move in moves:
+            move.wait_send()
+            self.ends.remove(move.wait_send)
+
     def finish(self):
         for end in self.ends:
             end()
-
-
-class ToAll:
-    def __init__(self, net, sems, src, dst):
-        self.net, self.sems, self.src, self.dst = net, sems, src, dst
-        net.ends.append(self.wait_send)
-
-    def one(self, j):
-        net = self.net
-        target = lax.rem(net.flat + j, net.g.devices)
-        return net.copy(self.src(target), self.dst, self.sems, j, net.device(target))
-
-    def each(self, act):
-        @pl.loop(1, self.net.g.devices)
-        def _(j):
-            act(self.one(j))
-
-    def start(self):
-        self.each(lambda copy: copy.start())
-
-    def wait(self):
-        self.each(lambda copy: copy.wait_recv())
-
-    def wait_send(self):
-        self.each(lambda copy: copy.wait_send())
 
 
 class AlongPlanes:
@@ -756,7 +765,7 @@
         net = self.net
         for j in range(1, net.g.planes):
             z = lax.rem(net.z + j, net.g.planes)
-            act(net.copy(self.src(z), self.dst, self.sems, j, net.in_plane(z)))
+            act(net.copy(self.src(z), self.dst, self.sems, j - 1, net.in_plane(z)))
 
     def start(self):
         self.each(lambda copy: copy.start())
@@ -768,9 +777,191 @@
         self.each(lambda copy: copy.wait_send())
 
 
+class ToMembers:
+    def __init__(self, net, sems, src, dst):
+        self.net, self.sems, self.src, self.dst = net, sems, src, dst
+        net.ends.append(self.wait_send)
+
+    def each(self, act):
+        net = self.net
+        for j in range(1, net.g.members):
+            m = lax.rem(net.m + j, net.g.members)
+            act(net.copy(self.src(m), self.dst, self.sems, j - 1, net.member(m)))
+
+    def start(self):
+        self.each(lambda copy: copy.start())
+
+    def wait(self):
+        self.each(lambda copy: copy.wait_recv())
+
+    def wait_send(self):
+        self.each(lambda copy: copy.wait_send())
+
+
+def relays(planes):
+    return [(2, 1, 0), (planes - 3, planes - 2, planes - 1)] if planes > 3 else []
+
+
+class LineGather:
+    def __init__(self, net, sems, pieces):
+        self.net, self.sems, self.pieces = net, sems, pieces
+        net.ends.append(self.wait_send)
+
+    def copies(self, source, target, handed):
+        n = len(self.pieces(0))
+        for k, piece in enumerate(self.pieces(source)):
+            sent = (self.net.g.planes if handed else target) * n + k
+            yield self.net.copy(piece, piece, self.sems, source * n + k, self.net.in_plane(target), sent)
+
+    def to_plane(self, target, act):
+        z = self.net.z
+        away = z != target
+        for source, _, end in relays(self.net.g.planes):
+            if end == target:
+                away = away & (z != source)
+
+        @pl.when(away)
+        def _():
+            for copy in self.copies(z, target, 0):
+                act(copy)
+
+    def start(self, far):
+        for target in range(self.net.g.planes):
+            near = (self.net.z == target - 1) | (self.net.z == target + 1)
+
+            @pl.when((near if not far else jnp.logical_not(near)))
+            def _():
+                self.to_plane(target, lambda copy: copy.start())
+
+    def hand_on(self):
+        for source, through, target in relays(self.net.g.planes):
+
+            @pl.when(self.net.z == through)
+            def _():
+                for copy in self.copies(source, target, 1):
+                    copy.wait_recv()
+                    copy.start()
+
+    def wait(self):
+        for source in range(self.net.g.planes):
+            due = self.net.z != source
+            for held, through, _ in relays(self.net.g.planes):
+                if held == source:
+                    due = due & (self.net.z != through)
+
+            @pl.when(due)
+            def _():
+                for copy in self.copies(source, 0, 0):
+                    copy.wait_recv()
+
+    def wait_send(self):
+        for target in range(self.net.g.planes):
+            self.to_plane(target, lambda copy: copy.wait_send())
+        for source, through, target in relays(self.net.g.planes):
+
+            @pl.when(self.net.z == through)
+            def _():
+                for copy in self.copies(source, target, 1):
+                    copy.wait_send()
+
+
+class LineSum:
+    def __init__(self, net, sems, own, slots, pre):
+        self.net, self.sems, self.own, self.slots, self.pre = net, sems, own, slots, pre
+        self.ends = [(t, through, 0 if t else net.g.planes - 1) for _, through, t in relays(net.g.planes)]
+        net.ends.append(self.wait_send)
+
+    def copies(self, target):
+        for k, (piece, slot) in enumerate(zip(self.own(target), self.slots(self.net.z))):
+            n = len(self.own(0))
+            yield self.net.copy(piece, slot, self.sems, self.net.z * n + k, self.net.in_plane(target), target * n + k)
+
+    def early(self, target, through):
+        n = len(self.own(0))
+        for k, (piece, held) in enumerate(zip(self.own(target), self.pre)):
+            at = self.net.g.planes * n + k
+            yield self.net.copy(piece, held, self.sems, at, self.net.in_plane(through), target * n + k)
+
+    def direct(self, target, act):
+        away = self.net.z != target
+        for end, through, far in self.ends:
+            if end == target:
+                away = away & (self.net.z != through) & (self.net.z != far)
+
+        @pl.when(away)
+        def _():
+            for copy in self.copies(target):
+                act(copy)
+
+    def start_early(self):
+        for target, through, far in self.ends:
+
+            @pl.when(self.net.z == far)
+            def _():
+                for copy in self.early(target, through):
+                    copy.start()
+
+    def start(self, far):
+        for target in range(self.net.g.planes):
+            near = (self.net.z == target - 1) | (self.net.z == target + 1)
+
+            @pl.when(jnp.logical_not(near) if far else near)
+            def _():
+                self.direct(target, lambda copy: copy.start())
+
+    def clear(self):
+        for target, _, far in self.ends:
+
+            @pl.when(self.net.z == target)
+            def _():
+                for slot in self.slots(far):
+                    slot[...] = jnp.zeros(slot.shape, slot.dtype)
+
+    def add_up(self):
+        for target, through, _ in self.ends:
+
+            @pl.when(self.net.z == through)
+            def _():
+                for copy in self.early(target, through):
+                    copy.wait_recv()
+                for piece, held in zip(self.own(target), self.pre):
+                    piece[...] = (piece[...].astype(f32) + held[...].astype(f32)).astype(bf16)
+                for copy in self.copies(target):
+                    copy.start()
+
+    def wait(self):
+        for source in range(self.net.g.planes):
+            due = self.net.z != source
+            for target, _, far in self.ends:
+                if far == source:
+                    due = due & (self.net.z != target)
+
+            @pl.when(due)
+            def _():
+                n = len(self.own(0))
+                for k, slot in enumerate(self.slots(source)):
+                    self.net.copy(slot, slot, self.sems, source * n + k, self.net.in_plane(source)).wait_recv()
+
+    def wait_send(self):
+        for target, through, far in self.ends:
+
+            @pl.when(self.net.z == far)
+            def _():
+                for copy in self.early(target, through):
+                    copy.wait_send()
+
+            @pl.when(self.net.z == through)
+            def _():
+                for copy in self.copies(target):
+                    copy.wait_send()
+
+        for target in range(self.net.g.planes):
+            self.direct(target, lambda copy: copy.wait_send())
+
+
 class PlaneGather:
-    def __init__(self, net, sems, piece, base=0):
-        self.net, self.sems, self.piece, self.base = net, sems, piece, base
+    def __init__(self, net, sems, piece):
+        self.net, self.sems, self.piece = net, sems, piece
         net.ends.append(self.wait_send)
 
     def peer(self, j):
@@ -782,12 +973,12 @@
     def across(self, j):
         net = self.net
         mine = self.piece(net.m)
-        return net.copy(mine, mine, self.sems, self.base + j, net.member(self.peer(j)))
+        return net.copy(mine, mine, self.sems, j - 1, net.member(self.peer(j)))
 
     def beside(self, j):
         net = self.net
         held = self.piece(self.source(j) if j else net.m)
-        return net.copy(held, held, self.sems, self.base + net.g.chips + j, net.member(net.sib))
+        return net.copy(held, held, self.sems, net.g.chips - 1 + j, net.member(net.sib))
 
     def start(self):
         for j in range(1, self.net.g.chips):
@@ -823,8 +1014,7 @@
             self.own, self.send = own, send
         else:
             self.own, self.send = after.own, after.send
-            after.wait_send()
-            net.ends.remove(after.wait_send)
+            net.sent(after)
         net.ends.append(self.wait_send)
 
     def block(self, ref, k):
@@ -843,7 +1033,7 @@
             self.block(self.send, chip),
             self.block(self.recv, j - 1),
             self.sems,
-            net.g.chips + j,
+            net.g.chips - 1 + j,
             net.member(2 * chip + net.c),
         )
 
@@ -953,23 +1143,12 @@
     return x[..., :LANES], x[..., LANES:]
 
 
-def later(here, before, by):
-    lane = lax.broadcasted_iota(jnp.int32, here.shape, 1)
-    return jnp.where(lane < by, pltpu.roll(before, by, 1), pltpu.roll(here, by, 1))
-
-
-def sooner(here, after, by):
-    lane = lax.broadcasted_iota(jnp.int32, here.shape, 1)
-    back = LANES - by
-    return jnp.where(lane >= back, pltpu.roll(after, back, 1), pltpu.roll(here, back, 1))
-
-
 def block_kernel(g, *refs):
     refs = list(refs)
     r = Inputs(*(refs.pop(0) for _ in Inputs._fields))
     block_out, tokens_grad, ct_out, ps_out, in_recv, up_recv, down_recv, out_recv = (refs.pop(0) for _ in range(8))
     w = types.SimpleNamespace(**{name: refs.pop(0) for name in scratch_buffers(g)})
-    sems = types.SimpleNamespace(**{name: (refs.pop(0), refs.pop(0)) for name in SEMAPHORES})
+    sems = types.SimpleNamespace(**{name: (refs.pop(0), refs.pop(0)) for name in semaphore_counts(g)})
     local_sem = refs.pop(0)
     net = Net(g)
     tok, width, pt, ch, ff = g.tok, g.width, g.plane_tokens, g.chan, g.ff_part
@@ -978,55 +1157,55 @@
     exact = lax.Precision.HIGHEST
 
     barrier = pltpu.get_barrier_semaphore()
-
-    @pl.loop(1, g.devices)
-    def _(j):
-        there = net.device(lax.rem(net.flat + j, g.devices))
+    partners = [net.member(lax.rem(net.m + j, members)) for j in range(1, members)]
+    partners += [net.in_plane(lax.rem(net.z + j, planes)) for j in range(1, planes)]
+    for there in partners:
         pl.semaphore_signal(barrier, inc=1, device_id=there, device_id_type=ON_MESH)
+
+    for m in range(members):
+        for b in range(3):
+            at = b * width + m * LANES
+            w.w_in_send[m * rows : (m + 1) * rows, b * LANES : (b + 1) * LANES] = r.input_weight[:, at : at + LANES]
+
+    own_rows = step_at(net.flat, rows)
+
+    def plane_rows(ref, z):
+        return [ref.at[step_at(x * planes + z, INNER * rows)] for x in range(g.n_dp)]
+
+    move_in = ToMembers(net, sems.w_in, lambda m: w.w_in_send.at[step_at(m, rows)], w.w_in.at[own_rows])
+    line_in = LineGather(net, sems.w_in_line, lambda z: plane_rows(w.w_in, z))
+    w.w_down[step_at(net.z, part), :] = r.down_weight[...]
+    w.w_out[step_at(net.m * planes + net.z, rows), :] = r.output_weight[...]
+    line_down = LineGather(net, sems.w_down, lambda z: [w.w_down.at[step_at(z, part)]])
+    line_out = LineGather(net, sems.w_out_line, lambda z: [w.w_out.at[step_at(net.m * planes + z, rows)]])
+    pl.semaphore_wait(barrier, len(partners))
+    move_in.start()
+    line_out.start(far=False)
 
     xhat_one, inverse_one = normalized(r.tokens[...].astype(f32))
     w.xhat_one[...] = xhat_one
     mine = step_at(net.m, tok)
     w.act_one[mine, :] = (xhat_one * r.first_gain[...] + r.first_shift[...]).astype(bf16)
-    w.cotan[mine, :] = r.cotangent[...]
+    gather_one = PlaneGather(net, sems.act_one, lambda m: w.act_one.at[step_at(m, tok)])
+    gather_one.start()
+
     for m in range(members):
-        for b in range(3):
-            at = b * width + m * LANES
-            w.w_in_send[m * rows : (m + 1) * rows, b * LANES : (b + 1) * LANES] = r.input_weight[:, at : at + LANES]
         for z in range(planes):
             at = ((m // INNER) * g.n_seq + z * INNER + m % INNER) * part
             w.w_up_send[m * rows : (m + 1) * rows, z * part : (z + 1) * part] = r.up_weight[:, at : at + part]
-    w.w_in[step_at(net.flat, rows), :] = w.w_in_send[step_at(net.m, rows), :]
-    w.w_up[step_at(net.flat, rows), :] = w.w_up_send[step_at(net.m, rows), :]
-    w.w_down[step_at(net.z, part), :] = r.down_weight[...]
-    w.w_out[step_at(net.flat, rows), :] = r.output_weight[...]
-
-    pl.semaphore_wait(barrier, g.devices - 1)
-
-    def member_of(target):
-        x, s = net.device(target)
-        return x * INNER + s % INNER
-
-    move_in = ToAll(
-        net, sems.w_in, lambda t: w.w_in_send.at[step_at(member_of(t), rows)], w.w_in.at[step_at(net.flat, rows)]
-    )
-    move_up = ToAll(
-        net, sems.w_up, lambda t: w.w_up_send.at[step_at(member_of(t), rows)], w.w_up.at[step_at(net.flat, rows)]
-    )
-    move_down = AlongPlanes(net, sems.w_down, lambda z: r.down_weight, w.w_down.at[step_at(net.z, part)])
-    gather_one = PlaneGather(net, sems.act_one, lambda m: w.act_one.at[step_at(m, tok)])
+    w.w_in[own_rows, :] = w.w_in_send[step_at(net.m, rows), :]
+    w.w_up[own_rows, :] = w.w_up_send[step_at(net.m, rows), :]
+    w.cotan[mine, :] = r.cotangent[...]
+    move_up = ToMembers(net, sems.w_up, lambda m: w.w_up_send.at[step_at(m, rows)], w.w_up.at[own_rows])
+    line_up = LineGather(net, sems.w_up_line, lambda z: plane_rows(w.w_up, z))
     gather_cotan = PlaneGather(net, sems.cotan, lambda m: w.cotan.at[step_at(m, tok)])
-    out_z = AlongPlanes(
-        net, sems.w_out_z, lambda z: w.w_out.at[step_at(net.flat, rows)], w.w_out.at[step_at(net.flat, rows)]
-    )
-
-    def out_rows(z):
-        return lambda m: w.w_out.at[step_at((m // INNER) * g.n_seq + z * INNER + m % INNER, rows)]
-
-    gather_out = [PlaneGather(net, sems.w_out, out_rows(z), 8 * z) for z in range(planes)]
-
-    gather_one.start()
-    move_in.start()
+
+    gather_out = PlaneGather(net, sems.w_out, lambda m: w.w_out.at[step_at(m, LANES)])
+    move_up.start()
+    line_out.start(far=True)
+    move_in.wait()
+    line_in.start(far=False)
+    line_in.start(far=True)
 
     w.square[...] = jnp.zeros_like(w.square)
     lane_of = step_at(net.m, LANES)
@@ -1044,15 +1223,16 @@
     w.param_cols[...] = w.square[...].T
     here = step_at(net.z, ch)
 
-    def spread(col):
-        return jnp.broadcast_to(w.param_cols[here, col : col + 1], (ch, LANES))
+    def spread(col, rows=slice(None)):
+        cols = w.param_cols[rows, col : col + 1]
+        return jnp.broadcast_to(cols, (cols.shape[0], LANES))
 
     for b in range(3):
         for i in range(3):
-            w.taps[i, b * ch : (b + 1) * ch, :] = spread(3 + 3 * i + b)
-        w.taps[3, b * ch : (b + 1) * ch, :] = spread(12 + b)
+            w.taps[i, b * LANES : (b + 1) * LANES, :] = spread(3 + 3 * i + b)
+        w.taps[3, b * LANES : (b + 1) * LANES, :] = spread(12 + b)
     w.skip[...] = spread(15)
-    w.decay[...] = spread(16)
+    w.decay[...] = spread(16, here)
 
     w.square[...] = jnp.zeros_like(w.square)
     for k, ref in enumerate((r.feat_bias, r.feat_freq, r.inner_bias, r.inner_freq)):
@@ -1094,94 +1274,192 @@
 
     to_spectrum(g, w.filt, ch, w.stage_filt, r.turns, r.forth_high, r.forth_low, w.spec_filt)
 
+    line_out.hand_on()
+    line_in.hand_on()
     gather_one.forward_all()
-    move_in.wait()
+    line_out.wait()
+    gather_out.start()
+    line_in.wait()
+    move_up.wait()
     for b in range(3):
         turned = w.w_in[:, b * LANES : (b + 1) * LANES].astype(f32).T.astype(bf16)
-        for z in range(planes):
-            at = z * 3 * ch + b * ch
-            w.w_in_t[at : at + ch, :] = turned[z * ch : (z + 1) * ch, :]
+        w.w_in_t[b * LANES : (b + 1) * LANES, :] = turned
     gather_one.wait_all()
-    biases = jnp.concatenate(
-        [w.param_cols[z * ch : (z + 1) * ch, b : b + 1] for z in range(planes) for b in range(3)], 0
-    )
-
-    @pl.loop(0, members // 2)
+    biases = jnp.concatenate([w.param_cols[:, b : b + 1] for b in range(3)], 0)
+
+    def project(step):
+        at = slice(step * 2 * tok, (step + 1) * 2 * tok)
+        w.proj[:, at] = (dot_nt(w.w_in_t[...], w.act_one[at, :]) + biases).astype(bf16)
+
+    def columns(a, n):
+        return slice((a * INNER + n) * tok, (a * INNER + n + 1) * tok)
+
+    def share_edge(values, n, rows, to_plane, from_plane, send, recv, sem, edge):
+        for a in range(2):
+            for b in range(3):
+                block = values[b * LANES : (b + 1) * LANES, columns(a, n)].astype(f32)
+                send[a * 8 : (a + 1) * 8, b * LANES : (b + 1) * LANES] = block.T[rows, :]
+        there = lax.rem(to_plane + planes, planes)
+        has_next = (to_plane >= 0) & (to_plane < planes)
+        has_before = (from_plane >= 0) & (from_plane < planes)
+
+        def copy():
+            return net.copy(send, recv, sem, 0, net.in_plane(there))
+
+        @pl.when(has_next)
+        def _():
+            copy().start()
+
+        @pl.when(jnp.logical_not(has_before))
+        def _():
+            recv[...] = jnp.zeros_like(recv)
+
+        def end():
+            @pl.when(has_next)
+            def _():
+                copy().wait_send()
+
+        net.ends.append(end)
+
+        def wait():
+            @pl.when(has_before)
+            def _():
+                copy().wait_recv()
+
+            w.square[...] = jnp.zeros_like(w.square)
+            for a in range(2):
+                for b in range(3):
+                    w.square[rows, :] = recv[a * 8 : (a + 1) * 8, b * LANES : (b + 1) * LANES]
+                    edge[a, b * LANES : (b + 1) * LANES, :] = w.square[...].T
+
+        return wait
+
+    for half in range(INNER // 2)[::-1]:
+        for a in range(2):
+            project(a * INNER // 2 + half)
+        if half == INNER // 2 - 1:
+            wait_edge = share_edge(
+                w.proj, INNER - 1, slice(LANES - 8, LANES), net.z + 1, net.z - 1, w.edge_send, w.edge_recv, sems.edge, w.edge
+            )
+            line_up.start(far=False)
+
+    net.sent(move_in, line_in, move_up, gather_one)
+
+    group = 32
+    lane = lax.broadcasted_iota(jnp.int32, (group, LANES), 1)
+
+    def rows_of(b, step):
+        return pl.ds(pl.multiple_of(b * LANES + step * group, group), group)
+
+    def rolled(x, by):
+        return pltpu.roll(x, by, 1), pltpu.roll(x, (2 * by) % LANES, 1)
+
+    def shifted(here, there, edge):
+        return jnp.where(edge(1), there[0], here[0]), jnp.where(edge(2), there[1], here[1])
+
+    from_left, from_right = (lambda k: lane < k), (lambda k: lane >= LANES - k)
+
+    def filter_blocks(step, which):
+        for a in range(2):
+            conv = {}
+            for b in range(3):
+                at = rows_of(b, step)
+                taps = [w.taps[i, at, :] for i in range(4)]
+                before = rolled(w.edge[a, at, :], 1) if 0 in which else None
+                for n in range(max(which) + 1):
+                    now = w.proj[at, columns(a, n)].astype(f32)
+                    turned = rolled(now, 1)
+                    if n in which:
+                        one, two = shifted(turned, before, from_left)
+                        conv[b, n] = taps[3] + taps[2] * now + taps[1] * one + taps[0] * two
+                        w.conv[at, columns(a, n)] = conv[b, n]
+                    before = turned
+            for n in which:
+                carried = conv[0, n] * conv[2, n]
+                w.carried[rows_of(0, step), columns(a, n)] = carried
+                w.car_send[rows_of(0, step), columns(a, n)] = carried.astype(bf16)
+
+    @pl.loop(0, LANES // group)
     def _(step):
-        at = step_at(step, 2 * tok)
-        w.proj_send[:, at] = (dot_nt(w.w_in_t[...], w.act_one[at, :]) + biases).astype(bf16)
-
-    move_proj = AlongPlanes(
-        net, sems.proj, lambda z: w.proj_send.at[step_at(z, 3 * ch)], w.proj_recv.at[step_at(net.z, 3 * ch)]
-    )
-    move_proj.start()
-    w.proj_recv[step_at(net.z, 3 * ch), :] = w.proj_send[step_at(net.z, 3 * ch), :]
-    gather_cotan.start()
-    out_z.start()
-    gather_cotan.forward_all()
-    out_z.wait()
-    for k in gather_out:
-        k.start()
-    move_proj.wait()
-    move_up.start()
+        filter_blocks(step, range(1, INNER))
+
+    wait_edge()
+
+    @pl.loop(0, LANES // group)
+    def _(step):
+        filter_blocks(step, range(1))
+
+    own_z = step_at(net.z, ch)
+
+    def along(sem, send, recv):
+        move = AlongPlanes(net, sem, lambda z: send.at[step_at(z, ch)], recv.at[own_z])
+        move.start()
+        recv[own_z, :] = send[own_z, :]
+        return move
 
     def place(d):
         a, n = d // blocks, d % blocks
-        return a, n, step_at(n // INNER, 3 * ch), step_at(a * INNER + n % INNER, LANES)
-
-    for a in range(2):
-        w.padded[a, 0] = jnp.zeros((3 * ch, LANES), f32)
-        w.grad_conv[a, blocks] = jnp.zeros((3 * ch, LANES), f32)
-
-    @pl.loop(0, 2 * blocks)
-    def _(d):
-        a, n, from_rows, from_lanes = place(d)
-        w.padded[a, n + 1] = w.proj_recv[from_rows, from_lanes].astype(f32)
-
-    @pl.loop(0, 2 * blocks)
-    def _(d):
-        a, n, _, _ = place(d)
-        now, before = w.padded[a, n + 1], w.padded[a, n]
-        conv = w.taps[3] + w.taps[2] * now + w.taps[1] * later(now, before, 1) + w.taps[0] * later(now, before, 2)
-        w.conv[d] = conv
-        w.carried[n, step_at(a, ch), :] = conv[:ch] * conv[2 * ch :]
+        return n, step_at(a, ch), step_at(n // INNER, ch), step_at(a * INNER + n % INNER, LANES)
+
+    def to_signal(recv):
+        @pl.loop(0, 2 * blocks)
+        def _(d):
+            n, at, from_rows, from_lanes = place(d)
+            w.signal[n, at, :] = recv[from_rows, from_lanes].astype(f32)
+
+    def to_planes(send):
+        @pl.loop(0, 2 * blocks)
+        def _(d):
+            n, at, to_row, to_lane = place(d)
+            send[to_row, to_lane] = w.back_sig[n, at, :].astype(bf16)
+
+    move_car = along(sems.car, w.car_send, w.car_recv)
+    gather_cotan.start()
+    line_up.hand_on()
+    move_car.wait()
+    line_down.start(far=False)
+    to_signal(w.car_recv)
 
     def both(filt):
         return jnp.concatenate([filt, filt], 1)
 
-    to_spectrum(g, w.carried, 2 * ch, w.stage, r.turns, r.forth_high, r.forth_low, w.spec_car)
+    to_spectrum(g, w.signal, 2 * ch, w.stage, r.turns, r.forth_high, r.forth_low, w.spec_car)
 
     def forth_product(at):
         (hr, hi), (xr, xi) = halves(both(w.spec_filt[at])), halves(w.spec_car[at])
         return xr * hr - xi * hi, xr * hi + xi * hr
 
     from_spectrum(g, forth_product, 2 * ch, w.stage, r.turns, r.back_high, r.back_low, w.back_sig)
-
-    @pl.loop(0, 2 * blocks)
-    def _(d):
-        a, n, _, _ = place(d)
-        at = step_at(a, ch)
-        long_out = w.back_sig[n, at, :] + w.skip[...] * w.carried[n, at, :]
-        w.long[n, at, :] = long_out
-        w.pre_send[step_at(d, ch), :] = (w.conv[d, ch : 2 * ch, :] * long_out).astype(bf16)
-
-    own_block, own_slot = step_at(net.chan_block, ch), step_at(net.flat, ch)
-
-    def chan_block_of(target):
-        x, s = net.device(target)
-        return (x * INNER + s % INNER) * planes + s // INNER
-
-    move_pre = ToAll(net, sems.pre, lambda t: w.pre_send.at[step_at(t, ch)], w.pre_recv.at[own_block])
+    to_planes(w.y_send)
+    move_y = along(sems.y, w.y_send, w.y_recv)
+    gather_out.forward_all()
+    move_y.wait()
+    line_up.start(far=True)
+    line_down.start(far=True)
+
+    @pl.loop(0, LANES // group)
+    def _(step):
+        at = rows_of(0, step)
+        long_out = w.y_recv[at, :].astype(f32) + jnp.tile(w.skip[at, :], (1, members)) * w.carried[at, :]
+        w.long[at, :] = long_out
+        w.act_pre[at, :] = (w.conv[rows_of(1, step), :] * long_out).astype(bf16)
+
+    own_block = step_at(net.m, LANES)
+    move_pre = ToMembers(net, sems.pre, lambda m: w.act_pre.at[:, step_at(m, tok)], w.pre_recv.at[own_block])
     move_pre.start()
-    w.pre_recv[own_block, :] = w.pre_send[own_slot, :]
-    for k in gather_out:
-        k.forward_all()
-    for k in gather_out:
-        k.wait_all()
+    w.pre_recv[own_block, :] = w.act_pre[:, mine]
+    gather_cotan.forward_all()
+    gather_out.wait_all()
     move_pre.wait()
-    move_down.start()
-
-    pre_rows = w.pre_recv[...].astype(f32).T.astype(bf16)
+
+    def by_line(piece):
+        m, z = divmod(piece, planes)
+        return (m // INNER) * g.n_seq + z * INNER + m % INNER
+
+    for k in range(members * planes):
+        at = by_line(k) * rows
+        w.pre_line[k * rows : (k + 1) * rows, :] = w.pre_recv[at : at + rows, :]
+    pre_rows = w.pre_line[...].astype(f32).T.astype(bf16)
     branch = dot_nn(pre_rows, w.w_out[...])
     residual = r.tokens[...].astype(f32) + branch + r.output_bias[...]
     w.residual[...] = residual
@@ -1190,26 +1468,71 @@
     w.act_two[mine, :] = (xhat_two * r.second_gain[...] + r.second_shift[...]).astype(bf16)
     gather_two = PlaneGather(net, sems.act_two, lambda m: w.act_two.at[step_at(m, tok)])
     gather_two.start()
+    net.sent(move_car, move_y, move_pre)
 
     gather_cotan.wait_all()
-    move_up.wait()
+    line_up.wait()
     sum_two = PlaneSum(net, sems.gn_two, w.gn_two_sib, w.gn_two_recv, w.gn_two_own, w.gn_two_send)
     w.ps[...] = jnp.zeros_like(w.ps)
     hidden_block = [net.x * g.n_seq + z * INNER + net.q for z in range(planes)]
     up_bias = jnp.concatenate([r.up_bias[:, step_at(k, part)] for k in hidden_block], 1)
     bias_sum = jnp.zeros((1, ff), f32)
+    slopes = []
     for j in range(chips):
         if j == 1:
             gather_two.forward_all()
+            line_down.hand_on()
         gather_two.wait(j)
-        chip = lax.rem(net.p + chips - j, chips)
+        at = step_at(lax.rem(net.p + chips - j, chips), 2 * tok)
+        gelu, slope = gelu_pair(dot_nn(w.act_two[at, :], w.w_up[...]) + up_bias)
+        w.act_three[at, :] = gelu.astype(bf16)
+        slopes.append(slope)
+    def to_local(src, dst):
+        copy = pltpu.make_async_copy(src, dst, local_sem.at[0])
+        copy.start()
+        copy.wait()
+
+    plane_part = INNER * rows
+
+    def parts_of(ref, z):
+        at = z * g.n_dp * plane_part
+        return [ref.at[pl.ds(at + x * plane_part, plane_part)] for x in range(g.n_dp)]
+
+    def added(ref):
+        group_rows = g.n_dp * plane_part
+        return sum(ref[z * group_rows : (z + 1) * group_rows, :].astype(f32) for z in range(planes)).astype(bf16)
+
+    def to_owners(sem, mid, out):
+        move = ToMembers(net, sem, lambda m: mid.at[step_at(m, rows)], out.at[step_at(net.m, rows)])
+        move.start()
+        to_local(mid.at[step_at(net.m, rows)], out.at[step_at(net.m, rows)])
+        return move
+
+    sum_up = LineSum(
+        net,
+        sems.up_grad,
+        lambda z: plane_rows(w.up_send, z),
+        lambda z: parts_of(w.up_parts, z),
+        [w.up_pre.at[x * plane_part : (x + 1) * plane_part] for x in range(g.n_dp)],
+    )
+    sum_down = LineSum(
+        net, sems.down_grad, lambda z: [w.down_send.at[step_at(z, part)]], lambda z: [w.down_parts.at[step_at(z, part)]], [w.down_pre]
+    )
+    @pl.loop(0, ff // 256)
+    def _(step):
+        at = step_at(step, 256)
+        turned = w.act_three[:, at].astype(f32).T.astype(bf16)
+        w.down_send[at, :] = dot_nn(turned, w.cotan[...]).astype(bf16)
+
+    sum_down.start_early()
+    line_down.wait()
+    sum_down.start(far=False)
+    sum_down.clear()
+    w.down_parts[step_at(net.z, part), :] = w.down_send[step_at(net.z, part), :]
+    for j in range(1, chips + 1):
+        chip = lax.rem(net.p + j, chips)
         at = step_at(chip, 2 * tok)
-        upper = dot_nn(w.act_two[at, :], w.w_up[...]) + up_bias
-        gelu, slope = gelu_pair(upper)
-        w.act_three[at, :] = gelu.astype(bf16)
-        if j == 0:
-            move_down.wait()
-        grad_upper = (dot_nt(w.cotan[at, :], w.w_down[...]) * slope).astype(bf16)
+        grad_upper = (dot_nt(w.cotan[at, :], w.w_down[...]) * slopes[-j]).astype(bf16)
         w.grad_up[at, :] = grad_upper
         bias_sum = bias_sum + column_sum(grad_upper.astype(f32))
         sum_two.own[at, :] = dot_nt(grad_upper, w.w_up[...]).astype(bf16)
@@ -1219,26 +1542,25 @@
     for j in range(1, chips):
         sum_two.relay(j)
 
-    def to_local(src, dst):
-        copy = pltpu.make_async_copy(src, dst, local_sem)
-        copy.start()
-        copy.wait()
-
-    own_rows = step_at(net.flat, rows)
-    move_up_grad = ToAll(net, sems.up_grad, lambda t: w.up_send.at[step_at(t, rows)], up_recv.at[own_rows])
-    @pl.loop(0, width // LANES)
+    @pl.loop(0, width // 256)
     def _(step):
-        at = step_at(step, LANES)
+        at = step_at(step, 256)
         turned = w.act_two[:, at].astype(f32).T.astype(bf16)
         w.up_send[at, :] = dot_nn(turned, w.grad_up[...]).astype(bf16)
 
-    move_up_grad.start()
-    to_local(w.up_send.at[own_rows], up_recv.at[own_rows])
-    sum_result = PlaneSum(net, sems.result, w.result_sib, w.result_recv, w.result_own, w.result_send)
+    sum_up.start_early()
+    sum_down.add_up()
+    sum_down.start(far=True)
+    for slot, piece in zip(parts_of(w.up_parts, net.z), plane_rows(w.up_send, net.z)):
+        slot[...] = piece[...]
+    net.sent(gather_cotan)
+    sum_result = PlaneSum(net, sems.result, w.result_sib, w.result_recv, w.cotan, w.result_send)
     for j in range(1, chips + 1):
         chip = lax.rem(net.p + j, chips)
         at = step_at(chip, 2 * tok)
         sum_result.own[at, :] = dot_nn(w.act_three[at, :], w.w_down[...]).astype(bf16)
+    sum_up.clear()
+    sum_up.start(far=False)
     grad_two = sum_two.result()
 
     xhat_two = w.xhat_two[...]
@@ -1252,95 +1574,53 @@
     w.grad_branch[...] = grad_branch
     to_rows(w.ps, AT_OUTPUT_BIAS, column_sum(grad_branch.astype(f32)))
 
-    @pl.loop(0, width // 256)
+    per_step = 256 // rows
+    for step in range(width // 256):
+        grad = dot_nt(w.w_out[step * 256 : (step + 1) * 256, :], w.grad_branch[...]).astype(bf16)
+        for k in range(per_step):
+            at = by_line(step * per_step + k) * rows
+            w.gpre_send[at : at + rows, :] = grad[k * rows : (k + 1) * rows, :]
+
+    move_gpre = ToMembers(net, sems.w_in, lambda m: w.gpre_send.at[step_at(m, LANES)], w.gpre.at[:, mine])
+    move_gpre.start()
+    w.gpre[:, mine] = w.gpre_send[own_block, :]
+
+    sum_out = PlaneSum(net, sems.w_out_grad, w.w_out_grad_sib, w.w_out_grad_recv, after=sum_two)
+    for m in range(members):
+        at = slice(m * LANES, (m + 1) * LANES)
+        sum_out.own[at, :] = dot_nn(w.pre_line[at, :], w.grad_branch[...]).astype(bf16)
+    sum_up.add_up()
+    move_gpre.wait()
+    for total in (sum_out, sum_result):
+        for j in range(1, chips + 1):
+            total.start(lax.rem(net.p + j, chips))
+
+    @pl.loop(0, LANES // group)
     def _(step):
-        at = step_at(step, 256)
-        w.gpre_send[at, :] = dot_nt(w.w_out[at, :], w.grad_branch[...]).astype(bf16)
-
-    move_gpre = ToAll(net, sems.gpre, lambda t: w.gpre_send.at[step_at(chan_block_of(t), ch)], w.gpre_recv.at[own_slot])
-    move_gpre.start()
-    w.gpre_recv[own_slot, :] = w.gpre_send[own_block, :]
-
-    for j in range(1, chips + 1):
-        sum_result.start(lax.rem(net.p + j, chips))
-
-    @pl.loop(0, ff // LANES)
-    def _(step):
-        at = step_at(step, LANES)
-        turned = w.act_three[:, at].astype(f32).T.astype(bf16)
-        w.down_send[at, :] = dot_nn(turned, w.cotan[...]).astype(bf16)
-
-    move_gpre.wait()
-    move_down_grad = AlongPlanes(
-        net, sems.down_grad, lambda z: w.down_send.at[step_at(z, part)], down_recv.at[step_at(net.z, part)]
-    )
-    move_down_grad.start()
-    to_local(w.down_send.at[step_at(net.z, part)], down_recv.at[step_at(net.z, part)])
-
-    w.sums[...] = jnp.zeros_like(w.sums)
-
-    @pl.loop(0, 2 * blocks)
-    def _(d):
-        a, n, _, _ = place(d)
-        at = step_at(a, ch)
-        grad_pre = w.gpre_recv[step_at(d, ch), :].astype(f32)
-        grad_long = grad_pre * w.conv[d, ch : 2 * ch, :]
-        w.grad_long[n, at, :] = grad_long
-        w.grad_conv[a, n, ch : 2 * ch, :] = grad_pre * w.long[n, at, :]
-        w.sums[5, :ch, :] += grad_long * w.carried[n, at, :]
-
-    to_spectrum(g, w.grad_long, 2 * ch, w.stage, r.turns, r.forth_high, r.forth_low, w.spec_grad)
+        at, second = rows_of(0, step), rows_of(1, step)
+        grad_pre = w.gpre[at, :].astype(f32)
+        grad_long = grad_pre * w.conv[second, :]
+        w.grad_long[at, :] = grad_long
+        w.gl_send[at, :] = grad_long.astype(bf16)
+        w.grad_conv[second, :] = grad_pre * w.long[at, :]
+
+    move_gl = along(sems.car, w.gl_send, w.gl_recv)
+    for j in range(1, chips):
+        sum_out.relay(j)
+    move_gl.wait()
+    sum_up.start(far=True)
+    to_signal(w.gl_recv)
+    to_spectrum(g, w.signal, 2 * ch, w.stage, r.turns, r.forth_high, r.forth_low, w.spec_grad)
 
     def back_product(at):
         (hr, hi), (gr, gi) = halves(both(w.spec_filt[at])), halves(w.spec_grad[at])
         return hr * gr + hi * gi, hr * gi - hi * gr
 
     from_spectrum(g, back_product, 2 * ch, w.stage, r.turns, r.back_high, r.back_low, w.back_sig)
-
-    @pl.loop(0, 2 * blocks)
-    def _(d):
-        a, n, _, _ = place(d)
-        at = step_at(a, ch)
-        grad_car = w.back_sig[n, at, :] + w.skip[...] * w.grad_long[n, at, :]
-        w.grad_conv[a, n, :ch, :] = grad_car * w.conv[d, 2 * ch :, :]
-        w.grad_conv[a, n, 2 * ch :, :] = grad_car * w.conv[d, :ch, :]
-
-    @pl.loop(0, 2 * blocks)
-    def _(d):
-        a, n, to_row, to_lane = place(d)
-        now, after = w.grad_conv[a, n], w.grad_conv[a, n + 1]
-        grad = w.taps[2] * now + w.taps[1] * sooner(now, after, 1) + w.taps[0] * sooner(now, after, 2)
-        grad = grad.astype(bf16)
-        w.gproj_send[to_row, to_lane] = grad
-        w.sums[4] += grad.astype(f32)
-
-    move_gproj = AlongPlanes(
-        net, sems.gproj, lambda z: w.gproj_send.at[step_at(z, 3 * ch)], w.gproj_recv.at[step_at(net.z, 3 * ch)]
-    )
-    move_gproj.start()
-    w.gproj_recv[step_at(net.z, 3 * ch), :] = w.gproj_send[step_at(net.z, 3 * ch), :]
-
+    to_planes(w.gc_send)
+    move_gc = along(sems.y, w.gc_send, w.gc_recv)
     for j in range(1, chips):
         sum_result.relay(j)
-
-    sum_out = PlaneSum(net, sems.w_out_grad, w.w_out_grad_sib, w.w_out_grad_recv, after=sum_two)
-    for j in range(1, chips + 1):
-        chip = lax.rem(net.p + j, chips)
-        at = step_at(chip, 2 * tok)
-        sum_out.own[at, :] = dot_nn(w.pre_recv[at, :], w.grad_branch[...]).astype(bf16)
-        sum_out.start(chip)
-
-    @pl.loop(0, 2 * blocks)
-    def _(d):
-        a, n, _, _ = place(d)
-        grad, now, before = w.grad_conv[a, n], w.padded[a, n + 1], w.padded[a, n]
-        w.sums[3] += grad
-        w.sums[2] += grad * now
-        w.sums[1] += grad * later(now, before, 1)
-        w.sums[0] += grad * later(now, before, 2)
-
-    for j in range(1, chips):
-        sum_out.relay(j)
 
     def filt_product(at):
         out = []
@@ -1375,68 +1655,97 @@
         r_one = slope_one * col(1)
         w.ps[AT_FEAT : AT_FEAT + features_rows, :FILT] += dot_nt(feats, r_one, exact)
         for k, x in enumerate((r_one, slope_one * w.p_one[:, at], r_two, slope_two * w.p_two[:, at])):
-            w.ps[AT_VECTOR + 8 * k : AT_VECTOR + 8 * k + 8, :FILT] += dot_nt(ones, x, exact)
-
-    lane = lax.broadcasted_iota(jnp.int32, (ch, LANES), 1)
-    tile = w.ct[chan_rows, :]
-
-    def put(tile, k, x):
-        return jnp.where(lane == CT_FILTER + k, jnp.sum(x, 1, keepdims=True), tile)
-
-    for b in range(3):
-        cut = slice(b * ch, (b + 1) * ch)
-        tile = put(tile, b, w.sums[4, cut, :])
-        for i in range(3):
-            tile = put(tile, 3 + 3 * i + b, w.sums[i, cut, :])
-        tile = put(tile, 12 + b, w.sums[3, cut, :])
-    tile = put(tile, 15, w.sums[5, :ch, :])
-    w.ct[chan_rows, :] = tile
+            w.ps[AT_VECTOR + k : AT_VECTOR + k + 1, :FILT] += dot_nt(ones, x, exact)[:1, :]
+
     ct_z = AlongPlanes(net, sems.ct_z, lambda z: w.ct.at[chan_rows], w.ct.at[chan_rows])
     ct_z.start()
-
+    sum_up.wait()
+    w.up_mid[...] = added(w.up_parts)
+    move_up_grad = to_owners(sems.w_up, w.up_mid, up_recv)
+    move_gc.wait()
+
+    @pl.loop(0, LANES // group)
+    def _(step):
+        at, last = rows_of(0, step), rows_of(2, step)
+        grad = w.gc_recv[at, :].astype(f32) + jnp.tile(w.skip[at, :], (1, members)) * w.grad_long[at, :]
+        w.grad_conv[at, :] = grad * w.conv[last, :]
+        w.grad_conv[last, :] = grad * w.conv[at, :]
+
+    wait_back_edge = share_edge(
+        w.grad_conv, 0, slice(0, 8), net.z - 1, net.z + 1, w.back_edge_send, w.back_edge_recv, sems.back_edge, w.back_edge
+    )
+
+    line_out_grad = LineSum(
+        net,
+        sems.out_grad,
+        lambda z: [w.out_sum.at[step_at(z, rows)]],
+        lambda z: [w.out_parts.at[step_at(z, rows)]],
+        [w.out_pre],
+    )
     w.out_sum[...] = sum_out.result().astype(bf16)
-    own_part = LANES // rows
-
-    def out_grad_copy(k):
-        return net.copy(
-            w.out_sum.at[k * rows : (k + 1) * rows],
-            out_recv.at[step_at(net.z, rows)],
-            sems.out_grad,
-            net.z,
-            net.device(net.m * own_part + k),
-            k,
-        )
-
-    def out_grad_send(k, act):
-        @pl.when(net.m * own_part + k != net.flat)
-        def _():
-            act(out_grad_copy(k))
-
-    for k in range(own_part):
-        out_grad_send(k, lambda copy: copy.start())
-
-        @pl.when(net.m * own_part + k == net.flat)
-        def _():
-            to_local(w.out_sum.at[k * rows : (k + 1) * rows], out_recv.at[step_at(net.z, rows)])
-
-    def out_grad_end():
-        for k in range(own_part):
-            out_grad_send(k, lambda copy: copy.wait_send())
-        for z in range(planes):
-
-            @pl.when((net.flat // own_part != net.m) | (net.z != z))
-            def _():
-                here = out_recv.at[z * rows : (z + 1) * rows]
-                net.copy(here, here, sems.out_grad, z, net.member(net.sib)).wait_recv()
-
+    line_out_grad.start_early()
+    line_out_grad.clear()
+    line_out_grad.start(far=False)
+    line_out_grad.start(far=True)
+    w.out_parts[step_at(net.z, rows), :] = w.out_sum[step_at(net.z, rows), :]
+
+
+    def filter_blocks_back(step, which):
+        for a in range(2):
+            for b in range(3):
+                at = rows_of(b, step)
+                taps = [w.taps[i, at, :] for i in range(3)]
+                after = rolled(w.back_edge[a, at, :], LANES - 1) if INNER - 1 in which else None
+                for n in range(min(which), INNER)[::-1]:
+                    now = w.grad_conv[at, columns(a, n)]
+                    turned = rolled(now, LANES - 1)
+                    if n in which:
+                        one, two = shifted(turned, after, from_right)
+                        w.gproj[at, columns(a, n)] = (taps[2] * now + taps[1] * one + taps[0] * two).astype(bf16)
+                    after = turned
+
+    @pl.loop(0, LANES // group)
+    def _(step):
+        filter_blocks_back(step, range(INNER - 1))
+
+    wait_back_edge()
+
+    @pl.loop(0, LANES // group)
+    def _(step):
+        filter_blocks_back(step, range(INNER - 1, INNER))
+
+    @pl.loop(0, width // 256)
+    def _(step):
+        at = step_at(step, 256)
+        grad = dot_nn(w.gproj[...], w.act_one[:, at])
+        for b in range(3):
+            cut = slice(b * LANES, (b + 1) * LANES)
+            w.in_send[at, cut] = grad[cut].T.astype(bf16)
+
+    sum_in = LineSum(
+        net,
+        sems.in_grad,
+        lambda z: plane_rows(w.in_send, z),
+        lambda z: parts_of(w.w_in, z),
+        [w.w_in_send.at[x * plane_part : (x + 1) * plane_part] for x in range(g.n_dp)],
+    )
+    line_out_grad.add_up()
+    sum_in.start_early()
+    sum_in.clear()
+    sum_in.start(far=False)
+    sum_in.start(far=True)
+    for slot, piece in zip(parts_of(w.w_in, net.z), plane_rows(w.in_send, net.z)):
+        slot[...] = piece[...]
+    ct_z.wait()
+    gather_ct = PlaneGather(net, sems.act_one, lambda m: w.ct.at[step_at(m, LANES)])
+    gather_ct.start()
     block_out[...] = (w.residual[...] + sum_result.result() + r.down_bias[...]).astype(bf16)
-    move_gproj.wait()
-    sum_one = PlaneSum(net, sems.gn_one, w.gn_one_sib, w.gn_one_recv, after=sum_result)
+    sum_one = PlaneSum(net, sems.gn_two, w.gn_one_sib, w.gn_one_recv, after=sum_result)
     shift_sum = gain_sum = jnp.zeros((1, width), f32)
     for j in range(1, chips + 1):
         chip = lax.rem(net.p + j, chips)
         at = step_at(chip, 2 * tok)
-        turned = w.gproj_recv[:, at].astype(f32).T.astype(bf16)
+        turned = w.gproj[:, at].astype(f32).T.astype(bf16)
         partial = dot_nn(turned, w.w_in_t[...])
         sum_one.own[at, :] = partial.astype(bf16)
         sum_one.start(chip)
@@ -1444,48 +1753,83 @@
         gain_sum = gain_sum + column_sum(partial * w.act_one[at, :].astype(f32))
     to_rows(w.ps, AT_FIRST_GAIN, (gain_sum - r.first_shift[...] * shift_sum) / r.first_gain[...])
     to_rows(w.ps, AT_FIRST_SHIFT, shift_sum)
-    share = PS_ROWS // g.devices
-    own_share = step_at(net.flat, share)
-    move_ps = ToAll(net, sems.ps, lambda t: w.ps.at[step_at(t, share)], w.ps_recv.at[own_share])
+
+    kept = w.conv
+
+    @pl.loop(0, LANES // group)
+    def _(step):
+        for b in range(3):
+            at = rows_of(b, step)
+            sums = [jnp.zeros((group, LANES), f32)] * 5
+            for a in range(2):
+                before = rolled(w.edge[a, at, :], 1)
+                for n in range(INNER):
+                    grad, now = w.grad_conv[at, columns(a, n)], w.proj[at, columns(a, n)].astype(f32)
+                    turned = rolled(now, 1)
+                    one, two = shifted(turned, before, from_left)
+                    terms = (grad * two, grad * one, grad * now, grad, w.gproj[at, columns(a, n)].astype(f32))
+                    sums = [x + y for x, y in zip(sums, terms)]
+                    before = turned
+            for k in range(5):
+                kept[at, k * LANES : (k + 1) * LANES] = sums[k]
+        at = rows_of(0, step)
+        product = w.grad_long[at, :] * w.carried[at, :]
+        kept[at, 5 * LANES : 6 * LANES] = sum(product[:, k * LANES : (k + 1) * LANES] for k in range(members))
+
+    which_lane = lax.broadcasted_iota(jnp.int32, (LANES, LANES), 1)
+    tile = jnp.zeros((LANES, LANES), f32)
+    for k, (kind, b) in enumerate(
+        [(4, b) for b in range(3)] + [(i, b) for i in range(3) for b in range(3)] + [(3, b) for b in range(3)] + [(5, 0)]
+    ):
+        part_sums = kept[b * LANES : (b + 1) * LANES, kind * LANES : (kind + 1) * LANES]
+        tile = jnp.where(which_lane == k, jnp.sum(part_sums, 1, keepdims=True), tile)
+    w.ps[pl.ds(pl.multiple_of(AT_CHANNEL + net.m * 16, 16), 16), :] = tile.T[:16, :]
+
+    share = PS_ROWS // members
+    own_share = step_at(net.m, share)
+    move_ps = ToMembers(net, sems.ps, lambda m: w.ps.at[step_at(m, share)], w.ps_recv.at[own_share])
     move_ps.start()
     w.ps_recv[own_share, :] = w.ps[own_share, :]
-
-    @pl.loop(0, width // LANES)
-    def _(step):
-        at = step_at(step, LANES)
-        grad = dot_nn(w.gproj_recv[...], w.act_one[:, at])
-        for b in range(3):
-            piece = [grad[z * 3 * ch + b * ch : z * 3 * ch + (b + 1) * ch] for z in range(planes)]
-            w.in_send[at, b * LANES : (b + 1) * LANES] = jnp.concatenate(piece, 0).T.astype(bf16)
-
-    move_in_grad = ToAll(net, sems.in_grad, lambda t: w.in_send.at[step_at(t, rows)], in_recv.at[own_rows])
-    move_in_grad.start()
-    to_local(w.in_send.at[own_rows], in_recv.at[own_rows])
     for j in range(1, chips):
         sum_one.relay(j)
-    ct_z.wait()
-    gather_ct = PlaneGather(net, sems.ct, lambda m: w.ct.at[step_at(m, LANES)])
-    gather_ct.start()
+    sum_in.add_up()
     move_ps.wait()
-    total = w.ps_recv[:share, :]
-    for k in range(1, g.devices):
-        total = total + w.ps_recv[k * share : (k + 1) * share, :]
-    w.ps_all[own_share, :] = total
-    move_back = ToAll(net, sems.ps_back, lambda t: w.ps_all.at[own_share], w.ps_all.at[own_share])
+
+    def shares_added(ref, count):
+        return sum(ref[k * share : (k + 1) * share, :] for k in range(count))
+
+    own_line = step_at(net.z, share)
+    w.ps_line[own_line, :] = shares_added(w.ps_recv, members)
+    line_ps = AlongPlanes(net, sems.ps_line, lambda z: w.ps_line.at[own_line], w.ps_line.at[own_line])
+    line_ps.start()
+    sum_down.wait()
+    w.down_total[...] = sum(w.down_parts[z * part : (z + 1) * part, :].astype(f32) for z in range(planes))
+    down_out = pltpu.make_async_copy(w.down_total, down_recv, local_sem.at[1])
+    down_out.start()
+    net.ends.append(down_out.wait)
+    gather_ct.forward_all()
+    line_ps.wait()
+    w.ps_all[own_share, :] = shares_added(w.ps_line, planes)
+    move_back = ToMembers(net, sems.ps_back, lambda m: w.ps_all.at[own_share], w.ps_all.at[own_share])
     move_back.start()
-    gather_ct.forward_all()
+    sum_in.wait()
+    w.in_mid[...] = added(w.w_in)
+    move_in_grad = to_owners(sems.pre, w.in_mid, in_recv)
     grad_one = sum_one.result()
 
     grad_tokens = norm_back(grad_one, w.xhat_one[...], inverse_one, r.first_gain[...])
     tokens_grad[...] = (w.grad_res[...] + grad_tokens).astype(bf16)
     gather_ct.wait_all()
     ct_out[...] = w.ct[...]
+    line_out_grad.wait()
+    w.out_total[...] = sum(w.out_parts[z * rows : (z + 1) * rows, :].astype(f32) for z in range(planes))
+    out_out = pltpu.make_async_copy(w.out_total, out_recv, local_sem.at[2])
+    out_out.start()
+    net.ends.append(out_out.wait)
     move_back.wait()
     ps_out[...] = w.ps_all[...]
     move_in_grad.wait()
     move_up_grad.wait()
-    move_down_grad.wait()
-    out_grad_end()
     net.finish()
 
 
@@ -1503,20 +1847,20 @@
     for m in range(g.members):
         x, q = m // INNER, m % INNER
         parts = [x * g.n_seq + z * INNER + q for z in range(planes)]
-        total = sum(in_recv[k * rows : (k + 1) * rows, :].astype(f32) for k in parts)
+        total = in_recv[m * rows : (m + 1) * rows, :].astype(f32)
         for b in range(3):
             input_weight[:, b * width + m * LANES : b * width + (m + 1) * LANES] = total[:, b * LANES : (b + 1) * LANES]
-        total = sum(up_recv[k * rows : (k + 1) * rows, :].astype(f32) for k in parts)
+        total = up_recv[m * rows : (m + 1) * rows, :].astype(f32)
         for z, k in enumerate(parts):
             cut = slice(z * g.down_rows, (z + 1) * g.down_rows)
             up_weight[:, k * g.down_rows : (k + 1) * g.down_rows] = total[:, cut]
-    down_weight[...] = sum(down_recv[z * g.down_rows : (z + 1) * g.down_rows, :].astype(f32) for z in range(planes))
-    output_weight[...] = sum(out_recv[z * rows : (z + 1) * rows, :].astype(f32) for z in range(planes))
+    down_weight[...] = down_recv[...]
+    output_weight[...] = out_recv[...]
     for m in range(g.members):
         cut = slice(m * LANES, (m + 1) * LANES)
         turned = ct[cut, :].T
         filter_weight[:, cut] = turned[:FILT, :]
-        line = lambda k: turned[CT_FILTER + k : CT_FILTER + k + 1, :]
+        line = lambda k: ps[AT_CHANNEL + 16 * m + k : AT_CHANNEL + 16 * m + k + 1, :]
         for b in range(3):
             at = b * g.members + m
             input_bias[at : at + 1, :] = line(b)
@@ -1532,7 +1876,7 @@
     feat_weight[...] = ps[AT_FEAT : AT_FEAT + FEAT, :FILT]
     inner_weight[...] = ps[:FILT, :FILT]
     for k, out in enumerate((feat_bias, feat_freq, inner_bias, inner_freq)):
-        out[...] = ps[AT_VECTOR + 8 * k : AT_VECTOR + 8 * k + 1, :FILT]
+        out[...] = ps[AT_VECTOR + k : AT_VECTOR + k + 1, :FILT]
 
 
 def on_device_in_kernels(g, *args):
@@ -1549,16 +1893,16 @@
             S((tok, width), bf16),
             S((width, LANES), f32),
             S((PS_ROWS, LANES), f32),
-            S((g.devices * g.rows, 3 * LANES), bf16),
-            S((g.devices * g.rows, g.ff_part), bf16),
-            S((g.planes * g.down_rows, width), bf16),
-            S((g.planes * g.rows, width), bf16),
+            S((g.members * g.rows, 3 * LANES), bf16),
+            S((g.members * g.rows, g.ff_part), bf16),
+            S((g.down_rows, width), f32),
+            S((g.rows, width), f32),
         ],
         in_specs=[in_vmem] * len(operands),
         out_specs=[in_vmem] * 4 + [anywhere] * 4,
         scratch_shapes=[pltpu.VMEM(shape, dtype) for shape, dtype in scratch_buffers(g).values()]
-        + [pltpu.SemaphoreType.DMA((count,)) for count in SEMAPHORES.values() for _ in range(2)]
-        + [pltpu.SemaphoreType.DMA],
+        + [pltpu.SemaphoreType.DMA((count,)) for pair in semaphore_counts(g).values() for count in pair]
+        + [pltpu.SemaphoreType.DMA((3,))],
         compiler_params=pltpu.CompilerParams(
             collective_id=0, has_side_effects=True, vmem_limit_bytes=63 * 1024 * 1024
         ),

time: 247 us -> 181 us (0.73); the launches traced: 243 us -> 181 us
  Pallas kernels: 242 us -> 180 us
    pallas_call x1, Pallas kernels: 238 us -> 177 us  [on_device_in_kernels(): pl.pallas_call(functools.partial(block_kernel, g), out_shape=[S((tok, wid...]
where the time goes in v2:
time: 181 us
  Pallas kernels  180 us (99%)
    pallas_call x1, Pallas kernels, on_device_in_kernels(): pl.pallas_call(functools.partial(block_kernel, g), out_shape=[S((tok, wid...  177 us

profile of v2, /device:TPU:0, one launch (start us, length us, event | category | flops | bytes accessed | tf_op | source)
XLA Modules:
  0.0 180.7 jit_solution(13128359700805024835)
XLA Ops:
  0.7 176.6 %block.1 = (bf16[128,1024]{1,0:T(8,128)(2,1)}, bf16[128,1024]{1,0:T(8,128)(2,1)}, f32[1024,128]{1,0:T(8,128)}, f32[320,128]{1,0:T(8,128)}, bf16[256,384]{1,0:T(8...) custom-call(bf16[128,1024]{1,0:T(8,128)(2,1)} %bitcast.33, ...), custom_call_target="tpu_custom_call" | custom-call | tf_op jit(solution)/shard_map/block/pallas_call | solution.py:1889
  177.3 3.2 %finish.1 = (bf16[128,1024]{1,0:T(8,128)(2,1)}, bf16[128,1024]{1,0:T(8,128)(2,1)}, f32[8,128]{1,0:T(8,128)}, f32[8,128]{1,0:T(8,128)}, f32[32,3072]{1,0:T(8,128)...) custom-call(bf16[128,1024]{1,0:T(8,128)(2,1)} %get-tuple-element.56., ...), custom_call_target="tpu_custom_call" | custom-call | tf_op jit(solution)/shard_map/finish/pallas_call | solution.py:1922

commit v3 on v2

--- a/solution.py
+++ b/solution.py
@@ -553,6 +553,17 @@
     tok, width, pt, ch = g.tok, g.width, g.plane_tokens, g.chan
     ff, blocks = g.ff_part, g.blocks
     return dict(
+        up_weight=((g.rows, g.hidden), bf16),
+        down_weight=((g.down_rows, width), bf16),
+        cotangent=((tok, width), bf16),
+        filter_weight=((FILT, width), f32),
+        features=((FEAT + -FEAT % 8, g.length), f32),
+        forth_high=((2 * LANES, 2 * LANES), bf16),
+        forth_low=((2 * LANES, 2 * LANES), bf16),
+        back_high=((2 * LANES, 2 * LANES), bf16),
+        back_low=((2 * LANES, 2 * LANES), bf16),
+        block_out=((tok, width), bf16),
+        tokens_grad=((tok, width), bf16),
         w_in=((width, 3 * LANES), bf16),
         w_in_send=((g.members * g.rows, 3 * LANES), bf16),
         w_up_send=((g.members * g.rows, ff), bf16),
@@ -635,6 +646,7 @@
         out_pre=((g.rows, width), bf16),
         out_total=((g.rows, width), f32),
         ct=((width, LANES), f32),
+        gain_sum=((1, width), f32),
         ps=((PS_ROWS, LANES), f32),
         ps_all=((PS_ROWS, LANES), f32),
         gn_two_own=((pt, width), bf16),
@@ -652,20 +664,18 @@
 
 
 def semaphore_counts(g):
-    plane, line, n, far = g.members - 1, g.planes - 1, g.planes, g.n_dp
-    gather, add = (n + 1, n), (n, n + 1)
-    both = lambda counts: (counts[0] * far, counts[1] * far)
+    plane, line = (g.members - 1,) * 2, (g.planes - 1,) * 2
     chips = (2 * g.chips - 1,) * 2
+    along, along_twice = (g.planes + 1,) * 2, (2 * g.planes + 2,) * 2
     return dict(
-        w_in=(plane,) * 2,
-        w_up=(plane,) * 2,
-        pre=(plane,) * 2,
-        ps=(plane,) * 2,
-        ps_back=(plane,) * 2,
-        car=(line,) * 2,
-        y=(line,) * 2,
-        ps_line=(line,) * 2,
-        ct_z=(line,) * 2,
+        w_in=plane,
+        w_up=plane,
+        pre=plane,
+        ps_back=plane,
+        car=line,
+        y=line,
+        ps_line=line,
+        ct_z=line,
         edge=(1, 1),
         back_edge=(1, 1),
         act_one=chips,
@@ -673,16 +683,10 @@
         cotan=chips,
         w_out=chips,
         gn_two=chips,
-        result=chips,
-        w_out_grad=chips,
-        w_in_line=both(gather),
-        w_up_line=both(gather),
-        w_down=gather,
-        w_out_line=gather,
-        up_grad=both(add),
-        in_grad=both(add),
-        down_grad=add,
-        out_grad=add,
+        w_in_line=along_twice,
+        w_up_line=along_twice,
+        w_out_line=along_twice,
+        w_down=along,
     )
 
 
@@ -922,12 +926,11 @@
 
             @pl.when(self.net.z == through)
             def _():
-                for copy in self.early(target, through):
-                    copy.wait_recv()
-                for piece, held in zip(self.own(target), self.pre):
+                arriving, leaving = self.early(target, through), self.copies(target)
+                for piece, held, come, go in zip(self.own(target), self.pre, arriving, leaving):
+                    come.wait_recv()
                     piece[...] = (piece[...].astype(f32) + held[...].astype(f32)).astype(bf16)
-                for copy in self.copies(target):
-                    copy.start()
+                    go.start()
 
     def wait(self):
         for source in range(self.net.g.planes):
@@ -1151,6 +1154,28 @@
     sems = types.SimpleNamespace(**{name: (refs.pop(0), refs.pop(0)) for name in semaphore_counts(g)})
     local_sem = refs.pop(0)
     net = Net(g)
+    local_count = [0]
+
+    def to_local(src, dst):
+        copy = pltpu.make_async_copy(src, dst, local_sem.at[local_count[0]])
+        local_count[0] += 1
+        copy.start()
+        return copy
+
+    def to_output(src, dst):
+        net.ends.append(to_local(src, dst).wait)
+
+    coming = {
+        name: to_local(getattr(r, name), getattr(w, name))
+        for name in w.__dict__
+        if name in Inputs._fields
+    }
+    r = r._replace(**{name: getattr(w, name) for name in coming})
+
+    def arrive(*refs):
+        for name in list(coming):
+            if any(getattr(w, name) is ref for ref in refs):
+                coming.pop(name).wait()
     tok, width, pt, ch, ff = g.tok, g.width, g.plane_tokens, g.chan, g.ff_part
     rows, planes, members, chips, blocks = g.rows, g.planes, g.members, g.chips, g.blocks
     part = g.down_rows
@@ -1174,6 +1199,7 @@
 
     move_in = ToMembers(net, sems.w_in, lambda m: w.w_in_send.at[step_at(m, rows)], w.w_in.at[own_rows])
     line_in = LineGather(net, sems.w_in_line, lambda z: plane_rows(w.w_in, z))
+    arrive(r.down_weight)
     w.w_down[step_at(net.z, part), :] = r.down_weight[...]
     w.w_out[step_at(net.m * planes + net.z, rows), :] = r.output_weight[...]
     line_down = LineGather(net, sems.w_down, lambda z: [w.w_down.at[step_at(z, part)]])
@@ -1181,6 +1207,7 @@
     pl.semaphore_wait(barrier, len(partners))
     move_in.start()
     line_out.start(far=False)
+    line_down.start(far=False)
 
     xhat_one, inverse_one = normalized(r.tokens[...].astype(f32))
     w.xhat_one[...] = xhat_one
@@ -1189,12 +1216,14 @@
     gather_one = PlaneGather(net, sems.act_one, lambda m: w.act_one.at[step_at(m, tok)])
     gather_one.start()
 
+    arrive(r.up_weight)
     for m in range(members):
         for z in range(planes):
             at = ((m // INNER) * g.n_seq + z * INNER + m % INNER) * part
             w.w_up_send[m * rows : (m + 1) * rows, z * part : (z + 1) * part] = r.up_weight[:, at : at + part]
     w.w_in[own_rows, :] = w.w_in_send[step_at(net.m, rows), :]
     w.w_up[own_rows, :] = w.w_up_send[step_at(net.m, rows), :]
+    arrive(r.cotangent)
     w.cotan[mine, :] = r.cotangent[...]
     move_up = ToMembers(net, sems.w_up, lambda m: w.w_up_send.at[step_at(m, rows)], w.w_up.at[own_rows])
     line_up = LineGather(net, sems.w_up_line, lambda z: plane_rows(w.w_up, z))
@@ -1234,6 +1263,7 @@
     w.skip[...] = spread(15)
     w.decay[...] = spread(16, here)
 
+    arrive(r.filter_weight, r.features, r.forth_high, r.forth_low, r.back_high, r.back_low)
     w.square[...] = jnp.zeros_like(w.square)
     for k, ref in enumerate((r.feat_bias, r.feat_freq, r.inner_bias, r.inner_freq)):
         w.square[k : k + 1, :FILT] = ref[...]
@@ -1343,7 +1373,7 @@
             )
             line_up.start(far=False)
 
-    net.sent(move_in, line_in, move_up, gather_one)
+    net.sent(move_in, line_in, line_out, move_up, gather_one)
 
     group = 32
     lane = lax.broadcasted_iota(jnp.int32, (group, LANES), 1)
@@ -1417,7 +1447,6 @@
     gather_cotan.start()
     line_up.hand_on()
     move_car.wait()
-    line_down.start(far=False)
     to_signal(w.car_recv)
 
     def both(filt):
@@ -1435,6 +1464,7 @@
     gather_out.forward_all()
     move_y.wait()
     line_up.start(far=True)
+    line_down.hand_on()
     line_down.start(far=True)
 
     @pl.loop(0, LANES // group)
@@ -1481,17 +1511,11 @@
     for j in range(chips):
         if j == 1:
             gather_two.forward_all()
-            line_down.hand_on()
         gather_two.wait(j)
         at = step_at(lax.rem(net.p + chips - j, chips), 2 * tok)
         gelu, slope = gelu_pair(dot_nn(w.act_two[at, :], w.w_up[...]) + up_bias)
         w.act_three[at, :] = gelu.astype(bf16)
         slopes.append(slope)
-    def to_local(src, dst):
-        copy = pltpu.make_async_copy(src, dst, local_sem.at[0])
-        copy.start()
-        copy.wait()
-
     plane_part = INNER * rows
 
     def parts_of(ref, z):
@@ -1505,18 +1529,27 @@
     def to_owners(sem, mid, out):
         move = ToMembers(net, sem, lambda m: mid.at[step_at(m, rows)], out.at[step_at(net.m, rows)])
         move.start()
-        to_local(mid.at[step_at(net.m, rows)], out.at[step_at(net.m, rows)])
+        to_output(mid.at[step_at(net.m, rows)], out.at[step_at(net.m, rows)])
         return move
 
     sum_up = LineSum(
         net,
-        sems.up_grad,
+        sems.w_in_line,
         lambda z: plane_rows(w.up_send, z),
         lambda z: parts_of(w.up_parts, z),
         [w.up_pre.at[x * plane_part : (x + 1) * plane_part] for x in range(g.n_dp)],
     )
+    half = part // 2
+
+    def halves_of(ref, z):
+        return [ref.at[step_at(2 * z + k, half)] for k in range(2)]
+
     sum_down = LineSum(
-        net, sems.down_grad, lambda z: [w.down_send.at[step_at(z, part)]], lambda z: [w.down_parts.at[step_at(z, part)]], [w.down_pre]
+        net,
+        sems.w_out_line,
+        lambda z: halves_of(w.down_send, z),
+        lambda z: halves_of(w.down_parts, z),
+        [w.down_pre.at[k * half : (k + 1) * half] for k in range(2)],
     )
     @pl.loop(0, ff // 256)
     def _(step):
@@ -1553,14 +1586,13 @@
     sum_down.start(far=True)
     for slot, piece in zip(parts_of(w.up_parts, net.z), plane_rows(w.up_send, net.z)):
         slot[...] = piece[...]
-    net.sent(gather_cotan)
-    sum_result = PlaneSum(net, sems.result, w.result_sib, w.result_recv, w.cotan, w.result_send)
+    net.sent(gather_cotan, gather_two, line_up, line_down)
+    sum_result = PlaneSum(net, sems.cotan, w.result_sib, w.result_recv, w.cotan, w.result_send)
     for j in range(1, chips + 1):
         chip = lax.rem(net.p + j, chips)
         at = step_at(chip, 2 * tok)
         sum_result.own[at, :] = dot_nn(w.act_three[at, :], w.w_down[...]).astype(bf16)
     sum_up.clear()
-    sum_up.start(far=False)
     grad_two = sum_two.result()
 
     xhat_two = w.xhat_two[...]
@@ -1585,7 +1617,7 @@
     move_gpre.start()
     w.gpre[:, mine] = w.gpre_send[own_block, :]
 
-    sum_out = PlaneSum(net, sems.w_out_grad, w.w_out_grad_sib, w.w_out_grad_recv, after=sum_two)
+    sum_out = PlaneSum(net, sems.act_two, w.w_out_grad_sib, w.w_out_grad_recv, after=sum_two)
     for m in range(members):
         at = slice(m * LANES, (m + 1) * LANES)
         sum_out.own[at, :] = dot_nn(w.pre_line[at, :], w.grad_branch[...]).astype(bf16)
@@ -1605,10 +1637,10 @@
         w.grad_conv[second, :] = grad_pre * w.long[at, :]
 
     move_gl = along(sems.car, w.gl_send, w.gl_recv)
+    sum_up.start(far=False)
     for j in range(1, chips):
         sum_out.relay(j)
     move_gl.wait()
-    sum_up.start(far=True)
     to_signal(w.gl_recv)
     to_spectrum(g, w.signal, 2 * ch, w.stage, r.turns, r.forth_high, r.forth_low, w.spec_grad)
 
@@ -1659,9 +1691,6 @@
 
     ct_z = AlongPlanes(net, sems.ct_z, lambda z: w.ct.at[chan_rows], w.ct.at[chan_rows])
     ct_z.start()
-    sum_up.wait()
-    w.up_mid[...] = added(w.up_parts)
-    move_up_grad = to_owners(sems.w_up, w.up_mid, up_recv)
     move_gc.wait()
 
     @pl.loop(0, LANES // group)
@@ -1674,22 +1703,16 @@
     wait_back_edge = share_edge(
         w.grad_conv, 0, slice(0, 8), net.z - 1, net.z + 1, w.back_edge_send, w.back_edge_recv, sems.back_edge, w.back_edge
     )
+    sum_up.start(far=True)
 
     line_out_grad = LineSum(
         net,
-        sems.out_grad,
+        sems.w_down,
         lambda z: [w.out_sum.at[step_at(z, rows)]],
         lambda z: [w.out_parts.at[step_at(z, rows)]],
         [w.out_pre],
     )
     w.out_sum[...] = sum_out.result().astype(bf16)
-    line_out_grad.start_early()
-    line_out_grad.clear()
-    line_out_grad.start(far=False)
-    line_out_grad.start(far=True)
-    w.out_parts[step_at(net.z, rows), :] = w.out_sum[step_at(net.z, rows), :]
-
-
     def filter_blocks_back(step, which):
         for a in range(2):
             for b in range(3):
@@ -1718,42 +1741,28 @@
     def _(step):
         at = step_at(step, 256)
         grad = dot_nn(w.gproj[...], w.act_one[:, at])
+        w.gain_sum[:, at] = column_sum(grad * w.w_in_t[:, at].astype(f32))
         for b in range(3):
             cut = slice(b * LANES, (b + 1) * LANES)
             w.in_send[at, cut] = grad[cut].T.astype(bf16)
 
     sum_in = LineSum(
         net,
-        sems.in_grad,
+        sems.w_up_line,
         lambda z: plane_rows(w.in_send, z),
         lambda z: parts_of(w.w_in, z),
         [w.w_in_send.at[x * plane_part : (x + 1) * plane_part] for x in range(g.n_dp)],
     )
-    line_out_grad.add_up()
     sum_in.start_early()
     sum_in.clear()
     sum_in.start(far=False)
-    sum_in.start(far=True)
     for slot, piece in zip(parts_of(w.w_in, net.z), plane_rows(w.in_send, net.z)):
         slot[...] = piece[...]
     ct_z.wait()
     gather_ct = PlaneGather(net, sems.act_one, lambda m: w.ct.at[step_at(m, LANES)])
     gather_ct.start()
-    block_out[...] = (w.residual[...] + sum_result.result() + r.down_bias[...]).astype(bf16)
-    sum_one = PlaneSum(net, sems.gn_two, w.gn_one_sib, w.gn_one_recv, after=sum_result)
-    shift_sum = gain_sum = jnp.zeros((1, width), f32)
-    for j in range(1, chips + 1):
-        chip = lax.rem(net.p + j, chips)
-        at = step_at(chip, 2 * tok)
-        turned = w.gproj[:, at].astype(f32).T.astype(bf16)
-        partial = dot_nn(turned, w.w_in_t[...])
-        sum_one.own[at, :] = partial.astype(bf16)
-        sum_one.start(chip)
-        shift_sum = shift_sum + column_sum(partial)
-        gain_sum = gain_sum + column_sum(partial * w.act_one[at, :].astype(f32))
-    to_rows(w.ps, AT_FIRST_GAIN, (gain_sum - r.first_shift[...] * shift_sum) / r.first_gain[...])
-    to_rows(w.ps, AT_FIRST_SHIFT, shift_sum)
-
+    w.block_out[...] = (w.residual[...] + sum_result.result() + r.down_bias[...]).astype(bf16)
+    to_output(w.block_out, block_out)
     kept = w.conv
 
     @pl.loop(0, LANES // group)
@@ -1783,16 +1792,28 @@
     ):
         part_sums = kept[b * LANES : (b + 1) * LANES, kind * LANES : (kind + 1) * LANES]
         tile = jnp.where(which_lane == k, jnp.sum(part_sums, 1, keepdims=True), tile)
+    channel_sum = jnp.sum(kept[:, 4 * LANES : 5 * LANES], 1, keepdims=True)
+    shift_sum = column_sum(channel_sum * w.w_in_t[...].astype(f32))
+    to_rows(w.ps, AT_FIRST_GAIN, (w.gain_sum[...] - r.first_shift[...] * shift_sum) / r.first_gain[...])
+    to_rows(w.ps, AT_FIRST_SHIFT, shift_sum)
     w.ps[pl.ds(pl.multiple_of(AT_CHANNEL + net.m * 16, 16), 16), :] = tile.T[:16, :]
 
     share = PS_ROWS // members
     own_share = step_at(net.m, share)
-    move_ps = ToMembers(net, sems.ps, lambda m: w.ps.at[step_at(m, share)], w.ps_recv.at[own_share])
+    move_ps = ToMembers(net, sems.w_in, lambda m: w.ps.at[step_at(m, share)], w.ps_recv.at[own_share])
+    net.sent(move_gpre)
     move_ps.start()
     w.ps_recv[own_share, :] = w.ps[own_share, :]
+    sum_one = PlaneSum(net, sems.gn_two, w.gn_one_sib, w.gn_one_recv, after=sum_result)
+    for j in range(1, chips + 1):
+        chip = lax.rem(net.p + j, chips)
+        at = step_at(chip, 2 * tok)
+        turned = w.gproj[:, at].astype(f32).T.astype(bf16)
+        sum_one.own[at, :] = dot_nn(turned, w.w_in_t[...]).astype(bf16)
+        sum_one.start(chip)
+    sum_in.add_up()
     for j in range(1, chips):
         sum_one.relay(j)
-    sum_in.add_up()
     move_ps.wait()
 
     def shares_added(ref, count):
@@ -1802,11 +1823,19 @@
     w.ps_line[own_line, :] = shares_added(w.ps_recv, members)
     line_ps = AlongPlanes(net, sems.ps_line, lambda z: w.ps_line.at[own_line], w.ps_line.at[own_line])
     line_ps.start()
+    sum_in.start(far=True)
+    line_out_grad.start_early()
+    line_out_grad.clear()
+    line_out_grad.start(far=False)
+    line_out_grad.start(far=True)
+    w.out_parts[step_at(net.z, rows), :] = w.out_sum[step_at(net.z, rows), :]
+    line_out_grad.add_up()
+    sum_up.wait()
+    w.up_mid[...] = added(w.up_parts)
+    move_up_grad = to_owners(sems.w_up, w.up_mid, up_recv)
     sum_down.wait()
     w.down_total[...] = sum(w.down_parts[z * part : (z + 1) * part, :].astype(f32) for z in range(planes))
-    down_out = pltpu.make_async_copy(w.down_total, down_recv, local_sem.at[1])
-    down_out.start()
-    net.ends.append(down_out.wait)
+    to_output(w.down_total, down_recv)
     gather_ct.forward_all()
     line_ps.wait()
     w.ps_all[own_share, :] = shares_added(w.ps_line, planes)
@@ -1818,16 +1847,15 @@
     grad_one = sum_one.result()
 
     grad_tokens = norm_back(grad_one, w.xhat_one[...], inverse_one, r.first_gain[...])
-    tokens_grad[...] = (w.grad_res[...] + grad_tokens).astype(bf16)
+    w.tokens_grad[...] = (w.grad_res[...] + grad_tokens).astype(bf16)
+    to_output(w.tokens_grad, tokens_grad)
     gather_ct.wait_all()
-    ct_out[...] = w.ct[...]
+    to_output(w.ct, ct_out)
     line_out_grad.wait()
     w.out_total[...] = sum(w.out_parts[z * rows : (z + 1) * rows, :].astype(f32) for z in range(planes))
-    out_out = pltpu.make_async_copy(w.out_total, out_recv, local_sem.at[2])
-    out_out.start()
-    net.ends.append(out_out.wait)
+    to_output(w.out_total, out_recv)
     move_back.wait()
-    ps_out[...] = w.ps_all[...]
+    to_output(w.ps_all, ps_out)
     move_in_grad.wait()
     move_up_grad.wait()
     net.finish()
@@ -1842,8 +1870,8 @@
         second_gain, second_shift, up_weight, up_bias, down_weight, down_bias,
     ) = outs
     rows, planes, width, ff = g.rows, g.planes, g.width, g.ff_part
-    block_out[...] = block_in[...]
-    tokens_grad[...] = tokens_in[...]
+    for src, dst in ((block_in, block_out), (tokens_in, tokens_grad), (down_recv, down_weight), (out_recv, output_weight)):
+        dst[...] = src[...]
     for m in range(g.members):
         x, q = m // INNER, m % INNER
         parts = [x * g.n_seq + z * INNER + q for z in range(planes)]
@@ -1854,8 +1882,6 @@
         for z, k in enumerate(parts):
             cut = slice(z * g.down_rows, (z + 1) * g.down_rows)
             up_weight[:, k * g.down_rows : (k + 1) * g.down_rows] = total[:, cut]
-    down_weight[...] = down_recv[...]
-    output_weight[...] = out_recv[...]
     for m in range(g.members):
         cut = slice(m * LANES, (m + 1) * LANES)
         turned = ct[cut, :].T
@@ -1886,6 +1912,7 @@
     in_vmem = pl.BlockSpec(memory_space=pltpu.VMEM)
     anywhere = pl.BlockSpec(memory_space=pl.ANY)
     S = jax.ShapeDtypeStruct
+    buffers = scratch_buffers(g)
     parts = pl.pallas_call(
         functools.partial(block_kernel, g),
         out_shape=[
@@ -1898,11 +1925,11 @@
             S((g.down_rows, width), f32),
             S((g.rows, width), f32),
         ],
-        in_specs=[in_vmem] * len(operands),
-        out_specs=[in_vmem] * 4 + [anywhere] * 4,
-        scratch_shapes=[pltpu.VMEM(shape, dtype) for shape, dtype in scratch_buffers(g).values()]
+        in_specs=[anywhere if name in buffers else in_vmem for name in Inputs._fields],
+        out_specs=[anywhere] * 8,
+        scratch_shapes=[pltpu.VMEM(shape, dtype) for shape, dtype in buffers.values()]
         + [pltpu.SemaphoreType.DMA((count,)) for pair in semaphore_counts(g).values() for count in pair]
-        + [pltpu.SemaphoreType.DMA((3,))],
+        + [pltpu.SemaphoreType.DMA((len(set(Inputs._fields) & set(buffers)) + 8,))],
         compiler_params=pltpu.CompilerParams(
             collective_id=0, has_side_effects=True, vmem_limit_bytes=63 * 1024 * 1024
         ),

time: 181 us -> 174 us (0.961)
  Pallas kernels: 180 us -> 173 us
    pallas_call x1, Pallas kernels: 177 us -> 170 us  [on_device_in_kernels(): pl.pallas_call(functools.partial(block_kernel, g), out_shape=[S((tok, wid...]
where the time goes in v3:
time: 174 us
  Pallas kernels  173 us (99%)
    pallas_call x1, Pallas kernels, on_device_in_kernels(): pl.pallas_call(functools.partial(block_kernel, g), out_shape=[S((tok, wid...  170 us

profile of v3, /device:TPU:0, one launch (start us, length us, event | category | flops | bytes accessed | tf_op | source)
XLA Modules:
  0.0 173.7 jit_solution(15328793685315551120)
XLA Ops:
  0.7 169.6 %block.1 = (bf16[128,1024]{1,0:T(8,128)(2,1)}, bf16[128,1024]{1,0:T(8,128)(2,1)}, f32[1024,128]{1,0:T(8,128)}, f32[320,128]{1,0:T(8,128)}, bf16[256,384]{1,0:T(8...) custom-call(bf16[128,1024]{1,0:T(8,128)(2,1)} %bitcast.33, ...), custom_call_target="tpu_custom_call" | custom-call | tf_op jit(solution)/shard_map/block/pallas_call | solution.py:1916
  170.3 3.2 %finish.1 = (bf16[128,1024]{1,0:T(8,128)(2,1)}, bf16[128,1024]{1,0:T(8,128)(2,1)}, f32[8,128]{1,0:T(8,128)}, f32[8,128]{1,0:T(8,128)}, f32[32,3072]{1,0:T(8,128)...) custom-call(bf16[128,1024]{1,0:T(8,128)(2,1)} %get-tuple-element.56., ...), custom_call_target="tpu_custom_call" | custom-call | tf_op jit(solution)/shard_map/finish/pallas_call | solution.py:1949

commit v4 on v3

--- a/solution.py
+++ b/solution.py
@@ -591,7 +591,6 @@
         act_pre=((LANES, pt), bf16),
         gpre=((LANES, pt), bf16),
         gproj=((3 * LANES, pt), bf16),
-        signal=((blocks, 2 * ch, LANES), f32),
         taps=((4, 3 * LANES, LANES), f32),
         skip=((LANES, LANES), f32),
         edge_send=((16, 3 * LANES), f32),
@@ -619,7 +618,6 @@
         spec_filt=((blocks, ch, 2 * LANES), f32),
         spec_car=((blocks, 2 * ch, 2 * LANES), f32),
         spec_grad=((blocks, 2 * ch, 2 * LANES), f32),
-        back_sig=((blocks, 2 * ch, LANES), f32),
         back_filt=((blocks, ch, LANES), f32),
         pre_recv=((width, tok), bf16),
         pre_line=((width, tok), bf16),
@@ -643,7 +641,6 @@
         in_send=((width, 3 * LANES), bf16),
         out_sum=((LANES, width), bf16),
         out_parts=((LANES, width), bf16),
-        out_pre=((g.rows, width), bf16),
         out_total=((g.rows, width), f32),
         ct=((width, LANES), f32),
         gain_sum=((1, width), f32),
@@ -870,9 +867,10 @@
 
 
 class LineSum:
-    def __init__(self, net, sems, own, slots, pre):
+    def __init__(self, net, sems, own, slots, pre=()):
         self.net, self.sems, self.own, self.slots, self.pre = net, sems, own, slots, pre
-        self.ends = [(t, through, 0 if t else net.g.planes - 1) for _, through, t in relays(net.g.planes)]
+        passing = relays(net.g.planes) if pre else []
+        self.ends = [(t, through, 0 if t else net.g.planes - 1) for _, through, t in passing]
         net.ends.append(self.wait_send)
 
     def copies(self, target):
@@ -1096,13 +1094,13 @@
     return v * half, half + 0.5 * v * (1.0 - t * t) * (scale * (1.0 + 3 * 0.044715 * v2))
 
 
-def to_spectrum(g, signal, rows, stage, turns, high, low, out):
-    @pl.loop(0, rows // 8)
+def to_spectrum(g, load, rows, stage, turns, high, low, out):
+    @pl.loop(0, rows // 16)
     def _(step):
-        at = step_at(step, 8)
+        at = step_at(step, 16)
         first = []
         for n in range(g.blocks):
-            block = signal[n, at, :]
+            block = load(n, step)
             angle = -2 * math.pi * n / (4 * g.blocks)
             first.append((block * math.cos(angle), block * math.sin(angle)))
         for k, (re, im) in enumerate(small_transform(first, -1)):
@@ -1119,7 +1117,7 @@
         out[at] = split_dot(x, high[...], low[...]).reshape(group, rows, 2 * LANES)
 
 
-def from_spectrum(g, product, rows, stage, turns, high, low, signal):
+def from_spectrum(g, product, rows, stage, turns, high, low, store):
     group = 256 // rows
 
     @pl.loop(0, g.blocks // group)
@@ -1129,9 +1127,9 @@
         x = jnp.concatenate([re, im], -1).reshape(group * rows, 2 * LANES)
         stage[at] = split_dot(x, high[...], low[...]).reshape(group, rows, 2 * LANES)
 
-    @pl.loop(0, rows // 8)
+    @pl.loop(0, rows // 16)
     def _(step):
-        at = step_at(step, 8)
+        at = step_at(step, 16)
         values = []
         for k in range(g.blocks):
             re, im = stage[k, at, :LANES], stage[k, at, LANES:]
@@ -1139,7 +1137,7 @@
             values.append((re * c - im * s, re * s + im * c))
         for n, (re, im) in enumerate(small_transform(values, 1)):
             angle = 2 * math.pi * n / (4 * g.blocks)
-            signal[n, at, :] = (re * math.cos(angle) - im * math.sin(angle)) * (1.0 / g.length)
+            store(n, step, (re * math.cos(angle) - im * math.sin(angle)) * (1.0 / g.length))
 
 
 def halves(x):
@@ -1302,7 +1300,7 @@
             cut = slice(k * LANES, (k + 1) * LANES)
             w.filt[step * (span // LANES) + k] = filters[:, cut] * jnp.exp(-w.decay[...] * feats[:1, cut])
 
-    to_spectrum(g, w.filt, ch, w.stage_filt, r.turns, r.forth_high, r.forth_low, w.spec_filt)
+    to_spectrum(g, lambda n, step: w.filt[n, step_at(step, 16), :], ch, w.stage_filt, r.turns, r.forth_high, r.forth_low, w.spec_filt)
 
     line_out.hand_on()
     line_in.hand_on()
@@ -1427,39 +1425,37 @@
         recv[own_z, :] = send[own_z, :]
         return move
 
-    def place(d):
-        a, n = d // blocks, d % blocks
-        return n, step_at(a, ch), step_at(n // INNER, ch), step_at(a * INNER + n % INNER, LANES)
-
-    def to_signal(recv):
-        @pl.loop(0, 2 * blocks)
-        def _(d):
-            n, at, from_rows, from_lanes = place(d)
-            w.signal[n, at, :] = recv[from_rows, from_lanes].astype(f32)
+    def piece_of(n, step):
+        a, part_rows = step * 16 // ch, step * 16 % ch
+        return (
+            pl.ds(pl.multiple_of(n // INNER * ch + part_rows, 16), 16),
+            pl.ds(pl.multiple_of((a * INNER + n % INNER) * tok, tok), tok),
+        )
+
+    def received(recv):
+        return lambda n, step: recv[piece_of(n, step)].astype(f32)
 
     def to_planes(send):
-        @pl.loop(0, 2 * blocks)
-        def _(d):
-            n, at, to_row, to_lane = place(d)
-            send[to_row, to_lane] = w.back_sig[n, at, :].astype(bf16)
+        def store(n, step, value):
+            send[piece_of(n, step)] = value.astype(bf16)
+
+        return store
 
     move_car = along(sems.car, w.car_send, w.car_recv)
     gather_cotan.start()
     line_up.hand_on()
     move_car.wait()
-    to_signal(w.car_recv)
 
     def both(filt):
         return jnp.concatenate([filt, filt], 1)
 
-    to_spectrum(g, w.signal, 2 * ch, w.stage, r.turns, r.forth_high, r.forth_low, w.spec_car)
+    to_spectrum(g, received(w.car_recv), 2 * ch, w.stage, r.turns, r.forth_high, r.forth_low, w.spec_car)
 
     def forth_product(at):
         (hr, hi), (xr, xi) = halves(both(w.spec_filt[at])), halves(w.spec_car[at])
         return xr * hr - xi * hi, xr * hi + xi * hr
 
-    from_spectrum(g, forth_product, 2 * ch, w.stage, r.turns, r.back_high, r.back_low, w.back_sig)
-    to_planes(w.y_send)
+    from_spectrum(g, forth_product, 2 * ch, w.stage, r.turns, r.back_high, r.back_low, to_planes(w.y_send))
     move_y = along(sems.y, w.y_send, w.y_recv)
     gather_out.forward_all()
     move_y.wait()
@@ -1570,10 +1566,10 @@
         bias_sum = bias_sum + column_sum(grad_upper.astype(f32))
         sum_two.own[at, :] = dot_nt(grad_upper, w.w_up[...]).astype(bf16)
         sum_two.start(chip)
+        if j > 1:
+            sum_two.relay(j - 1)
     for z, k in enumerate(hidden_block):
         w.ps[pl.ds(AT_UP_BIAS + k, 1), :] = bias_sum[:, z * part : (z + 1) * part]
-    for j in range(1, chips):
-        sum_two.relay(j)
 
     @pl.loop(0, width // 256)
     def _(step):
@@ -1641,15 +1637,13 @@
     for j in range(1, chips):
         sum_out.relay(j)
     move_gl.wait()
-    to_signal(w.gl_recv)
-    to_spectrum(g, w.signal, 2 * ch, w.stage, r.turns, r.forth_high, r.forth_low, w.spec_grad)
+    to_spectrum(g, received(w.gl_recv), 2 * ch, w.stage, r.turns, r.forth_high, r.forth_low, w.spec_grad)
 
     def back_product(at):
         (hr, hi), (gr, gi) = halves(both(w.spec_filt[at])), halves(w.spec_grad[at])
         return hr * gr + hi * gi, hr * gi - hi * gr
 
-    from_spectrum(g, back_product, 2 * ch, w.stage, r.turns, r.back_high, r.back_low, w.back_sig)
-    to_planes(w.gc_send)
+    from_spectrum(g, back_product, 2 * ch, w.stage, r.turns, r.back_high, r.back_low, to_planes(w.gc_send))
     move_gc = along(sems.y, w.gc_send, w.gc_recv)
     for j in range(1, chips):
         sum_result.relay(j)
@@ -1662,7 +1656,10 @@
             out.append((xr * gr + xi * gi, xr * gi - xi * gr))
         return out[0][0] + out[1][0], out[0][1] + out[1][1]
 
-    from_spectrum(g, filt_product, ch, w.stage_filt, r.turns, r.back_high, r.back_low, w.back_filt)
+    def keep_filter(n, step, value):
+        w.back_filt[n, step_at(step, 16), :] = value
+
+    from_spectrum(g, filt_product, ch, w.stage_filt, r.turns, r.back_high, r.back_low, keep_filter)
 
     ones = jnp.ones((8, span), f32)
     chan_rows = step_at(net.chan_block, ch)
@@ -1710,7 +1707,6 @@
         sems.w_down,
         lambda z: [w.out_sum.at[step_at(z, rows)]],
         lambda z: [w.out_parts.at[step_at(z, rows)]],
-        [w.out_pre],
     )
     w.out_sum[...] = sum_out.result().astype(bf16)
     def filter_blocks_back(step, which):
@@ -1751,10 +1747,7 @@
         sems.w_up_line,
         lambda z: plane_rows(w.in_send, z),
         lambda z: parts_of(w.w_in, z),
-        [w.w_in_send.at[x * plane_part : (x + 1) * plane_part] for x in range(g.n_dp)],
-    )
-    sum_in.start_early()
-    sum_in.clear()
+    )
     sum_in.start(far=False)
     for slot, piece in zip(parts_of(w.w_in, net.z), plane_rows(w.in_send, net.z)):
         slot[...] = piece[...]
@@ -1811,9 +1804,8 @@
         turned = w.gproj[:, at].astype(f32).T.astype(bf16)
         sum_one.own[at, :] = dot_nn(turned, w.w_in_t[...]).astype(bf16)
         sum_one.start(chip)
-    sum_in.add_up()
-    for j in range(1, chips):
-        sum_one.relay(j)
+        if j > 1:
+            sum_one.relay(j - 1)
     move_ps.wait()
 
     def shares_added(ref, count):
@@ -1824,12 +1816,9 @@
     line_ps = AlongPlanes(net, sems.ps_line, lambda z: w.ps_line.at[own_line], w.ps_line.at[own_line])
     line_ps.start()
     sum_in.start(far=True)
-    line_out_grad.start_early()
-    line_out_grad.clear()
     line_out_grad.start(far=False)
     line_out_grad.start(far=True)
     w.out_parts[step_at(net.z, rows), :] = w.out_sum[step_at(net.z, rows), :]
-    line_out_grad.add_up()
     sum_up.wait()
     w.up_mid[...] = added(w.up_parts)
     move_up_grad = to_owners(sems.w_up, w.up_mid, up_recv)

time: 174 us -> 172 us (0.989)
  Pallas kernels: 173 us -> 171 us
    pallas_call x1, Pallas kernels: 170 us -> 167 us  [on_device_in_kernels(): pl.pallas_call(functools.partial(block_kernel, g), out_shape=[S((tok, wid...]
where the time goes in v4:
time: 172 us
  Pallas kernels  171 us (99%)
    pallas_call x1, Pallas kernels, on_device_in_kernels(): pl.pallas_call(functools.partial(block_kernel, g), out_shape=[S((tok, wid...  167 us

profile of v4, /device:TPU:0, one launch (start us, length us, event | category | flops | bytes accessed | tf_op | source)
XLA Modules:
  0.0 171.6 jit_solution(18099773541735061690)
XLA Ops:
  0.7 167.5 %block.1 = (bf16[128,1024]{1,0:T(8,128)(2,1)}, bf16[128,1024]{1,0:T(8,128)(2,1)}, f32[1024,128]{1,0:T(8,128)}, f32[320,128]{1,0:T(8,128)}, bf16[256,384]{1,0:T(8...) custom-call(bf16[128,1024]{1,0:T(8,128)(2,1)} %bitcast.33, ...), custom_call_target="tpu_custom_call" | custom-call | tf_op jit(solution)/shard_map/block/pallas_call | solution.py:1905
  168.2 3.2 %finish.1 = (bf16[128,1024]{1,0:T(8,128)(2,1)}, bf16[128,1024]{1,0:T(8,128)(2,1)}, f32[8,128]{1,0:T(8,128)}, f32[8,128]{1,0:T(8,128)}, f32[32,3072]{1,0:T(8,128)...) custom-call(bf16[128,1024]{1,0:T(8,128)(2,1)} %get-tuple-element.56., ...), custom_call_target="tpu_custom_call" | custom-call | tf_op jit(solution)/shard_map/finish/pallas_call | solution.py:1938

commit v5 on v4

--- a/solution.py
+++ b/solution.py
@@ -493,7 +493,7 @@
 def split_dot(x, high, low):
     head = x.astype(bf16)
     tail = (x - head.astype(f32)).astype(bf16)
-    return dot_nn(head, high) + dot_nn(tail, high) + dot_nn(head, low)
+    return dot_nn(jnp.concatenate([head, tail, head], 1), jnp.concatenate([high, high, low], 0))
 
 
 def sin_cos(x):

time: 172 us -> 172 us (level)
  no operation moved by 1% of the time
where the time goes in v5:
time: 172 us
  Pallas kernels  171 us (99%)
    pallas_call x1, Pallas kernels, on_device_in_kernels(): pl.pallas_call(functools.partial(block_kernel, g), out_shape=[S((tok, wid...  168 us

profile of v5, /device:TPU:0, one launch (start us, length us, event | category | flops | bytes accessed | tf_op | source)
XLA Modules:
  0.0 171.6 jit_solution(48487160953611532)
XLA Ops:
  0.7 167.5 %block.1 = (bf16[128,1024]{1,0:T(8,128)(2,1)}, bf16[128,1024]{1,0:T(8,128)(2,1)}, f32[1024,128]{1,0:T(8,128)}, f32[320,128]{1,0:T(8,128)}, bf16[256,384]{1,0:T(8...) custom-call(bf16[128,1024]{1,0:T(8,128)(2,1)} %bitcast.33, ...), custom_call_target="tpu_custom_call" | custom-call | tf_op jit(solution)/shard_map/block/pallas_call | solution.py:1905
  168.2 3.2 %finish.1 = (bf16[128,1024]{1,0:T(8,128)(2,1)}, bf16[128,1024]{1,0:T(8,128)(2,1)}, f32[8,128]{1,0:T(8,128)}, f32[8,128]{1,0:T(8,128)}, f32[32,3072]{1,0:T(8,128)...) custom-call(bf16[128,1024]{1,0:T(8,128)(2,1)} %get-tuple-element.56., ...), custom_call_target="tpu_custom_call" | custom-call | tf_op jit(solution)/shard_map/finish/pallas_call | solution.py:1938
